TPU v7x, 32 devices: a whole 2x2x4 slice. The times are simulated.
32 devices in a mesh: seq: 16 (over z, y, core), kvh: 2 (over x).
Axes of the slice: x: 2, y: 2, z: 4, core: 2. Of those that a mesh axis runs over, the one named last changes fastest.
Arguments:
- queries: bfloat16 [4096, 2048], P('seq', 'kvh'), may hold values from -2.5 to 2.5
- key_vector_rows: bfloat16 [4096, 256], P(('seq', 'kvh')), may hold values from -2.5 to 2.5
- value_vector_rows: bfloat16 [4096, 256], P(('seq', 'kvh')), may hold values from -5 to 5
- output_gradient: bfloat16 [4096, 2048], P('seq', 'kvh'), may hold values from -24 to 24
- key_lists: int32 [32, 24], replicated, may hold values from 0 to 31, as said below
- block_counts: int32 [32], replicated, may hold values from 1 to 24, as said below
- span_table: int32 [32], replicated, may hold values from 0 to 31, each once
Outputs:
- grad_queries: bfloat16 [4096, 2048], P('seq', 'kvh')
- key_gradient: bfloat16 [4096, 256], P(('seq', 'kvh'))
- value_gradient: bfloat16 [4096, 256], P(('seq', 'kvh'))
Inputs may be any that keep to these rules, and one draw needn't show every extreme that they name: `key_lists`: row b lists, by position, the key blocks of query block b: its first block_counts[b] entries are distinct blocks at or before b, the first being b itself; the remaining entries are 0. block_counts[b] is at most b + 1 and at most 24; the last block's count is 24. `span_table`: each position block appears once.
All inputs are finite; a program needn't handle non-finite values.
Results may differ from a plain program's by a relative error of at most 0.0055.
Values may be sent and summed in bfloat16 or wider, within the bound.
No kernel may reach another device: no remote copies, remote signals or barrier semaphores. Data moves between devices by JAX's collectives and lax.ppermute only.
A program may use at most 128 MiB of HBM per device.

v0:
```python
import jax
import jax.numpy as jnp
from jax import lax
from jax.sharding import PartitionSpec as P

HEAD_SIZE = 128
QUERY_PER_KEY = 8
BLOCK_TOKENS = 128


def shards(
    queries,
    key_vector_rows,
    value_vector_rows,
    output_gradient,
    key_lists,
    block_counts,
    span_table,
):
    key_heads, value_heads = (
        lax.all_to_all(key_vector_rows, "kvh", split_axis=1, concat_axis=0, tiled=True),
        lax.all_to_all(value_vector_rows, "kvh", split_axis=1, concat_axis=0, tiled=True),
    )
    keys_all, values_all = (
        lax.all_gather(key_heads, "seq", axis=0, tiled=True),
        lax.all_gather(value_heads, "seq", axis=0, tiled=True),
    )
    head_dim = HEAD_SIZE
    group_size = QUERY_PER_KEY
    block_rows = BLOCK_TOKENS
    logit_scale = HEAD_SIZE ** (-0.5)
    local_rows = queries.shape[0]
    local_blocks = local_rows // block_rows
    total_blocks = keys_all.shape[0] // block_rows
    queries_grouped = queries.reshape(local_rows, group_size, head_dim)
    grads_grouped = output_gradient.reshape(local_rows, group_size, head_dim)
    inverse = (
        jnp.zeros((total_blocks,), jnp.int32)
        .at[span_table]
        .set(jnp.arange(total_blocks, dtype=jnp.int32))
    )
    first_slot = lax.axis_index("seq") * local_blocks
    lower_mask = jnp.arange(block_rows)[None, :] <= jnp.arange(block_rows)[:, None]

    def block_scores(query_blk, key_pos, query_pos):
        row_start = inverse[key_pos] * block_rows
        key_blk = lax.dynamic_slice_in_dim(keys_all, row_start, block_rows, 0)
        value_blk = lax.dynamic_slice_in_dim(values_all, row_start, block_rows, 0)
        scores = (
            jnp.einsum("tgd,sd->gts", query_blk, key_blk, preferred_element_type=jnp.float32)
            * logit_scale
        )
        allowed = jnp.logical_or(key_pos != query_pos, lower_mask)
        return (scores, allowed, key_blk, value_blk, row_start)

    def forward_maker(query_blk, query_pos):

        def forward_step(entry_id, carried):
            row_total, weighted = carried
            key_pos = key_lists[query_pos, entry_id]
            scores, allowed, key_blk, value_blk, row_start = block_scores(
                query_blk, key_pos, query_pos
            )
            exp_scores = jnp.where(allowed, jnp.exp(scores), 0.0)
            row_total = row_total + jnp.sum(exp_scores, -1)
            weighted = weighted + jnp.einsum(
                "gts,sd->tgd",
                exp_scores.astype(jnp.bfloat16),
                value_blk,
                preferred_element_type=jnp.float32,
            )
            return (row_total, weighted)

        return forward_step

    prepared = []
    for index_local in range(local_blocks):
        query_blk = queries_grouped[index_local * block_rows : (index_local + 1) * block_rows]
        grad_blk = grads_grouped[index_local * block_rows : (index_local + 1) * block_rows]
        query_pos = span_table[first_slot + index_local]
        entries = block_counts[query_pos]
        starting_carry = (
            jnp.zeros((group_size, block_rows), jnp.float32),
            jnp.zeros((block_rows, group_size, head_dim), jnp.float32),
        )
        row_total, weighted = lax.fori_loop(
            0, entries, forward_maker(query_blk, query_pos), starting_carry
        )
        attended = weighted / jnp.transpose(row_total)[:, :, None]
        row_delta = jnp.transpose(jnp.sum(grad_blk.astype(jnp.float32) * attended, -1))
        prepared.append((query_blk, grad_blk, query_pos, entries, jnp.log(row_total), row_delta))

    def pair_grads(prepared_item, key_pos):
        query_blk, grad_blk, query_pos, entries, log_total, row_delta = prepared_item
        scores, allowed, key_blk, value_blk, row_start = block_scores(query_blk, key_pos, query_pos)
        weights = jnp.where(allowed, jnp.exp(scores - log_total[:, :, None]), 0.0)
        value_part = jnp.einsum(
            "gts,tgd->sd",
            weights.astype(jnp.bfloat16),
            grad_blk,
            preferred_element_type=jnp.float32,
        )
        weight_grads = jnp.einsum(
            "tgd,sd->gts", grad_blk, value_blk, preferred_element_type=jnp.float32
        )
        score_grads = (weights * (weight_grads - row_delta[:, :, None])).astype(jnp.bfloat16)
        query_part = jnp.einsum(
            "gts,sd->tgd", score_grads, key_blk, preferred_element_type=jnp.float32
        )
        key_part = jnp.einsum(
            "gts,tgd->sd", score_grads, query_blk, preferred_element_type=jnp.float32
        )
        return (query_part, jnp.concatenate([key_part, value_part], 1), row_start)

    def grad_maker(prepared_item):

        def grad_step(entry_id, carried):
            query_grad, buffer = carried
            query_part, pair_kv, row_start = pair_grads(
                prepared_item, key_lists[prepared_item[2], entry_id]
            )
            previous = lax.dynamic_slice_in_dim(buffer, row_start, block_rows, 0)
            buffer = lax.dynamic_update_slice_in_dim(buffer, previous + pair_kv, row_start, 0)
            return (query_grad + query_part, buffer)

        return grad_step

    zero_grad = jnp.zeros((block_rows, group_size, head_dim), jnp.float32)
    query_grads = []
    buffer = jnp.zeros((total_blocks * block_rows, 2 * head_dim), jnp.float32)
    for prepared_item in prepared:
        query_grad, buffer = lax.fori_loop(
            0, prepared_item[3], grad_maker(prepared_item), (zero_grad, buffer)
        )
        query_grads.append(query_grad)
    kv_sums = lax.psum_scatter(buffer, "seq", scatter_dimension=0, tiled=True)
    query_all = jnp.concatenate(query_grads, 0) * logit_scale
    grad_queries = query_all.reshape(local_rows, group_size * head_dim).astype(jnp.bfloat16)
    key_out = (kv_sums[:, :head_dim] * logit_scale).astype(jnp.bfloat16)
    value_out = kv_sums[:, head_dim:].astype(jnp.bfloat16)
    key_gradient, value_gradient = (
        lax.all_to_all(key_out, "kvh", split_axis=0, concat_axis=1, tiled=True),
        lax.all_to_all(value_out, "kvh", split_axis=0, concat_axis=1, tiled=True),
    )
    return (grad_queries, key_gradient, value_gradient)


def solution(mesh):
    placed = (
        P("seq", "kvh"),
        P(("seq", "kvh"), None),
        P(("seq", "kvh"), None),
        P("seq", "kvh"),
        P(),
        P(),
        P(),
    )
    return jax.shard_map(
        shards,
        mesh=mesh,
        in_specs=placed,
        out_specs=(P("seq", "kvh"), P(("seq", "kvh"), None), P(("seq", "kvh"), None)),
        check_vma=False,
    )
```

profile of v0, /device:TPU:0, one launch (start us, length us, event | category | flops | bytes accessed | tf_op | source)
XLA Modules:
  0.0 962.0 jit_solution(6576819639040802137)
XLA Ops:
  8.0 8.2 all_to_all.76
  17.2 7.2 all_to_all.77
  24.4 1.4 fusion.81
  33.3 21.8 %all-gather.5.cloned.1.call-done = bf16[4096,128]{1,0:T(8,128)(2,1)} async-done(((bf16[256,128]{1,0:T(8,128)(2,1)}), bf16[4096,128]{1,0:T(8,128)(2,1)}) %all-gather.5.cloned.1.call-update) | async-done | bytes 1048592 | tf_op jit(solution)/shard_map/all_gather | solution.py:26
  55.1 1.5 copy.116
  56.6 37.6 %all-gather.3.cloned.1.call-done = bf16[4096,128]{1,0:T(8,128)(2,1)} async-done(((bf16[256,128]{1,0:T(8,128)(2,1)}), bf16[4096,128]{1,0:T(8,128)(2,1)}) %all-gather.3.cloned.1.call-update) | async-done | bytes 1048592 | tf_op jit(solution)/shard_map/all_gather | solution.py:25
  94.2 54.8 %while.62 = (s32[]{:T(128)}, f32[8,128]{1,0:T(8,128)S(1)}, f32[128,8,128]{0,2,1:T(8,128)S(1)}, s32[]{:T(128)}, s32[32,24]{0,1:T(8,128)}, /*index=5*/s32[]{:T(128...) while((s32[]{:T(128)}, f32[8,128]{1,0:T(8,128)S(1)}, ...), condition=%wide.region_9.10_spmd.clone, body=%wide.region_7.0_spmd.clone.sunk | while | flops 67797008 | bytes 1950017 | solution.py:86
  94.8 1.3 dynamic_slice.206
  102.5 1.3 dynamic_slice.206
  110.3 1.3 dynamic_slice.206
  118.0 1.3 dynamic_slice.206
  125.7 1.3 dynamic_slice.206
  149.0 153.3 %while.60 = (s32[]{:T(128)}, f32[8,128]{1,0:T(8,128)S(1)}, f32[128,8,128]{0,2,1:T(8,128)S(1)}, s32[]{:T(128)}, s32[32,24]{0,1:T(8,128)}, /*index=5*/s32[]{:T(128...) while((s32[]{:T(128)}, f32[8,128]{1,0:T(8,128)S(1)}, ...), condition=%wide.region_3.4_spmd.clone, body=%wide.region_1.3_spmd.clone.sunk | while | flops 67797008 | bytes 1950017 | solution.py:86
  302.5 2.4 broadcast_in_dim.56
  304.9 229.5 %while.61 = (s32[]{:T(128)}, f32[128,8,128]{0,2,1:T(8,128)S(1)}, f32[4096,256]{0,1:T(8,128)}, s32[]{:T(128)}, s32[32,24]{0,1:T(8,128)}, /*index=5*/s32[]{:T(128)...) while((s32[]{:T(128)}, f32[128,8,128]{0,2,1:T(8,128)S(1)}, ...), condition=%wide.region_6.0_spmd.clone, body=%wide.region_5.6_spmd.clone.sunk | while | flops 168919056 | bytes 5120353 | solution.py:132
  314.7 1.6 fusion.162
  326.2 1.6 fusion.162
  337.6 1.6 fusion.162
  349.1 1.6 fusion.162
  360.5 1.6 fusion.162
  372.0 1.6 fusion.162
  383.4 1.6 fusion.162
  394.9 1.6 fusion.162
  406.3 1.6 fusion.162
  417.7 1.6 fusion.162
  429.2 1.6 fusion.162
  440.6 1.6 fusion.162
  452.1 1.6 fusion.162
  463.5 1.6 fusion.162
  475.0 1.6 fusion.162
  486.4 1.6 fusion.162
  497.9 1.6 fusion.162
  509.3 1.6 fusion.162
  520.8 1.6 fusion.162
  532.2 1.6 fusion.162
  534.5 81.5 %while.63 = (s32[]{:T(128)}, f32[128,8,128]{0,2,1:T(8,128)S(1)}, f32[4096,256]{0,1:T(8,128)}, s32[]{:T(128)}, s32[32,24]{0,1:T(8,128)}, /*index=5*/s32[]{:T(128)...) while((s32[]{:T(128)}, f32[128,8,128]{0,2,1:T(8,128)S(1)}, ...), condition=%wide.region_12.13_spmd.clone, body=%wide.region_11.12_spmd.clone.sunk | while | flops 168919056 | bytes 5120353 | solution.py:132
  544.5 1.6 fusion.183
  556.0 1.6 fusion.183
  567.5 1.6 fusion.183
  579.1 1.6 fusion.183
  590.6 1.6 fusion.183
  602.2 1.6 fusion.183
  613.7 1.6 fusion.183
  616.4 321.6 %reduce-scatter.2.cloned.1.call-done = f32[256,256]{0,1:T(8,128)} async-done(((f32[4096,256]{0,1:T(8,128)}), f32[256,256]{0,1:T(8,128)}) %reduce-scatter.2.cloned.1.call-update) | async-done | bytes 262160 | tf_op jit(solution)/shard_map/reduce_scatter | solution.py:136
  939.7 3.3 all-to-all-start.3
  944.7 2.5 all-to-all-done.3
  947.1 3.3 all-to-all-start.2
  952.2 2.3 all-to-all-done.2
  (422 shorter events, 237.6 us)
Async XLA Ops:
  7.2 0.8 copy-start
  7.2 24.7 %copy-start.2 = (s32[32]{0:T(128)S(1)}, s32[32]{0:T(128)}, u32[]{:S(2)}) copy-start(s32[32]{0:T(128)} %param.21) | copy-start | bytes 388
  7.2 23.0 %copy-start.1 = (bf16[256,1024]{1,0:T(8,128)(2,1)S(1)}, bf16[256,1024]{1,0:T(8,128)(2,1)}, u32[]{:S(2)}) copy-start(bf16[256,1024]{1,0:T(8,128)(2,1)} %param.18) | copy-start | bytes 1572868
  7.2 25.4 %copy-start.3 = (s32[32]{0:T(128)S(1)}, s32[32]{0:T(128)}, u32[]{:S(2)}) copy-start(s32[32]{0:T(128)} %param.20) | copy-start | bytes 388
  7.2 47.9 %all-gather.5.cloned.1.call-start = ((), (), s32[]{:S(2)}) async-start(), calls=%async_computation.6 | async-start | bytes 1114112 | tf_op jit(solution)/shard_map/all_gather | solution.py:26
  16.3 77.9 %all-gather.3.cloned.1.call-start = ((), (), s32[]{:S(2)}) async-start(), calls=%async_computation.5 | async-start | bytes 1114112 | tf_op jit(solution)/shard_map/all_gather | solution.py:25
  24.4 913.7 %reduce-scatter.2.cloned.1.call-start = ((), (), s32[]{:S(2)}) async-start(), calls=%async_computation.7 | async-start | bytes 4456448 | tf_op jit(solution)/shard_map/reduce_scatter | solution.py:136
  939.7 7.4 all-to-all-start.3
  947.1 7.4 all-to-all-start.2
Sparse Core Ops, SparseCore 0:
  16.4 38.6 all-gather.4
  57.2 36.8 all-gather.2
  616.2 321.8 reduce-scatter.1
where the time goes:
time: 952 us; the launch traced here: 962 us
  waiting for transfers between devices  386 us (41%)
  loops' own time  244 us (26%)
  matrix products  128 us (13%)
  local copies, waits for them, and re-layouts  118 us (12%)
  other arithmetic  46.4 us (5%)
  between operations  17.9 us (2%)
  blocking collectives  15.4 us (2%)
    reduce_scatter x1, waiting for transfers between devices, shards(): kv_sums = lax.psum_scatter(buffer, 'seq', scatter_dimension=0, tiled=True)  322 us
    another operation x2, loops' own time, shards(): lax.fori_loop(0, prepared_item[3], grad_maker(prepared_item), (zero_grad,...  122 us
    another operation x2, loops' own time, shards(): lax.fori_loop(0, entries, forward_maker(query_blk, query_pos), starting_c...  121 us
    dot_general x54, matrix products, block_scores(): jnp.einsum('tgd,sd->gts', query_blk, key_blk, preferred_element_type=jnp....  55.5 us
    dynamic_update_slice x27, other arithmetic, grad_step(): lax.dynamic_update_slice_in_dim(buffer, previous + pair_kv, row_start, 0)  43.3 us
    all_gather x1, waiting for transfers between devices, shards(): lax.all_gather(key_heads, 'seq', axis=0, tiled=True)  37.6 us
    dynamic_slice x27, local copies, waits for them, and re-layouts, forward_step(): key_pos = key_lists[query_pos, entry_id]  35.1 us
    dynamic_slice x27, local copies, waits for them, and re-layouts, grad_step(): key_lists[prepared_item[2], entry_id]  34.9 us
  transfers between devices with their start and end apart: 5, of which 5 were waited for; matrix products, arithmetic and copies ran while one was open for 1% of the time, Pallas kernels for 0%

commit v1 on v0

v1 whole, which is shorter than its diff:
```python
import functools

import jax
import jax.numpy as jnp
from jax import lax
from jax.experimental import pallas as pl
from jax.experimental.pallas import tpu as pltpu
from jax.sharding import PartitionSpec as P

HEAD = 128
GROUP = 8
BLOCK = 128
SCALE = HEAD ** (-0.5)
LOG2E = 1.4426950408889634
SCORE_SCALE = SCALE * LOG2E
TILE = 2 * BLOCK
WIDE = GROUP * BLOCK
BF16 = jnp.bfloat16
F32 = jnp.float32


def attend_kernel(
    counts,
    slots,
    qt_ref,
    dot_ref,
    qs_ref,
    dos_ref,
    kv_ref,
    dqt_ref,
    dkv_ref,
    kt_scr,
    total_scr,
    delta_scr,
    w_scr,
    ds_scr,
    acc_scr,
):
    local_blocks = qt_ref.shape[0]
    n_slots = kv_ref.shape[0] // BLOCK
    acc_scr[...] = jnp.zeros_like(acc_scr)
    dqt_ref[...] = jnp.zeros_like(dqt_ref)
    total_scr[...] = jnp.zeros_like(total_scr)
    delta_scr[...] = jnp.zeros_like(delta_scr)

    def turn(j, carry):
        rows = pl.ds(pl.multiple_of(j * BLOCK, BLOCK), BLOCK)
        kt_scr[j] = kv_ref[rows, :HEAD].T
        return carry

    lax.fori_loop(0, n_slots, turn, 0)

    def rows_of(i, entry):
        return pl.ds(pl.multiple_of(slots[i, entry] * BLOCK, BLOCK), BLOCK)

    def allowed(i, chunk):
        key_at = lax.broadcasted_iota(jnp.int32, (TILE, TILE), 0)
        query_at = lax.broadcasted_iota(jnp.int32, (TILE, TILE), 1) & (BLOCK - 1)
        second = key_at >= BLOCK
        entry = 2 * chunk + second.astype(jnp.int32)
        here = key_at & (BLOCK - 1)
        causal = jnp.logical_or(entry > 0, here <= query_at)
        return jnp.logical_and(entry < counts[i], causal)

    def pair(ref, i, chunk, lanes):
        return jnp.concatenate(
            [ref[rows_of(i, 2 * chunk), lanes], ref[rows_of(i, 2 * chunk + 1), lanes]], 0
        )

    def first_pass(i, chunk, masked):
        keys = pair(kv_ref, i, chunk, slice(0, HEAD))
        values = pair(kv_ref, i, chunk, slice(HEAD, 2 * HEAD))
        mask = allowed(i, chunk) if masked else None
        for h in range(0, WIDE, TILE):
            lanes = slice(h, h + TILE)
            scores = jnp.dot(keys, qt_ref[i, :, lanes], preferred_element_type=F32)
            expd = jnp.exp2(scores * SCORE_SCALE)
            if masked:
                expd = jnp.where(mask, expd, 0.0)
            total_scr[i, :, lanes] += jnp.sum(expd.reshape(TILE // 8, 8, TILE), 0)
            dweights = jnp.dot(values, dot_ref[i, :, lanes], preferred_element_type=F32)
            delta_scr[i, :, lanes] += jnp.sum((expd * dweights).reshape(TILE // 8, 8, TILE), 0)

    def second_pass(i, chunk, masked):
        keys = pair(kv_ref, i, chunk, slice(0, HEAD))
        values = pair(kv_ref, i, chunk, slice(HEAD, 2 * HEAD))
        mask = allowed(i, chunk) if masked else None
        keys_t = jnp.concatenate([kt_scr[slots[i, 2 * chunk]], kt_scr[slots[i, 2 * chunk + 1]]], 1)
        for h in range(0, WIDE, TILE):
            lanes = slice(h, h + TILE)
            scores = jnp.dot(keys, qt_ref[i, :, lanes], preferred_element_type=F32)
            weights = jnp.exp2(scores * SCORE_SCALE - total_scr[i, 0:1, lanes])
            if masked:
                weights = jnp.where(mask, weights, 0.0)
            dweights = jnp.dot(values, dot_ref[i, :, lanes], preferred_element_type=F32)
            dscores = (weights * (dweights - delta_scr[i, 0:1, lanes])).astype(BF16)
            w_scr[:, lanes] = weights.astype(BF16)
            ds_scr[:, lanes] = dscores
            dqt_ref[i, :, lanes] += jnp.dot(keys_t, dscores, preferred_element_type=F32)
        dk = jnp.dot(ds_scr[...], qs_ref[i], preferred_element_type=F32)
        dv = jnp.dot(w_scr[...], dos_ref[i], preferred_element_type=F32)
        for half in range(2):
            rows = rows_of(i, 2 * chunk + half)
            part = slice(half * BLOCK, (half + 1) * BLOCK)
            acc_scr[rows, :HEAD] += dk[part]
            acc_scr[rows, HEAD:] += dv[part]

    def sweep(i, step):
        chunks = (counts[i] + 1) // 2

        def body(chunk, carry):
            special = jnp.logical_or(chunk == 0, 2 * chunk + 2 > counts[i])

            @pl.when(special)
            def _():
                step(i, chunk, True)

            @pl.when(jnp.logical_not(special))
            def _():
                step(i, chunk, False)

            return carry

        lax.fori_loop(0, chunks, body, 0)

    def one_block(i, carry):
        sweep(i, first_pass)
        total = jnp.sum(total_scr[i], 0, keepdims=True)
        delta = jnp.sum(delta_scr[i], 0, keepdims=True) / total
        total_scr[i] = jnp.broadcast_to(jnp.log2(total), (8, WIDE))
        delta_scr[i] = jnp.broadcast_to(delta, (8, WIDE))
        sweep(i, second_pass)
        return carry

    lax.fori_loop(0, local_blocks, one_block, 0)
    dkv_ref[...] = acc_scr[...].astype(dkv_ref.dtype)


def attend(counts, slots, qt, dot, qs, dos, kv):
    local_blocks = qt.shape[0]
    smem = pl.BlockSpec(memory_space=pltpu.SMEM)
    vmem = pl.BlockSpec(memory_space=pltpu.VMEM)
    return pl.pallas_call(
        attend_kernel,
        in_specs=[smem, smem] + [vmem] * 5,
        out_specs=[vmem, vmem],
        out_shape=[
            jax.ShapeDtypeStruct((local_blocks, HEAD, WIDE), F32),
            jax.ShapeDtypeStruct(kv.shape, BF16),
        ],
        scratch_shapes=[
            pltpu.VMEM((kv.shape[0] // BLOCK, HEAD, BLOCK), BF16),
            pltpu.VMEM((local_blocks, 8, WIDE), F32),
            pltpu.VMEM((local_blocks, 8, WIDE), F32),
            pltpu.VMEM((TILE, WIDE), BF16),
            pltpu.VMEM((TILE, WIDE), BF16),
            pltpu.VMEM(kv.shape, F32),
        ],
        compiler_params=pltpu.CompilerParams(vmem_limit_bytes=48 << 20),
        name="attend",
    )(counts, slots, qt, dot, qs, dos, kv)


def shards(
    queries,
    key_vector_rows,
    value_vector_rows,
    output_gradient,
    key_lists,
    block_counts,
    span_table,
):
    local_blocks = queries.shape[0] // BLOCK
    kv_devices = lax.axis_size("kvh")
    per_kvh = key_vector_rows.shape[0]
    kv_rows = jnp.stack(
        [key_vector_rows.reshape(per_kvh, kv_devices, HEAD), value_vector_rows.reshape(per_kvh, kv_devices, HEAD)], 2
    )
    kv_rows = jnp.transpose(kv_rows, (1, 0, 2, 3)).reshape(kv_devices * per_kvh, 2 * HEAD)
    kv_head = lax.all_to_all(kv_rows, "kvh", split_axis=0, concat_axis=0, tiled=True)
    kv_all = lax.all_gather(kv_head, "seq", axis=0, tiled=True)

    first_slot = lax.axis_index("seq") * local_blocks
    positions = lax.dynamic_slice_in_dim(span_table, first_slot, local_blocks, 0)
    counts = block_counts[positions]
    lists = key_lists[positions]
    slot_ids = jnp.arange(span_table.shape[0], dtype=jnp.int32)
    slots = jnp.sum(
        jnp.where(lists[:, :, None] == span_table[None, None, :], slot_ids, 0), -1, dtype=jnp.int32
    )

    def by_head(x):
        x = x.reshape(local_blocks, BLOCK, GROUP, HEAD)
        stacked = jnp.transpose(x, (0, 2, 1, 3)).reshape(local_blocks, WIDE, HEAD)
        turned = jnp.transpose(x, (0, 3, 2, 1)).reshape(local_blocks, HEAD, WIDE)
        return stacked, turned

    qs, qt = by_head(queries)
    dos, dot = by_head(output_gradient)
    dqt, dkv = attend(counts, slots, qt, dot, qs, dos, kv_all)
    dq = jnp.transpose(dqt.reshape(local_blocks, HEAD, GROUP, BLOCK), (0, 3, 2, 1)) * SCALE
    grad_queries = dq.reshape(queries.shape).astype(BF16)

    seq_devices = lax.axis_size("seq")
    parts = lax.all_to_all(
        dkv.reshape(seq_devices, local_blocks * BLOCK, 2 * HEAD), "seq", split_axis=0, concat_axis=0
    )
    sums = jnp.sum(parts.astype(F32), 0)
    sums = jnp.concatenate([sums[:, :HEAD] * SCALE, sums[:, HEAD:]], 1).astype(BF16)
    mine = lax.all_to_all(
        sums.reshape(kv_devices, per_kvh, 2 * HEAD), "kvh", split_axis=0, concat_axis=0
    )
    mine = jnp.transpose(mine, (1, 0, 2)).reshape(per_kvh, kv_devices, 2, HEAD)
    key_gradient = mine[:, :, 0].reshape(per_kvh, kv_devices * HEAD)
    value_gradient = mine[:, :, 1].reshape(per_kvh, kv_devices * HEAD)
    return grad_queries, key_gradient, value_gradient


def solution(mesh):
    placed = (
        P("seq", "kvh"),
        P(("seq", "kvh"), None),
        P(("seq", "kvh"), None),
        P("seq", "kvh"),
        P(),
        P(),
        P(),
    )
    return jax.shard_map(
        shards,
        mesh=mesh,
        in_specs=placed,
        out_specs=(P("seq", "kvh"), P(("seq", "kvh"), None), P(("seq", "kvh"), None)),
        check_vma=False,
    )
```

time: 952 us -> 170 us (0.18)
  the two profiles are of different devices: /device:TPU:0 before, /device:TPU:16 now
where the time goes in v1:
time: 170 us; the launch traced here: 173 us
  waiting for transfers between devices  86.1 us (51%)
  starting transfers between devices  30.4 us (18%)
  Pallas kernels  22.3 us (13%)
  between operations  14.2 us (8%)
  local copies, waits for them, and re-layouts  10.5 us (6%)
  blocking collectives  7.53 us (4%)
    all_to_all x1, waiting for transfers between devices, shards(): lax.all_to_all(dkv.reshape(seq_devices, local_blocks * BLOCK, 2 * HEAD),...  47.5 us
    all_gather x1, waiting for transfers between devices, shards(): kv_all = lax.all_gather(kv_head, 'seq', axis=0, tiled=True)  35.5 us
    all_to_all x1, starting transfers between devices, shards(): lax.all_to_all(dkv.reshape(seq_devices, local_blocks * BLOCK, 2 * HEAD),...  27 us
    pallas_call x1, Pallas kernels, attend(): pl.pallas_call(attend_kernel, in_specs=[smem, smem] + [vmem] * 5, out_spe...  22.3 us
    all_to_all x1, blocking collectives, shards(): lax.all_to_all(kv_rows, 'kvh', split_axis=0, concat_axis=0, tiled=True)  7.53 us
    unnamed x17, local copies, waits for them, and re-layouts  5.14 us
  transfers between devices with their start and end apart: 3, of which 3 were waited for; matrix products, arithmetic and copies ran while one was open for 3% of the time, Pallas kernels for 0%

profile of v1, /device:TPU:16, one launch (start us, length us, event | category | flops | bytes accessed | tf_op | source)
XLA Modules:
  0.0 172.6 jit_solution(15911245206612007714)
XLA Ops:
  7.2 0.0 copy-start
  7.2 0.0 all-gather.2.cloned.1.call-start
  7.2 0.9 stack_reshape.6
  8.1 0.9 stack_reshape.7
  8.9 0.2 maximum_bitcast_fusion
  9.1 0.0 copy-start.2
  9.2 0.1 copy.41
  9.3 0.1 all_to_all.14
  9.4 7.5 %all_to_all.22 = bf16[2,128,256]{2,1,0:T(8,128)(2,1)} all-to-all(bf16[2,128,256]{2,1,0:T(8,128)(2,1)S(1)} %all_to_all.14), channel_id=1, replica_groups=mesh['seq'=16,'kvh'=2] {'kvh'}, dimensions={0} | all-to-all | bytes 262144 | tf_op jit(solution)/shard_map/all_to_all | solution.py:180
  16.9 0.0 all-gather.2.cloned.1.call-update
  16.9 1.1 copy.46
  18.1 0.1 copy.39
  18.2 0.0 copy-start.3
  18.2 0.0 copy-start.4
  18.2 0.5 copy.37
  18.7 0.0 copy-done.2
  18.7 0.1 copy.47
  18.8 0.1 copy.40
  18.9 0.5 copy.38
  19.4 0.0 copy-done.3
  19.4 0.1 copy.36
  19.4 0.0 copy-done.4
  19.4 0.1 compare_select_fusion
  19.5 0.0 copy-done
  19.5 0.6 gather_fusion
  20.2 0.6 gather_fusion.1
  20.7 0.2 reshape.48.qt_ref
  21.0 0.2 reshape.50.dot_ref
  21.2 0.2 select_reduce_fusion.slots
  21.4 35.5 %all-gather.2.cloned.1.call-done.kv_ref = bf16[4096,256]{1,0:T(8,128)(2,1)} async-done(((bf16[256,256]{1,0:T(8,128)(2,1)}), bf16[4096,256]{1,0:T(8,128)(2,1)}) %all-gather.2.cloned.1.call-update) | async-done | bytes 2097168 | tf_op jit(solution)/shard_map/all_gather | solution.py:181
  56.9 22.3 %attend.1 = (f32[2,128,1024]{2,1,0:T(8,128)S(1)}, bf16[4096,256]{1,0:T(8,128)(2,1)S(1)}) custom-call(s32[2]{0:T(128)S(1)} %gather_fusion, s32[2,24]{1,0:T(2,128)S(1)} %select_reduce_fusion.slots, bf16[2,128,1024]{2,1,0:T(8,128)(2,1)S(1)} %reshape.48.qt_ref, bf16[2,128,1024]{2,1,0:T(8,128)(2,1)S(1)} %reshape.50.dot_ref, bf16[2,1024,128]{2,1,0:T(8,128)(2,1)S(1)} %bitcast.41, ...), custom_call_target="tpu_custom_call" | custom-call | tf_op jit(solution)/shard_map/attend/pallas_call | solution.py:143
  79.2 0.0 copy-start.1
  79.2 1.3 copy-done.1
  80.6 27.0 %all-to-all-start.1 = ((bf16[16,256,256]{2,1,0:T(8,128)(2,1)}), bf16[16,256,256]{2,1,0:T(8,128)(2,1)S(1)}, u32[]{:S(2)}, u32[]{:S(2)}) async-start(bf16[16,256,256]{2,1,0:T(8,128)(2,1)} %bitcast.43), calls=%async_computation.1 | async-start | bytes 4194304 | tf_op jit(solution)/shard_map/all_to_all | solution.py:205
  107.6 0.1 multiply_convert_fusion
  107.7 0.1 copy.48
  107.8 47.5 %all-to-all-done.1 = bf16[16,256,256]{2,1,0:T(8,128)(2,1)S(1)} async-done(((bf16[16,256,256]{2,1,0:T(8,128)(2,1)}), bf16[16,256,256]{2,1,0:T(8,128)(2,1)S(1)}, u32[]{:S(2)}, u32[]{:S(2)}) %all-to-all-start.1) | async-done | bytes 2097184 | tf_op jit(solution)/shard_map/all_to_all | solution.py:205
  155.2 0.3 convert_reduce_fusion
  155.6 0.7 pad_maximum_fusion
  156.3 3.4 %all-to-all-start.2 = ((bf16[2,128,256]{2,1,0:T(8,128)(2,1)}), bf16[2,128,256]{2,1,0:T(8,128)(2,1)S(1)}, u32[]{:S(2)}, u32[]{:S(2)}) async-start(bf16[2,128,256]{2,1,0:T(8,128)(2,1)} %pad_maximum_fusion), calls=%async_computation.2 | async-start | bytes 262144 | tf_op jit(solution)/shard_map/all_to_all | solution.py:210
  159.7 0.5 copy.42
  160.1 0.9 copy.51
  161.0 3.1 %all-to-all-done.2 = bf16[2,128,256]{2,1,0:T(8,128)(2,1)S(1)} async-done(((bf16[2,128,256]{2,1,0:T(8,128)(2,1)}), bf16[2,128,256]{2,1,0:T(8,128)(2,1)S(1)}, u32[]{:S(2)}, u32[]{:S(2)}) %all-to-all-start.2) | async-done | bytes 131104 | tf_op jit(solution)/shard_map/all_to_all | solution.py:210
  164.1 0.1 copy.43
  164.2 0.7 copy.45
  165.0 0.7 copy.44
  (5 shorter events, 0.1 us)
Async XLA Ops:
  7.2 12.4 %copy-start = (s32[32]{0:T(128)S(1)}, s32[32]{0:T(128)}, u32[]{:S(2)}) copy-start(s32[32]{0:T(128)} %param.12) | copy-start | bytes 388
  7.2 49.7 %all-gather.2.cloned.1.call-start = ((), (), s32[]{:S(2)}) async-start(), calls=%async_computation.3 | async-start | bytes 2228224 | tf_op jit(solution)/shard_map/all_gather | solution.py:181
  9.1 9.5 %copy-start.2 = (bf16[256,1024]{1,0:T(8,128)(2,1)S(1)}, bf16[256,1024]{1,0:T(8,128)(2,1)}, u32[]{:S(2)}) copy-start(bf16[256,1024]{1,0:T(8,128)(2,1)} %param.10) | copy-start | bytes 1572868
  18.2 1.2 copy-start.3
  18.2 1.2 copy-start.4
  79.2 1.3 copy-start.1
  80.6 74.7 %all-to-all-start.1 = ((bf16[16,256,256]{2,1,0:T(8,128)(2,1)}), bf16[16,256,256]{2,1,0:T(8,128)(2,1)S(1)}, u32[]{:S(2)}, u32[]{:S(2)}) async-start(bf16[16,256,256]{2,1,0:T(8,128)(2,1)} %bitcast.43), calls=%async_computation.1 | async-start | bytes 4194304 | tf_op jit(solution)/shard_map/all_to_all | solution.py:205
  156.3 7.8 %all-to-all-start.2 = ((bf16[2,128,256]{2,1,0:T(8,128)(2,1)}), bf16[2,128,256]{2,1,0:T(8,128)(2,1)S(1)}, u32[]{:S(2)}, u32[]{:S(2)}) async-start(bf16[2,128,256]{2,1,0:T(8,128)(2,1)} %pad_maximum_fusion), calls=%async_computation.2 | async-start | bytes 262144 | tf_op jit(solution)/shard_map/all_to_all | solution.py:210
Sparse Core Ops, SparseCore 0:
  17.1 39.7 all-gather.1

commit v2 on v1

--- a/solution.py
+++ b/solution.py
@@ -19,29 +19,36 @@
 F32 = jnp.float32
 
 
-def attend_kernel(
-    counts,
-    slots,
-    qt_ref,
-    dot_ref,
-    qs_ref,
-    dos_ref,
-    kv_ref,
-    dqt_ref,
-    dkv_ref,
-    kt_scr,
-    total_scr,
-    delta_scr,
-    w_scr,
-    ds_scr,
-    acc_scr,
-):
+def attend_kernel(groups, pieces, place, counts, slots, qt_ref, dot_ref, qs_ref, dos_ref, *refs):
+    group_refs, refs = refs[:groups], refs[groups:]
+    dqt_ref, refs = refs[0], refs[1:]
+    out_refs, refs = refs[:groups], refs[groups:]
+    kv_ref, kt_scr, total_scr, delta_scr, w_scr, ds_scr, acc_scr, sems = refs
     local_blocks = qt_ref.shape[0]
     n_slots = kv_ref.shape[0] // BLOCK
+    span = kv_ref.shape[0] // groups
+    part = span // pieces
+
+    def rows_at(p, j):
+        return pl.ds(pl.multiple_of(p * span + (place[0] ^ j) * part, part), part)
+
+    copies = []
+    for p in range(groups):
+        for j in range(pieces):
+            copies.append(
+                pltpu.make_async_copy(
+                    group_refs[p].at[pl.ds(j * part, part)], kv_ref.at[rows_at(p, j)], sems.at[p, j]
+                )
+            )
+    for copy in copies:
+        copy.start()
     acc_scr[...] = jnp.zeros_like(acc_scr)
     dqt_ref[...] = jnp.zeros_like(dqt_ref)
     total_scr[...] = jnp.zeros_like(total_scr)
     delta_scr[...] = jnp.zeros_like(delta_scr)
+
+    for copy in copies:
+        copy.wait()
 
     def turn(j, carry):
         rows = pl.ds(pl.multiple_of(j * BLOCK, BLOCK), BLOCK)
@@ -133,32 +140,35 @@
         return carry
 
     lax.fori_loop(0, local_blocks, one_block, 0)
-    dkv_ref[...] = acc_scr[...].astype(dkv_ref.dtype)
-
-
-def attend(counts, slots, qt, dot, qs, dos, kv):
+    for p in range(groups):
+        for j in range(pieces):
+            out_refs[p][j * part : (j + 1) * part] = acc_scr[rows_at(p, j)].astype(out_refs[p].dtype)
+
+
+def attend(place, counts, slots, qt, dot, qs, dos, groups, pieces):
     local_blocks = qt.shape[0]
+    rows = groups[0].shape[0] * len(groups)
     smem = pl.BlockSpec(memory_space=pltpu.SMEM)
     vmem = pl.BlockSpec(memory_space=pltpu.VMEM)
     return pl.pallas_call(
-        attend_kernel,
-        in_specs=[smem, smem] + [vmem] * 5,
-        out_specs=[vmem, vmem],
-        out_shape=[
-            jax.ShapeDtypeStruct((local_blocks, HEAD, WIDE), F32),
-            jax.ShapeDtypeStruct(kv.shape, BF16),
-        ],
+        functools.partial(attend_kernel, len(groups), pieces),
+        in_specs=[smem] * 3 + [vmem] * 4 + [pl.BlockSpec(memory_space=pl.ANY)] * len(groups),
+        out_specs=[vmem] * (1 + len(groups)),
+        out_shape=[jax.ShapeDtypeStruct((local_blocks, HEAD, WIDE), F32)]
+        + [jax.ShapeDtypeStruct(g.shape, BF16 if p & 1 else F32) for p, g in enumerate(groups)],
         scratch_shapes=[
-            pltpu.VMEM((kv.shape[0] // BLOCK, HEAD, BLOCK), BF16),
+            pltpu.VMEM((rows, 2 * HEAD), BF16),
+            pltpu.VMEM((rows // BLOCK, HEAD, BLOCK), BF16),
             pltpu.VMEM((local_blocks, 8, WIDE), F32),
             pltpu.VMEM((local_blocks, 8, WIDE), F32),
             pltpu.VMEM((TILE, WIDE), BF16),
             pltpu.VMEM((TILE, WIDE), BF16),
-            pltpu.VMEM(kv.shape, F32),
+            pltpu.VMEM((rows, 2 * HEAD), F32),
+            pltpu.SemaphoreType.DMA((len(groups), pieces)),
         ],
         compiler_params=pltpu.CompilerParams(vmem_limit_bytes=48 << 20),
         name="attend",
-    )(counts, slots, qt, dot, qs, dos, kv)
+    )(place, counts, slots, qt, dot, qs, dos, *groups)
 
 
 def shards(
@@ -171,20 +181,48 @@
     span_table,
 ):
     local_blocks = queries.shape[0] // BLOCK
-    kv_devices = lax.axis_size("kvh")
+    seq_devices, kv_devices = lax.axis_size("seq"), lax.axis_size("kvh")
+    seq_at, kv_at = lax.axis_index("seq"), lax.axis_index("kvh")
     per_kvh = key_vector_rows.shape[0]
-    kv_rows = jnp.stack(
-        [key_vector_rows.reshape(per_kvh, kv_devices, HEAD), value_vector_rows.reshape(per_kvh, kv_devices, HEAD)], 2
-    )
-    kv_rows = jnp.transpose(kv_rows, (1, 0, 2, 3)).reshape(kv_devices * per_kvh, 2 * HEAD)
-    kv_head = lax.all_to_all(kv_rows, "kvh", split_axis=0, concat_axis=0, tiled=True)
-    kv_all = lax.all_gather(kv_head, "seq", axis=0, tiled=True)
-
-    first_slot = lax.axis_index("seq") * local_blocks
+
+    def swap(x, seq_step, kv_step):
+        if seq_step == 0 and kv_step == 0:
+            return x
+        pairs = [
+            (s * kv_devices + h, (s ^ seq_step) * kv_devices + (h ^ kv_step))
+            for s in range(seq_devices)
+            for h in range(kv_devices)
+        ]
+        return lax.ppermute(x, ("seq", "kvh"), pairs)
+
+    def head_rows(head):
+        start = head * HEAD
+        return jnp.concatenate(
+            [
+                lax.dynamic_slice_in_dim(key_vector_rows, start, HEAD, 1),
+                lax.dynamic_slice_in_dim(value_vector_rows, start, HEAD, 1),
+            ],
+            1,
+        )
+
+    to_send = [head_rows(kv_at ^ j) for j in range(kv_devices)]
+    far_first = range(seq_devices - 4, -1, -4)
+    groups = [None] * seq_devices
+    for far in far_first:
+        groups[far] = jnp.concatenate(
+            [swap(to_send[j], far, j) for j in range(kv_devices)], 0
+        )
+    for far in far_first:
+        groups[far + 2] = swap(groups[far], 2, 0)
+    for far in far_first:
+        groups[far + 1] = swap(groups[far], 1, 0)
+        groups[far + 3] = swap(groups[far + 2], 1, 0)
+
+    first_slot = seq_at * local_blocks
     positions = lax.dynamic_slice_in_dim(span_table, first_slot, local_blocks, 0)
     counts = block_counts[positions]
     lists = key_lists[positions]
-    slot_ids = jnp.arange(span_table.shape[0], dtype=jnp.int32)
+    slot_ids = jnp.arange(span_table.shape[0], dtype=jnp.int32) ^ first_slot
     slots = jnp.sum(
         jnp.where(lists[:, :, None] == span_table[None, None, :], slot_ids, 0), -1, dtype=jnp.int32
     )
@@ -197,22 +235,23 @@
 
     qs, qt = by_head(queries)
     dos, dot = by_head(output_gradient)
-    dqt, dkv = attend(counts, slots, qt, dot, qs, dos, kv_all)
+    place = jnp.full((1,), kv_at, jnp.int32)
+    dqt, *partials = attend(place, counts, slots, qt, dot, qs, dos, groups, kv_devices)
     dq = jnp.transpose(dqt.reshape(local_blocks, HEAD, GROUP, BLOCK), (0, 3, 2, 1)) * SCALE
     grad_queries = dq.reshape(queries.shape).astype(BF16)
 
-    seq_devices = lax.axis_size("seq")
-    parts = lax.all_to_all(
-        dkv.reshape(seq_devices, local_blocks * BLOCK, 2 * HEAD), "seq", split_axis=0, concat_axis=0
-    )
-    sums = jnp.sum(parts.astype(F32), 0)
-    sums = jnp.concatenate([sums[:, :HEAD] * SCALE, sums[:, HEAD:]], 1).astype(BF16)
-    mine = lax.all_to_all(
-        sums.reshape(kv_devices, per_kvh, 2 * HEAD), "kvh", split_axis=0, concat_axis=0
-    )
-    mine = jnp.transpose(mine, (1, 0, 2)).reshape(per_kvh, kv_devices, 2, HEAD)
-    key_gradient = mine[:, :, 0].reshape(per_kvh, kv_devices * HEAD)
-    value_gradient = mine[:, :, 1].reshape(per_kvh, kv_devices * HEAD)
+    sums = [0.0] * kv_devices
+    for far in far_first:
+        near = [partials[far + y] + swap(partials[far + y + 1], 1, 0).astype(F32) for y in (0, 2)]
+        other = swap(near[1].astype(BF16), 2, 0)
+        chip = (near[0] + other.astype(F32)).astype(BF16)
+        for j in range(kv_devices):
+            got = swap(chip[j * per_kvh : (j + 1) * per_kvh], far, j)
+            sums[j] = sums[j] + got.astype(F32)
+    stacked = jnp.stack(sums)
+    heads = [lax.dynamic_index_in_dim(stacked, kv_at ^ j, 0, False) for j in range(kv_devices)]
+    key_gradient = jnp.concatenate([x[:, :HEAD] * SCALE for x in heads], 1).astype(BF16)
+    value_gradient = jnp.concatenate([x[:, HEAD:] for x in heads], 1).astype(BF16)
     return grad_queries, key_gradient, value_gradient
 
 

time: 170 us -> 135 us (0.79)
  the two profiles are of different devices: /device:TPU:16 before, /device:TPU:0 now
where the time goes in v2:
time: 135 us; the launch traced here: 137 us
  starting transfers between devices  54.6 us (40%)
  Pallas kernels  32.2 us (24%)
  local copies, waits for them, and re-layouts  23.3 us (17%)
  waiting for transfers between devices  21.7 us (16%)
  other arithmetic  4.3 us (3%)
    ppermute x38, starting transfers between devices, swap(): return lax.ppermute(x, ('seq', 'kvh'), pairs)  54.6 us
    pallas_call x1, Pallas kernels, attend(): pl.pallas_call(functools.partial(attend_kernel, len(groups), pieces), in_...  32.2 us
    ppermute x38, waiting for transfers between devices, swap(): return lax.ppermute(x, ('seq', 'kvh'), pairs)  21.7 us
    unnamed x68, local copies, waits for them, and re-layouts  16 us
    reshape x4, local copies, waits for them, and re-layouts, by_head(): x = x.reshape(local_blocks, BLOCK, GROUP, HEAD)  2.72 us
  transfers between devices with their start and end apart: 38, of which 10 were waited for; matrix products, arithmetic and copies ran while one was open for 9% of the time, Pallas kernels for 0%

profile of v2, /device:TPU:0, one launch (start us, length us, event | category | flops | bytes accessed | tf_op | source)
XLA Modules:
  0.0 137.3 jit_solution(3116665934130669115)
XLA Ops:
  0.7 0.8 constant_dynamic-slice_fusion.2
  1.5 4.1 %collective-permute-start.9 = (bf16[128,256]{1,0:T(8,128)(2,1)S(1)}, bf16[128,256]{1,0:T(8,128)(2,1)S(1)}, u32[]{:S(2)}, u32[]{:S(2)}) collective-permute-start(bf16[128,256]{1,0:T(8,128)(2,1)S(1)} %pad_maximum_fusion.1), channel_id=1, source_target_pairs={{0,16},{1,17},{2,18},{3,19},{4,20},{5,21},{6,22},{7,23},{8,24},{9,... | collective-permute-start | bytes 196616 | tf_op jit(solution)/shard_map/ppermute | solution.py:196
  5.6 1.3 collective-permute-start.14
  7.0 2.7 %collective-permute-start.10 = (bf16[128,256]{1,0:T(8,128)(2,1)S(1)}, bf16[128,256]{1,0:T(8,128)(2,1)S(1)}, u32[]{:S(2)}, u32[]{:S(2)}) collective-permute-start(bf16[128,256]{1,0:T(8,128)(2,1)S(1)} %pad_maximum_fusion.2), channel_id=1, source_target_pairs={{0,17},{1,16},{2,19},{3,18},{4,21},{5,20},{6,23},{7,22},{8,25},{9,... | collective-permute-start | bytes 196616 | tf_op jit(solution)/shard_map/ppermute | solution.py:196
  9.6 0.9 collective-permute-start.15
  10.5 0.9 collective-permute-start.4
  11.4 3.3 %collective-permute-start.5 = (bf16[128,256]{1,0:T(8,128)(2,1)S(1)}, bf16[128,256]{1,0:T(8,128)(2,1)S(1)}, u32[]{:S(2)}, u32[]{:S(2)}) collective-permute-start(bf16[128,256]{1,0:T(8,128)(2,1)S(1)} %pad_maximum_fusion.2), channel_id=1, source_target_pairs={{0,9},{1,8},{2,11},{3,10},{4,13},{5,12},{6,15},{7,14},{8,1},{9,0},... | collective-permute-start | bytes 196616 | tf_op jit(solution)/shard_map/ppermute | solution.py:196
  14.8 2.9 %collective-permute-done.10 = bf16[128,256]{1,0:T(8,128)(2,1)S(1)} collective-permute-done((bf16[128,256]{1,0:T(8,128)(2,1)S(1)}, bf16[128,256]{1,0:T(8,128)(2,1)S(1)}, u32[]{:S(2)}, u32[]{:S(2)}) %collective-permute-start.10) | collective-permute-done | bytes 65568 | tf_op jit(solution)/shard_map/ppermute | solution.py:196
  18.2 1.6 %collective-permute-start.12 = (bf16[256,256]{1,0:T(8,128)(2,1)S(1)}, bf16[256,256]{1,0:T(8,128)(2,1)S(1)}, u32[]{:S(2)}, u32[]{:S(2)}) collective-permute-start(bf16[256,256]{1,0:T(8,128)(2,1)S(1)} %constant_dynamic-update-slice_fusion.2.refs_8_), channel_id=1, source_target_pairs={{0,4},{1,5},{2,6},{3,7},{4,0},{5,1},{6,2},{7,3},{8,12},{9,13},{10,... | collective-permute-start | bytes 393224 | tf_op jit(solution)/shard_map/ppermute | solution.py:196
  20.7 1.2 collective-permute-done
  21.9 1.5 %collective-permute-start.7 = (bf16[256,256]{1,0:T(8,128)(2,1)S(1)}, bf16[256,256]{1,0:T(8,128)(2,1)S(1)}, u32[]{:S(2)}, u32[]{:S(2)}) collective-permute-start(bf16[256,256]{1,0:T(8,128)(2,1)S(1)} %constant_dynamic-update-slice_fusion.refs_4_), channel_id=1, source_target_pairs={{0,4},{1,5},{2,6},{3,7},{4,0},{5,1},{6,2},{7,3},{8,12},{9,13},{10,... | collective-permute-start | bytes 393224 | tf_op jit(solution)/shard_map/ppermute | solution.py:196
  23.5 2.8 %collective-permute-done.17.refs_14_ = bf16[256,256]{1,0:T(8,128)(2,1)S(1)} collective-permute-done((bf16[256,256]{1,0:T(8,128)(2,1)S(1)}, bf16[256,256]{1,0:T(8,128)(2,1)S(1)}, u32[]{:S(2)}, u32[]{:S(2)}) %collective-permute-start.17) | collective-permute-done | bytes 131104 | tf_op jit(solution)/shard_map/ppermute | solution.py:196
  26.3 2.5 %collective-permute-start.2 = (bf16[256,256]{1,0:T(8,128)(2,1)S(1)}, bf16[256,256]{1,0:T(8,128)(2,1)S(1)}, u32[]{:S(2)}, u32[]{:S(2)}) collective-permute-start(bf16[256,256]{1,0:T(8,128)(2,1)S(1)} %pad_maximum_fusion.refs_0_), channel_id=1, source_target_pairs={{0,4},{1,5},{2,6},{3,7},{4,0},{5,1},{6,2},{7,3},{8,12},{9,13},{10,... | collective-permute-start | bytes 393224 | tf_op jit(solution)/shard_map/ppermute | solution.py:196
  30.2 1.6 %collective-permute-done.2.refs_2_ = bf16[256,256]{1,0:T(8,128)(2,1)S(1)} collective-permute-done((bf16[256,256]{1,0:T(8,128)(2,1)S(1)}, bf16[256,256]{1,0:T(8,128)(2,1)S(1)}, u32[]{:S(2)}, u32[]{:S(2)}) %collective-permute-start.2) | collective-permute-done | bytes 131104 | tf_op jit(solution)/shard_map/ppermute | solution.py:196
  32.9 0.9 copy.25
  34.5 0.9 copy.26
  37.0 1.0 reshape.35.dot_ref
  38.2 0.6 copy-done.9
  38.8 0.7 copy-done.11
  39.5 0.6 copy-done.13
  40.1 0.7 copy-done.15
  40.8 0.6 copy-done.17
  41.4 0.9 copy-done.2
  42.3 0.9 copy-done.4
  43.2 0.9 copy-done.6
  44.1 0.9 copy-done.8
  45.0 0.9 copy-done.10
  45.9 0.9 copy-done.12
  46.9 0.9 copy-done.14
  47.8 0.9 copy-done.16
  48.7 0.9 copy-done.18
  49.6 32.2 %attend.1 = (f32[2,128,1024]{2,1,0:T(8,128)}, f32[256,256]{1,0:T(8,128)S(1)}, bf16[256,256]{1,0:T(8,128)(2,1)}, f32[256,256]{1,0:T(8,128)S(1)}, bf16[256,256]{1,...) custom-call(s32[1]{0:T(128)} %bitcast.place, ...), custom_call_target="tpu_custom_call" | custom-call | tf_op jit(solution)/shard_map/attend/pallas_call | solution.py:153
  82.9 1.3 multiply_convert_fusion
  84.4 1.3 copy.27
  85.7 2.0 %copy.33 = bf16[32,8,8,128]{3,1,2,0:T(8,128)(2,1)} copy(bf16[32,8,8,128]{3,2,1,0:T(8,128)(2,1)} %bitcast.48) | data formatting | bytes 1048576
  88.7 1.0 add_convert_fusion.1
  89.9 0.9 copy-done.20
  91.2 9.2 %collective-permute-start.21 = (bf16[256,256]{1,0:T(8,128)(2,1)S(1)}, bf16[256,256]{1,0:T(8,128)(2,1)S(1)}, u32[]{:S(2)}, u32[]{:S(2)}) collective-permute-start(bf16[256,256]{1,0:T(8,128)(2,1)S(1)} %add_convert_fusion.7), channel_id=1, source_target_pairs={{0,4},{1,5},{2,6},{3,7},{4,0},{5,1},{6,2},{7,3},{8,12},{9,13},{10,... | collective-permute-start | bytes 393224 | tf_op jit(solution)/shard_map/ppermute | solution.py:196
  100.6 4.2 %collective-permute-done.21 = bf16[256,256]{1,0:T(8,128)(2,1)S(1)} collective-permute-done((bf16[256,256]{1,0:T(8,128)(2,1)S(1)}, bf16[256,256]{1,0:T(8,128)(2,1)S(1)}, u32[]{:S(2)}, u32[]{:S(2)}) %collective-permute-start.21) | collective-permute-done | bytes 131104 | tf_op jit(solution)/shard_map/ppermute | solution.py:196
  104.7 2.1 %collective-permute-start.25 = (bf16[256,256]{1,0:T(8,128)(2,1)S(1)}, bf16[256,256]{1,0:T(8,128)(2,1)S(1)}, u32[]{:S(2)}, u32[]{:S(2)}) collective-permute-start(bf16[256,256]{1,0:T(8,128)(2,1)S(1)} %add_convert_fusion.5), channel_id=1, source_target_pairs={{0,4},{1,5},{2,6},{3,7},{4,0},{5,1},{6,2},{7,3},{8,12},{9,13},{10,... | collective-permute-start | bytes 393224 | tf_op jit(solution)/shard_map/ppermute | solution.py:196
  107.0 4.2 %collective-permute-done.25 = bf16[256,256]{1,0:T(8,128)(2,1)S(1)} collective-permute-done((bf16[256,256]{1,0:T(8,128)(2,1)S(1)}, bf16[256,256]{1,0:T(8,128)(2,1)S(1)}, u32[]{:S(2)}, u32[]{:S(2)}) %collective-permute-start.25) | collective-permute-done | bytes 131104 | tf_op jit(solution)/shard_map/ppermute | solution.py:196
  111.2 12.3 %collective-permute-start.22 = (bf16[128,256]{1,0:T(8,128)(2,1)S(1)}, bf16[128,256]{1,0:T(8,128)(2,1)S(1)}, u32[]{:S(2)}, u32[]{:S(2)}) collective-permute-start(bf16[128,256]{1,0:T(8,128)(2,1)S(1)} %get-tuple-element.40), channel_id=1, source_target_pairs={{0,24},{1,25},{2,26},{3,27},{4,28},{5,29},{6,30},{7,31},{8,16},{9,... | collective-permute-start | bytes 196616 | tf_op jit(solution)/shard_map/ppermute | solution.py:196
  124.4 1.6 %collective-permute-start.37 = (bf16[128,256]{1,0:T(8,128)(2,1)S(1)}, bf16[128,256]{1,0:T(8,128)(2,1)S(1)}, u32[]{:S(2)}, u32[]{:S(2)}) collective-permute-start(bf16[128,256]{1,0:T(8,128)(2,1)S(1)} %slice.61), channel_id=1, source_target_pairs={{0,1},{1,0},{2,3},{3,2},{4,5},{5,4},{6,7},{7,6},{8,9},{9,8},{10,11... | collective-permute-start | bytes 196616 | tf_op jit(solution)/shard_map/ppermute | solution.py:196
  126.0 3.8 %collective-permute-start.34 = (bf16[128,256]{1,0:T(8,128)(2,1)S(1)}, bf16[128,256]{1,0:T(8,128)(2,1)S(1)}, u32[]{:S(2)}, u32[]{:S(2)}) collective-permute-start(bf16[128,256]{1,0:T(8,128)(2,1)S(1)} %get-tuple-element.39), channel_id=1, source_target_pairs={{0,25},{1,24},{2,27},{3,26},{4,29},{5,28},{6,31},{7,30},{8,17},{9,... | collective-permute-start | bytes 196616 | tf_op jit(solution)/shard_map/ppermute | solution.py:196
  129.8 1.4 %collective-permute-start.36 = (bf16[128,256]{1,0:T(8,128)(2,1)S(1)}, bf16[128,256]{1,0:T(8,128)(2,1)S(1)}, u32[]{:S(2)}, u32[]{:S(2)}) collective-permute-start(bf16[128,256]{1,0:T(8,128)(2,1)S(1)} %get-tuple-element.43), channel_id=1, source_target_pairs={{0,9},{1,8},{2,11},{3,10},{4,13},{5,12},{6,15},{7,14},{8,1},{9,0},... | collective-permute-start | bytes 196616 | tf_op jit(solution)/shard_map/ppermute | solution.py:196
  131.3 2.0 %collective-permute-done.34 = bf16[128,256]{1,0:T(8,128)(2,1)S(1)} collective-permute-done((bf16[128,256]{1,0:T(8,128)(2,1)S(1)}, bf16[128,256]{1,0:T(8,128)(2,1)S(1)}, u32[]{:S(2)}, u32[]{:S(2)}) %collective-permute-start.34) | collective-permute-done | bytes 65568 | tf_op jit(solution)/shard_map/ppermute | solution.py:196
  133.3 2.5 %collective-permute-done.35 = bf16[128,256]{1,0:T(8,128)(2,1)S(1)} collective-permute-done((bf16[128,256]{1,0:T(8,128)(2,1)S(1)}, bf16[128,256]{1,0:T(8,128)(2,1)S(1)}, u32[]{:S(2)}, u32[]{:S(2)}) %collective-permute-start.35) | collective-permute-done | bytes 65568 | tf_op jit(solution)/shard_map/ppermute | solution.py:196
  136.0 0.6 pad_maximum_fusion.4
  (140 shorter events, 11.5 us)
Async XLA Ops:
  0.6 35.4 %copy-start = (s32[32]{0:T(128)S(1)}, s32[32]{0:T(128)}, u32[]{:S(2)}) copy-start(s32[32]{0:T(128)} %param.12) | copy-start | bytes 388
  1.5 9.9 %collective-permute-start.9 = (bf16[128,256]{1,0:T(8,128)(2,1)S(1)}, bf16[128,256]{1,0:T(8,128)(2,1)S(1)}, u32[]{:S(2)}, u32[]{:S(2)}) collective-permute-start(bf16[128,256]{1,0:T(8,128)(2,1)S(1)} %pad_maximum_fusion.1), channel_id=1, source_target_pairs={{0,16},{1,17},{2,18},{3,19},{4,20},{5,21},{6,22},{7,23},{8,24},{9,... | collective-permute-start | bytes 196616 | tf_op jit(solution)/shard_map/ppermute | solution.py:196
  5.6 12.5 %collective-permute-start.14 = (bf16[128,256]{1,0:T(8,128)(2,1)S(1)}, bf16[128,256]{1,0:T(8,128)(2,1)S(1)}, u32[]{:S(2)}, u32[]{:S(2)}) collective-permute-start(bf16[128,256]{1,0:T(8,128)(2,1)S(1)} %pad_maximum_fusion.1), channel_id=1, source_target_pairs={{0,24},{1,25},{2,26},{3,27},{4,28},{5,29},{6,30},{7,31},{8,16},{9,... | collective-permute-start | bytes 196616 | tf_op jit(solution)/shard_map/ppermute | solution.py:196
  7.0 10.7 %collective-permute-start.10 = (bf16[128,256]{1,0:T(8,128)(2,1)S(1)}, bf16[128,256]{1,0:T(8,128)(2,1)S(1)}, u32[]{:S(2)}, u32[]{:S(2)}) collective-permute-start(bf16[128,256]{1,0:T(8,128)(2,1)S(1)} %pad_maximum_fusion.2), channel_id=1, source_target_pairs={{0,17},{1,16},{2,19},{3,18},{4,21},{5,20},{6,23},{7,22},{8,25},{9,... | collective-permute-start | bytes 196616 | tf_op jit(solution)/shard_map/ppermute | solution.py:196
  9.6 10.1 %collective-permute-start.15 = (bf16[128,256]{1,0:T(8,128)(2,1)S(1)}, bf16[128,256]{1,0:T(8,128)(2,1)S(1)}, u32[]{:S(2)}, u32[]{:S(2)}) collective-permute-start(bf16[128,256]{1,0:T(8,128)(2,1)S(1)} %pad_maximum_fusion.2), channel_id=1, source_target_pairs={{0,25},{1,24},{2,27},{3,26},{4,29},{5,28},{6,31},{7,30},{8,17},{9,... | collective-permute-start | bytes 196616 | tf_op jit(solution)/shard_map/ppermute | solution.py:196
  10.5 9.4 %collective-permute-start.4 = (bf16[128,256]{1,0:T(8,128)(2,1)S(1)}, bf16[128,256]{1,0:T(8,128)(2,1)S(1)}, u32[]{:S(2)}, u32[]{:S(2)}) collective-permute-start(bf16[128,256]{1,0:T(8,128)(2,1)S(1)} %pad_maximum_fusion.1), channel_id=1, source_target_pairs={{0,8},{1,9},{2,10},{3,11},{4,12},{5,13},{6,14},{7,15},{8,0},{9,1},... | collective-permute-start | bytes 196616 | tf_op jit(solution)/shard_map/ppermute | solution.py:196
  11.4 20.3 %copy-start.25 = (bf16[256,1024]{1,0:T(8,128)(2,1)S(1)}, bf16[256,1024]{1,0:T(8,128)(2,1)}, u32[]{:S(2)}) copy-start(bf16[256,1024]{1,0:T(8,128)(2,1)} %param.7) | copy-start | bytes 1572868
  11.4 9.0 %collective-permute-start.5 = (bf16[128,256]{1,0:T(8,128)(2,1)S(1)}, bf16[128,256]{1,0:T(8,128)(2,1)S(1)}, u32[]{:S(2)}, u32[]{:S(2)}) collective-permute-start(bf16[128,256]{1,0:T(8,128)(2,1)S(1)} %pad_maximum_fusion.2), channel_id=1, source_target_pairs={{0,9},{1,8},{2,11},{3,10},{4,13},{5,12},{6,15},{7,14},{8,1},{9,0},... | collective-permute-start | bytes 196616 | tf_op jit(solution)/shard_map/ppermute | solution.py:196
  17.6 4.3 %collective-permute-start = (bf16[128,256]{1,0:T(8,128)(2,1)S(1)}, bf16[128,256]{1,0:T(8,128)(2,1)S(1)}, u32[]{:S(2)}, u32[]{:S(2)}) collective-permute-start(bf16[128,256]{1,0:T(8,128)(2,1)S(1)} %pad_maximum_fusion.2), channel_id=1, source_target_pairs={{0,1},{1,0},{2,3},{3,2},{4,5},{5,4},{6,7},{7,6},{8,9},{9,8},{10,11... | collective-permute-start | bytes 196616 | tf_op jit(solution)/shard_map/ppermute | solution.py:196
  18.2 5.3 %collective-permute-start.12 = (bf16[256,256]{1,0:T(8,128)(2,1)S(1)}, bf16[256,256]{1,0:T(8,128)(2,1)S(1)}, u32[]{:S(2)}, u32[]{:S(2)}) collective-permute-start(bf16[256,256]{1,0:T(8,128)(2,1)S(1)} %constant_dynamic-update-slice_fusion.2.refs_8_), channel_id=1, source_target_pairs={{0,4},{1,5},{2,6},{3,7},{4,0},{5,1},{6,2},{7,3},{8,12},{9,13},{10,... | collective-permute-start | bytes 393224 | tf_op jit(solution)/shard_map/ppermute | solution.py:196
  19.8 9.4 %collective-permute-start.11 = (bf16[256,256]{1,0:T(8,128)(2,1)S(1)}, bf16[256,256]{1,0:T(8,128)(2,1)S(1)}, u32[]{:S(2)}, u32[]{:S(2)}) collective-permute-start(bf16[256,256]{1,0:T(8,128)(2,1)S(1)} %constant_dynamic-update-slice_fusion.2.refs_8_), channel_id=1, source_target_pairs={{0,2},{1,3},{2,0},{3,1},{4,6},{5,7},{6,4},{7,5},{8,10},{9,11},{10,... | collective-permute-start | bytes 393224 | tf_op jit(solution)/shard_map/ppermute | solution.py:196
  19.9 6.4 %collective-permute-start.17 = (bf16[256,256]{1,0:T(8,128)(2,1)S(1)}, bf16[256,256]{1,0:T(8,128)(2,1)S(1)}, u32[]{:S(2)}, u32[]{:S(2)}) collective-permute-start(bf16[256,256]{1,0:T(8,128)(2,1)S(1)} %constant_dynamic-update-slice_fusion.4.refs_12_), channel_id=1, source_target_pairs={{0,4},{1,5},{2,6},{3,7},{4,0},{5,1},{6,2},{7,3},{8,12},{9,13},{10,... | collective-permute-start | bytes 393224 | tf_op jit(solution)/shard_map/ppermute | solution.py:196
  20.4 9.2 %collective-permute-start.16 = (bf16[256,256]{1,0:T(8,128)(2,1)S(1)}, bf16[256,256]{1,0:T(8,128)(2,1)S(1)}, u32[]{:S(2)}, u32[]{:S(2)}) collective-permute-start(bf16[256,256]{1,0:T(8,128)(2,1)S(1)} %constant_dynamic-update-slice_fusion.4.refs_12_), channel_id=1, source_target_pairs={{0,2},{1,3},{2,0},{3,1},{4,6},{5,7},{6,4},{7,5},{8,10},{9,11},{10,... | collective-permute-start | bytes 393224 | tf_op jit(solution)/shard_map/ppermute | solution.py:196
  20.7 8.1 %copy-start.29 = (s32[32]{0:T(128)S(1)}, s32[32]{0:T(128)}, u32[]{:S(2)}) copy-start(s32[32]{0:T(128)} %param.13) | copy-start | bytes 388
  21.9 7.2 %collective-permute-start.7 = (bf16[256,256]{1,0:T(8,128)(2,1)S(1)}, bf16[256,256]{1,0:T(8,128)(2,1)S(1)}, u32[]{:S(2)}, u32[]{:S(2)}) collective-permute-start(bf16[256,256]{1,0:T(8,128)(2,1)S(1)} %constant_dynamic-update-slice_fusion.refs_4_), channel_id=1, source_target_pairs={{0,4},{1,5},{2,6},{3,7},{4,0},{5,1},{6,2},{7,3},{8,12},{9,13},{10,... | collective-permute-start | bytes 393224 | tf_op jit(solution)/shard_map/ppermute | solution.py:196
  23.5 6.2 %collective-permute-start.6 = (bf16[256,256]{1,0:T(8,128)(2,1)S(1)}, bf16[256,256]{1,0:T(8,128)(2,1)S(1)}, u32[]{:S(2)}, u32[]{:S(2)}) collective-permute-start(bf16[256,256]{1,0:T(8,128)(2,1)S(1)} %constant_dynamic-update-slice_fusion.refs_4_), channel_id=1, source_target_pairs={{0,2},{1,3},{2,0},{3,1},{4,6},{5,7},{6,4},{7,5},{8,10},{9,11},{10,... | collective-permute-start | bytes 393224 | tf_op jit(solution)/shard_map/ppermute | solution.py:196
  26.3 5.4 %collective-permute-start.2 = (bf16[256,256]{1,0:T(8,128)(2,1)S(1)}, bf16[256,256]{1,0:T(8,128)(2,1)S(1)}, u32[]{:S(2)}, u32[]{:S(2)}) collective-permute-start(bf16[256,256]{1,0:T(8,128)(2,1)S(1)} %pad_maximum_fusion.refs_0_), channel_id=1, source_target_pairs={{0,4},{1,5},{2,6},{3,7},{4,0},{5,1},{6,2},{7,3},{8,12},{9,13},{10,... | collective-permute-start | bytes 393224 | tf_op jit(solution)/shard_map/ppermute | solution.py:196
  29.1 2.7 %copy-start.3 = (bf16[256,256]{1,0:T(8,128)(2,1)}, bf16[256,256]{1,0:T(8,128)(2,1)S(1)}, u32[]{:S(2)}) copy-start(bf16[256,256]{1,0:T(8,128)(2,1)S(1)} %collective-permute-done.7.refs_6_) | copy-start | bytes 393220
  29.1 9.0 %collective-permute-start.1 = (bf16[256,256]{1,0:T(8,128)(2,1)S(1)}, bf16[256,256]{1,0:T(8,128)(2,1)S(1)}, u32[]{:S(2)}, u32[]{:S(2)}) collective-permute-start(bf16[256,256]{1,0:T(8,128)(2,1)S(1)} %pad_maximum_fusion.refs_0_), channel_id=1, source_target_pairs={{0,2},{1,3},{2,0},{3,1},{4,6},{5,7},{6,4},{7,5},{8,10},{9,11},{10,... | collective-permute-start | bytes 393224 | tf_op jit(solution)/shard_map/ppermute | solution.py:196
  29.1 9.7 %collective-permute-start.13 = (bf16[256,256]{1,0:T(8,128)(2,1)S(1)}, bf16[256,256]{1,0:T(8,128)(2,1)S(1)}, u32[]{:S(2)}, u32[]{:S(2)}) collective-permute-start(bf16[256,256]{1,0:T(8,128)(2,1)S(1)} %collective-permute-done.12.refs_10_), channel_id=1, source_target_pairs={{0,2},{1,3},{2,0},{3,1},{4,6},{5,7},{6,4},{7,5},{8,10},{9,11},{10,... | collective-permute-start | bytes 393224 | tf_op jit(solution)/shard_map/ppermute | solution.py:196
  29.7 2.2 %copy-start.1 = (bf16[256,256]{1,0:T(8,128)(2,1)}, bf16[256,256]{1,0:T(8,128)(2,1)S(1)}, u32[]{:S(2)}) copy-start(bf16[256,256]{1,0:T(8,128)(2,1)S(1)} %collective-permute-done.16.refs_13_) | copy-start | bytes 393220
  29.7 9.8 %collective-permute-start.18 = (bf16[256,256]{1,0:T(8,128)(2,1)S(1)}, bf16[256,256]{1,0:T(8,128)(2,1)S(1)}, u32[]{:S(2)}, u32[]{:S(2)}) collective-permute-start(bf16[256,256]{1,0:T(8,128)(2,1)S(1)} %collective-permute-done.17.refs_14_), channel_id=1, source_target_pairs={{0,2},{1,3},{2,0},{3,1},{4,6},{5,7},{6,4},{7,5},{8,10},{9,11},{10,... | collective-permute-start | bytes 393224 | tf_op jit(solution)/shard_map/ppermute | solution.py:196
  29.7 2.1 %copy-start.5 = (bf16[256,256]{1,0:T(8,128)(2,1)}, bf16[256,256]{1,0:T(8,128)(2,1)S(1)}, u32[]{:S(2)}) copy-start(bf16[256,256]{1,0:T(8,128)(2,1)S(1)} %collective-permute-done.6.refs_5_) | copy-start | bytes 393220
  29.7 10.4 %collective-permute-start.8 = (bf16[256,256]{1,0:T(8,128)(2,1)S(1)}, bf16[256,256]{1,0:T(8,128)(2,1)S(1)}, u32[]{:S(2)}, u32[]{:S(2)}) collective-permute-start(bf16[256,256]{1,0:T(8,128)(2,1)S(1)} %collective-permute-done.7.refs_6_), channel_id=1, source_target_pairs={{0,2},{1,3},{2,0},{3,1},{4,6},{5,7},{6,4},{7,5},{8,10},{9,11},{10,... | collective-permute-start | bytes 393224 | tf_op jit(solution)/shard_map/ppermute | solution.py:196
  31.7 9.0 %collective-permute-start.3 = (bf16[256,256]{1,0:T(8,128)(2,1)S(1)}, bf16[256,256]{1,0:T(8,128)(2,1)S(1)}, u32[]{:S(2)}, u32[]{:S(2)}) collective-permute-start(bf16[256,256]{1,0:T(8,128)(2,1)S(1)} %collective-permute-done.2.refs_2_), channel_id=1, source_target_pairs={{0,2},{1,3},{2,0},{3,1},{4,6},{5,7},{6,4},{7,5},{8,10},{9,11},{10,... | collective-permute-start | bytes 393224 | tf_op jit(solution)/shard_map/ppermute | solution.py:196
  81.7 2.5 %copy-start.19 = (bf16[256,256]{1,0:T(8,128)(2,1)}, bf16[256,256]{1,0:T(8,128)(2,1)S(1)}, u32[]{:S(2)}) copy-start(bf16[256,256]{1,0:T(8,128)(2,1)S(1)} %get-tuple-element.30) | copy-start | bytes 393220
  81.7 2.5 %copy-start.21 = (bf16[256,256]{1,0:T(8,128)(2,1)}, bf16[256,256]{1,0:T(8,128)(2,1)S(1)}, u32[]{:S(2)}) copy-start(bf16[256,256]{1,0:T(8,128)(2,1)S(1)} %get-tuple-element.26) | copy-start | bytes 393220
  81.8 2.5 %copy-start.23 = (bf16[256,256]{1,0:T(8,128)(2,1)}, bf16[256,256]{1,0:T(8,128)(2,1)S(1)}, u32[]{:S(2)}) copy-start(bf16[256,256]{1,0:T(8,128)(2,1)S(1)} %get-tuple-element.32) | copy-start | bytes 393220
  81.8 5.9 %collective-permute-start.32 = (bf16[256,256]{1,0:T(8,128)(2,1)}, bf16[256,256]{1,0:T(8,128)(2,1)S(1)}, u32[]{:S(2)}, u32[]{:S(2)}) collective-permute-start(bf16[256,256]{1,0:T(8,128)(2,1)} %get-tuple-element.36), channel_id=1, source_target_pairs={{0,2},{1,3},{2,0},{3,1},{4,6},{5,7},{6,4},{7,5},{8,10},{9,11},{10,... | collective-permute-start | bytes 393224 | tf_op jit(solution)/shard_map/ppermute | solution.py:196
  81.8 42.5 %collective-permute-start.31 = (bf16[256,256]{1,0:T(8,128)(2,1)}, bf16[256,256]{1,0:T(8,128)(2,1)S(1)}, u32[]{:S(2)}, u32[]{:S(2)}) collective-permute-start(bf16[256,256]{1,0:T(8,128)(2,1)} %get-tuple-element.34), channel_id=1, source_target_pairs={{0,2},{1,3},{2,0},{3,1},{4,6},{5,7},{6,4},{7,5},{8,10},{9,11},{10,... | collective-permute-start | bytes 393224 | tf_op jit(solution)/shard_map/ppermute | solution.py:196
  82.3 7.4 %collective-permute-start.20 = (bf16[256,256]{1,0:T(8,128)(2,1)}, bf16[256,256]{1,0:T(8,128)(2,1)S(1)}, u32[]{:S(2)}, u32[]{:S(2)}) collective-permute-start(bf16[256,256]{1,0:T(8,128)(2,1)} %get-tuple-element.24), channel_id=1, source_target_pairs={{0,2},{1,3},{2,0},{3,1},{4,6},{5,7},{6,4},{7,5},{8,10},{9,11},{10,... | collective-permute-start | bytes 393224 | tf_op jit(solution)/shard_map/ppermute | solution.py:196
  82.4 18.1 %collective-permute-start.19 = (bf16[256,256]{1,0:T(8,128)(2,1)}, bf16[256,256]{1,0:T(8,128)(2,1)S(1)}, u32[]{:S(2)}, u32[]{:S(2)}) collective-permute-start(bf16[256,256]{1,0:T(8,128)(2,1)} %get-tuple-element.22), channel_id=1, source_target_pairs={{0,2},{1,3},{2,0},{3,1},{4,6},{5,7},{6,4},{7,5},{8,10},{9,11},{10,... | collective-permute-start | bytes 393224 | tf_op jit(solution)/shard_map/ppermute | solution.py:196
  82.8 7.1 %collective-permute-start.24 = (bf16[256,256]{1,0:T(8,128)(2,1)}, bf16[256,256]{1,0:T(8,128)(2,1)S(1)}, u32[]{:S(2)}, u32[]{:S(2)}) collective-permute-start(bf16[256,256]{1,0:T(8,128)(2,1)} %get-tuple-element.28), channel_id=1, source_target_pairs={{0,2},{1,3},{2,0},{3,1},{4,6},{5,7},{6,4},{7,5},{8,10},{9,11},{10,... | collective-permute-start | bytes 393224 | tf_op jit(solution)/shard_map/ppermute | solution.py:196
  85.7 2.6 %copy-start.22 = (bf16[256,256]{1,0:T(8,128)(2,1)S(1)}, bf16[256,256]{1,0:T(8,128)(2,1)}, u32[]{:S(2)}) copy-start(bf16[256,256]{1,0:T(8,128)(2,1)} %copy-done.21) | copy-start | bytes 393220
  88.3 18.6 %collective-permute-start.23 = (bf16[256,256]{1,0:T(8,128)(2,1)S(1)}, bf16[256,256]{1,0:T(8,128)(2,1)S(1)}, u32[]{:S(2)}, u32[]{:S(2)}) collective-permute-start(bf16[256,256]{1,0:T(8,128)(2,1)S(1)} %copy-done.22), channel_id=1, source_target_pairs={{0,2},{1,3},{2,0},{3,1},{4,6},{5,7},{6,4},{7,5},{8,10},{9,11},{10,... | collective-permute-start | bytes 393224 | tf_op jit(solution)/shard_map/ppermute | solution.py:196
  89.7 1.5 %collective-permute-start.28 = (bf16[256,256]{1,0:T(8,128)(2,1)S(1)}, bf16[256,256]{1,0:T(8,128)(2,1)S(1)}, u32[]{:S(2)}, u32[]{:S(2)}) collective-permute-start(bf16[256,256]{1,0:T(8,128)(2,1)S(1)} %copy-done.24), channel_id=1, source_target_pairs={{0,2},{1,3},{2,0},{3,1},{4,6},{5,7},{6,4},{7,5},{8,10},{9,11},{10,... | collective-permute-start | bytes 393224 | tf_op jit(solution)/shard_map/ppermute | solution.py:196
  90.8 32.8 %collective-permute-start.27 = (bf16[256,256]{1,0:T(8,128)(2,1)S(1)}, bf16[256,256]{1,0:T(8,128)(2,1)S(1)}, u32[]{:S(2)}, u32[]{:S(2)}) collective-permute-start(bf16[256,256]{1,0:T(8,128)(2,1)S(1)} %copy-done.20), channel_id=1, source_target_pairs={{0,2},{1,3},{2,0},{3,1},{4,6},{5,7},{6,4},{7,5},{8,10},{9,11},{10,... | collective-permute-start | bytes 393224 | tf_op jit(solution)/shard_map/ppermute | solution.py:196
  91.2 13.5 %collective-permute-start.21 = (bf16[256,256]{1,0:T(8,128)(2,1)S(1)}, bf16[256,256]{1,0:T(8,128)(2,1)S(1)}, u32[]{:S(2)}, u32[]{:S(2)}) collective-permute-start(bf16[256,256]{1,0:T(8,128)(2,1)S(1)} %add_convert_fusion.7), channel_id=1, source_target_pairs={{0,4},{1,5},{2,6},{3,7},{4,0},{5,1},{6,2},{7,3},{8,12},{9,13},{10,... | collective-permute-start | bytes 393224 | tf_op jit(solution)/shard_map/ppermute | solution.py:196
  100.5 23.8 %collective-permute-start.33 = (bf16[256,256]{1,0:T(8,128)(2,1)S(1)}, bf16[256,256]{1,0:T(8,128)(2,1)S(1)}, u32[]{:S(2)}, u32[]{:S(2)}) collective-permute-start(bf16[256,256]{1,0:T(8,128)(2,1)S(1)} %add_convert_fusion.1), channel_id=1, source_target_pairs={{0,4},{1,5},{2,6},{3,7},{4,0},{5,1},{6,2},{7,3},{8,12},{9,13},{10,... | collective-permute-start | bytes 393224 | tf_op jit(solution)/shard_map/ppermute | solution.py:196
  104.7 6.5 %collective-permute-start.25 = (bf16[256,256]{1,0:T(8,128)(2,1)S(1)}, bf16[256,256]{1,0:T(8,128)(2,1)S(1)}, u32[]{:S(2)}, u32[]{:S(2)}) collective-permute-start(bf16[256,256]{1,0:T(8,128)(2,1)S(1)} %add_convert_fusion.5), channel_id=1, source_target_pairs={{0,4},{1,5},{2,6},{3,7},{4,0},{5,1},{6,2},{7,3},{8,12},{9,13},{10,... | collective-permute-start | bytes 393224 | tf_op jit(solution)/shard_map/ppermute | solution.py:196
  106.9 16.7 %collective-permute-start.29 = (bf16[256,256]{1,0:T(8,128)(2,1)S(1)}, bf16[256,256]{1,0:T(8,128)(2,1)S(1)}, u32[]{:S(2)}, u32[]{:S(2)}) collective-permute-start(bf16[256,256]{1,0:T(8,128)(2,1)S(1)} %add_convert_fusion.3), channel_id=1, source_target_pairs={{0,4},{1,5},{2,6},{3,7},{4,0},{5,1},{6,2},{7,3},{8,12},{9,13},{10,... | collective-permute-start | bytes 393224 | tf_op jit(solution)/shard_map/ppermute | solution.py:196
  111.2 18.5 %collective-permute-start.22 = (bf16[128,256]{1,0:T(8,128)(2,1)S(1)}, bf16[128,256]{1,0:T(8,128)(2,1)S(1)}, u32[]{:S(2)}, u32[]{:S(2)}) collective-permute-start(bf16[128,256]{1,0:T(8,128)(2,1)S(1)} %get-tuple-element.40), channel_id=1, source_target_pairs={{0,24},{1,25},{2,26},{3,27},{4,28},{5,29},{6,30},{7,31},{8,16},{9,... | collective-permute-start | bytes 196616 | tf_op jit(solution)/shard_map/ppermute | solution.py:196
  123.6 6.3 %collective-permute-start.26 = (bf16[128,256]{1,0:T(8,128)(2,1)S(1)}, bf16[128,256]{1,0:T(8,128)(2,1)S(1)}, u32[]{:S(2)}, u32[]{:S(2)}) collective-permute-start(bf16[128,256]{1,0:T(8,128)(2,1)S(1)} %get-tuple-element.42), channel_id=1, source_target_pairs={{0,16},{1,17},{2,18},{3,19},{4,20},{5,21},{6,22},{7,23},{8,24},{9,... | collective-permute-start | bytes 196616 | tf_op jit(solution)/shard_map/ppermute | solution.py:196
  123.7 7.5 %collective-permute-start.30 = (bf16[128,256]{1,0:T(8,128)(2,1)S(1)}, bf16[128,256]{1,0:T(8,128)(2,1)S(1)}, u32[]{:S(2)}, u32[]{:S(2)}) collective-permute-start(bf16[128,256]{1,0:T(8,128)(2,1)S(1)} %get-tuple-element.44), channel_id=1, source_target_pairs={{0,8},{1,9},{2,10},{3,11},{4,12},{5,13},{6,14},{7,15},{8,0},{9,1},... | collective-permute-start | bytes 196616 | tf_op jit(solution)/shard_map/ppermute | solution.py:196
  124.4 6.9 %collective-permute-start.37 = (bf16[128,256]{1,0:T(8,128)(2,1)S(1)}, bf16[128,256]{1,0:T(8,128)(2,1)S(1)}, u32[]{:S(2)}, u32[]{:S(2)}) collective-permute-start(bf16[128,256]{1,0:T(8,128)(2,1)S(1)} %slice.61), channel_id=1, source_target_pairs={{0,1},{1,0},{2,3},{3,2},{4,5},{5,4},{6,7},{7,6},{8,9},{9,8},{10,11... | collective-permute-start | bytes 196616 | tf_op jit(solution)/shard_map/ppermute | solution.py:196
  126.0 7.3 %collective-permute-start.34 = (bf16[128,256]{1,0:T(8,128)(2,1)S(1)}, bf16[128,256]{1,0:T(8,128)(2,1)S(1)}, u32[]{:S(2)}, u32[]{:S(2)}) collective-permute-start(bf16[128,256]{1,0:T(8,128)(2,1)S(1)} %get-tuple-element.39), channel_id=1, source_target_pairs={{0,25},{1,24},{2,27},{3,26},{4,29},{5,28},{6,31},{7,30},{8,17},{9,... | collective-permute-start | bytes 196616 | tf_op jit(solution)/shard_map/ppermute | solution.py:196
  129.7 6.1 %collective-permute-start.35 = (bf16[128,256]{1,0:T(8,128)(2,1)S(1)}, bf16[128,256]{1,0:T(8,128)(2,1)S(1)}, u32[]{:S(2)}, u32[]{:S(2)}) collective-permute-start(bf16[128,256]{1,0:T(8,128)(2,1)S(1)} %get-tuple-element.41), channel_id=1, source_target_pairs={{0,17},{1,16},{2,19},{3,18},{4,21},{5,20},{6,23},{7,22},{8,25},{9,... | collective-permute-start | bytes 196616 | tf_op jit(solution)/shard_map/ppermute | solution.py:196
  129.8 6.0 %collective-permute-start.36 = (bf16[128,256]{1,0:T(8,128)(2,1)S(1)}, bf16[128,256]{1,0:T(8,128)(2,1)S(1)}, u32[]{:S(2)}, u32[]{:S(2)}) collective-permute-start(bf16[128,256]{1,0:T(8,128)(2,1)S(1)} %get-tuple-element.43), channel_id=1, source_target_pairs={{0,9},{1,8},{2,11},{3,10},{4,13},{5,12},{6,15},{7,14},{8,1},{9,0},... | collective-permute-start | bytes 196616 | tf_op jit(solution)/shard_map/ppermute | solution.py:196
  (20 other events, 16.6 us)

commit v3 on v1

--- a/solution.py
+++ b/solution.py
@@ -19,36 +19,27 @@
 F32 = jnp.float32
 
 
-def attend_kernel(
-    counts,
-    slots,
-    qt_ref,
-    dot_ref,
-    qs_ref,
-    dos_ref,
-    kv_ref,
-    dqt_ref,
-    dkv_ref,
-    kt_scr,
-    total_scr,
-    delta_scr,
-    w_scr,
-    ds_scr,
-    acc_scr,
-):
+def attend_kernel(counts, slots, qt_ref, dot_ref, qs_ref, dos_ref, *refs):
+    part_refs, (dqt_ref, *out_refs), scratch = refs[:4], refs[4:9], refs[9:]
+    kv_ref, total_scr, delta_scr, w_scr, ds_scr, acc_scr, sems = scratch
     local_blocks = qt_ref.shape[0]
-    n_slots = kv_ref.shape[0] // BLOCK
+    part_rows = kv_ref.shape[0] // 4
+
+    def part_of(p):
+        return slice(p * part_rows, (p + 1) * part_rows)
+
+    copies = [
+        pltpu.make_async_copy(part_refs[p], kv_ref.at[part_of(p)], sems.at[p]) for p in range(4)
+    ]
+    for copy in copies:
+        copy.start()
     acc_scr[...] = jnp.zeros_like(acc_scr)
     dqt_ref[...] = jnp.zeros_like(dqt_ref)
     total_scr[...] = jnp.zeros_like(total_scr)
     delta_scr[...] = jnp.zeros_like(delta_scr)
 
-    def turn(j, carry):
-        rows = pl.ds(pl.multiple_of(j * BLOCK, BLOCK), BLOCK)
-        kt_scr[j] = kv_ref[rows, :HEAD].T
-        return carry
-
-    lax.fori_loop(0, n_slots, turn, 0)
+    for copy in copies:
+        copy.wait()
 
     def rows_of(i, entry):
         return pl.ds(pl.multiple_of(slots[i, entry] * BLOCK, BLOCK), BLOCK)
@@ -85,7 +76,6 @@
         keys = pair(kv_ref, i, chunk, slice(0, HEAD))
         values = pair(kv_ref, i, chunk, slice(HEAD, 2 * HEAD))
         mask = allowed(i, chunk) if masked else None
-        keys_t = jnp.concatenate([kt_scr[slots[i, 2 * chunk]], kt_scr[slots[i, 2 * chunk + 1]]], 1)
         for h in range(0, WIDE, TILE):
             lanes = slice(h, h + TILE)
             scores = jnp.dot(keys, qt_ref[i, :, lanes], preferred_element_type=F32)
@@ -96,7 +86,7 @@
             dscores = (weights * (dweights - delta_scr[i, 0:1, lanes])).astype(BF16)
             w_scr[:, lanes] = weights.astype(BF16)
             ds_scr[:, lanes] = dscores
-            dqt_ref[i, :, lanes] += jnp.dot(keys_t, dscores, preferred_element_type=F32)
+        dqt_ref[i] += jnp.dot(keys.T, ds_scr[...], preferred_element_type=F32)
         dk = jnp.dot(ds_scr[...], qs_ref[i], preferred_element_type=F32)
         dv = jnp.dot(w_scr[...], dos_ref[i], preferred_element_type=F32)
         for half in range(2):
@@ -133,32 +123,33 @@
         return carry
 
     lax.fori_loop(0, local_blocks, one_block, 0)
-    dkv_ref[...] = acc_scr[...].astype(dkv_ref.dtype)
-
-
-def attend(counts, slots, qt, dot, qs, dos, kv):
+    for p in range(4):
+        out_refs[p][...] = acc_scr[part_of(p)].astype(out_refs[p].dtype)
+
+
+def attend(counts, slots, qt, dot, qs, dos, parts):
     local_blocks = qt.shape[0]
+    rows = 4 * parts[0].shape[0]
     smem = pl.BlockSpec(memory_space=pltpu.SMEM)
     vmem = pl.BlockSpec(memory_space=pltpu.VMEM)
     return pl.pallas_call(
         attend_kernel,
-        in_specs=[smem, smem] + [vmem] * 5,
-        out_specs=[vmem, vmem],
-        out_shape=[
-            jax.ShapeDtypeStruct((local_blocks, HEAD, WIDE), F32),
-            jax.ShapeDtypeStruct(kv.shape, BF16),
-        ],
+        in_specs=[smem] * 2 + [vmem] * 4 + [pl.BlockSpec(memory_space=pl.ANY)] * 4,
+        out_specs=[vmem] * 5,
+        out_shape=[jax.ShapeDtypeStruct((local_blocks, HEAD, WIDE), F32)]
+        + [jax.ShapeDtypeStruct(x.shape, BF16 if p & 1 else F32) for p, x in enumerate(parts)],
         scratch_shapes=[
-            pltpu.VMEM((kv.shape[0] // BLOCK, HEAD, BLOCK), BF16),
+            pltpu.VMEM((rows, 2 * HEAD), BF16),
             pltpu.VMEM((local_blocks, 8, WIDE), F32),
             pltpu.VMEM((local_blocks, 8, WIDE), F32),
             pltpu.VMEM((TILE, WIDE), BF16),
             pltpu.VMEM((TILE, WIDE), BF16),
-            pltpu.VMEM(kv.shape, F32),
+            pltpu.VMEM((rows, 2 * HEAD), F32),
+            pltpu.SemaphoreType.DMA((4,)),
         ],
-        compiler_params=pltpu.CompilerParams(vmem_limit_bytes=48 << 20),
+        compiler_params=pltpu.CompilerParams(vmem_limit_bytes=(16 << 20) + rows * 4096),
         name="attend",
-    )(counts, slots, qt, dot, qs, dos, kv)
+    )(counts, slots, qt, dot, qs, dos, *parts)
 
 
 def shards(
@@ -171,22 +162,54 @@
     span_table,
 ):
     local_blocks = queries.shape[0] // BLOCK
-    kv_devices = lax.axis_size("kvh")
+    seq_devices, kv_devices = lax.axis_size("seq"), lax.axis_size("kvh")
+    seq_at = lax.axis_index("seq")
     per_kvh = key_vector_rows.shape[0]
-    kv_rows = jnp.stack(
-        [key_vector_rows.reshape(per_kvh, kv_devices, HEAD), value_vector_rows.reshape(per_kvh, kv_devices, HEAD)], 2
-    )
-    kv_rows = jnp.transpose(kv_rows, (1, 0, 2, 3)).reshape(kv_devices * per_kvh, 2 * HEAD)
-    kv_head = lax.all_to_all(kv_rows, "kvh", split_axis=0, concat_axis=0, tiled=True)
-    kv_all = lax.all_gather(kv_head, "seq", axis=0, tiled=True)
-
-    first_slot = lax.axis_index("seq") * local_blocks
+    half, middles = seq_devices // 2, seq_devices // 4
+    near_devices = middles * kv_devices
+    near_groups = [
+        [
+            (top * half + middle * 2 + core) * kv_devices + head
+            for middle in range(middles)
+            for head in range(kv_devices)
+        ]
+        for top in range(2)
+        for core in range(2)
+    ]
+
+    def swap_core(x):
+        return lax.ppermute(x, "seq", [(s, s ^ 1) for s in range(seq_devices)])
+
+    def swap_far(x):
+        return lax.ppermute(x, "seq", [(s, s ^ half) for s in range(seq_devices)])
+
+    def exchange_near(x):
+        return lax.all_to_all(x, ("seq", "kvh"), 0, 0, axis_index_groups=near_groups)
+
+    def by_kv_head(x):
+        return jnp.transpose(x.reshape(per_kvh, kv_devices, HEAD), (1, 0, 2))
+
+    def to_all_near(x):
+        x = jnp.broadcast_to(x[None], (middles, *x.shape))
+        x = exchange_near(x.reshape(near_devices, per_kvh, 2 * HEAD))
+        return x.reshape(near_devices * per_kvh, 2 * HEAD)
+
+    own = jnp.concatenate([by_kv_head(key_vector_rows), by_kv_head(value_vector_rows)], 2)
+    far = swap_far(own)
+    near_part = to_all_near(own)
+    far_part = to_all_near(far)
+    parts = [near_part, swap_core(near_part), far_part, swap_core(far_part)]
+
+    first_slot = seq_at * local_blocks
     positions = lax.dynamic_slice_in_dim(span_table, first_slot, local_blocks, 0)
     counts = block_counts[positions]
     lists = key_lists[positions]
     slot_ids = jnp.arange(span_table.shape[0], dtype=jnp.int32)
+    owner = slot_ids // local_blocks
+    part = (owner // half ^ seq_at // half) * 2 + (owner % 2 ^ seq_at % 2)
+    place = (part * middles + owner % half // 2) * local_blocks + slot_ids % local_blocks
     slots = jnp.sum(
-        jnp.where(lists[:, :, None] == span_table[None, None, :], slot_ids, 0), -1, dtype=jnp.int32
+        jnp.where(lists[:, :, None] == span_table[None, None, :], place, 0), -1, dtype=jnp.int32
     )
 
     def by_head(x):
@@ -197,23 +220,22 @@
 
     qs, qt = by_head(queries)
     dos, dot = by_head(output_gradient)
-    dqt, dkv = attend(counts, slots, qt, dot, qs, dos, kv_all)
+    dqt, *partials = attend(counts, slots, qt, dot, qs, dos, parts)
     dq = jnp.transpose(dqt.reshape(local_blocks, HEAD, GROUP, BLOCK), (0, 3, 2, 1)) * SCALE
     grad_queries = dq.reshape(queries.shape).astype(BF16)
 
-    seq_devices = lax.axis_size("seq")
-    parts = lax.all_to_all(
-        dkv.reshape(seq_devices, local_blocks * BLOCK, 2 * HEAD), "seq", split_axis=0, concat_axis=0
-    )
-    sums = jnp.sum(parts.astype(F32), 0)
-    sums = jnp.concatenate([sums[:, :HEAD] * SCALE, sums[:, HEAD:]], 1).astype(BF16)
-    mine = lax.all_to_all(
-        sums.reshape(kv_devices, per_kvh, 2 * HEAD), "kvh", split_axis=0, concat_axis=0
-    )
-    mine = jnp.transpose(mine, (1, 0, 2)).reshape(per_kvh, kv_devices, 2, HEAD)
-    key_gradient = mine[:, :, 0].reshape(per_kvh, kv_devices * HEAD)
-    value_gradient = mine[:, :, 1].reshape(per_kvh, kv_devices * HEAD)
-    return grad_queries, key_gradient, value_gradient
+    def near_sums(kept, sent):
+        chip = (kept + swap_core(sent).astype(F32)).astype(BF16)
+        got = exchange_near(chip.reshape(near_devices, per_kvh, 2 * HEAD))
+        return jnp.sum(got.reshape(middles, kv_devices, per_kvh, 2 * HEAD).astype(F32), 0)
+
+    far_sums = swap_far(near_sums(partials[2], partials[3]).astype(BF16))
+    sums = near_sums(partials[0], partials[1]) + far_sums.astype(F32)
+
+    def by_token(x):
+        return jnp.transpose(x, (1, 0, 2)).reshape(per_kvh, kv_devices * HEAD).astype(BF16)
+
+    return grad_queries, by_token(sums[:, :, :HEAD] * SCALE), by_token(sums[:, :, HEAD:])
 
 
 def solution(mesh):

time: 170 us -> 107 us (0.63)
  the two profiles are of different devices: /device:TPU:16 before, /device:TPU:0 now
where the time goes in v3:
time: 107 us
  starting transfers between devices  39.7 us (37%)
  waiting for transfers between devices  33.3 us (31%)
  Pallas kernels  17.1 us (16%)
  local copies, waits for them, and re-layouts  13.9 us (13%)
  other arithmetic  2.61 us (2%)
    all_to_all x4, waiting for transfers between devices, exchange_near(): lax.all_to_all(x, ('seq', 'kvh'), 0, 0, axis_index_groups=near_groups)  24.2 us
    all_to_all x4, starting transfers between devices, exchange_near(): lax.all_to_all(x, ('seq', 'kvh'), 0, 0, axis_index_groups=near_groups)  18.1 us
    pallas_call x1, Pallas kernels, attend(): pl.pallas_call(attend_kernel, in_specs=[smem] * 2 + [vmem] * 4 + [pl.Bloc...  17.1 us
    ppermute x4, starting transfers between devices, swap_core(): return lax.ppermute(x, 'seq', [(s, s ^ 1) for s in range(seq_devices)])  15.8 us
    ppermute x2, waiting for transfers between devices, swap_far(): return lax.ppermute(x, 'seq', [(s, s ^ half) for s in range(seq_devices)])  5.99 us
    unnamed x29, local copies, waits for them, and re-layouts  5.97 us
    ppermute x2, starting transfers between devices, swap_far(): return lax.ppermute(x, 'seq', [(s, s ^ half) for s in range(seq_devices)])  5.78 us
    ppermute x4, waiting for transfers between devices, swap_core(): return lax.ppermute(x, 'seq', [(s, s ^ 1) for s in range(seq_devices)])  3.08 us
  transfers between devices with their start and end apart: 10, of which 7 were waited for; matrix products, arithmetic and copies ran while one was open for 8% of the time, Pallas kernels for 0%

profile of v3, /device:TPU:0, one launch (start us, length us, event | category | flops | bytes accessed | tf_op | source)
XLA Modules:
  0.0 107.5 jit_solution(9208623335214342163)
XLA Ops:
  0.7 0.9 reshape.74
  1.6 0.1 pad_maximum_fusion
  1.8 0.8 broadcast_in_dim.29
  2.6 6.2 %all-to-all-start = ((bf16[8,128,256]{2,1,0:T(8,128)(2,1)}), bf16[8,128,256]{2,1,0:T(8,128)(2,1)S(1)}, u32[]{:S(2)}, u32[]{:S(2)}) async-start(bf16[8,128,256]{2,1,0:T(8,128)(2,1)} %bitcast.8), calls=%async_computation | async-start | bytes 1048576 | tf_op jit(solution)/shard_map/all_to_all | solution.py:187
  8.8 2.6 %collective-permute-start.1 = (bf16[2,128,256]{2,0,1:T(2,128)(2,1)S(1)}, bf16[2,128,256]{2,0,1:T(2,128)(2,1)S(1)}, u32[]{:S(2)}, u32[]{:S(2)}) collective-permute-start(bf16[2,128,256]{2,0,1:T(2,128)(2,1)S(1)} %pad_maximum_fusion), channel_id=1, source_target_pairs={{0,16},{2,18},{4,20},{6,22},{8,24},{10,26},{12,28},{14,30},{16,0},... | collective-permute-start | bytes 393224 | tf_op jit(solution)/shard_map/ppermute | solution.py:184
  11.4 6.0 %collective-permute-done.1 = bf16[2,128,256]{2,0,1:T(2,128)(2,1)S(1)} collective-permute-done((bf16[2,128,256]{2,0,1:T(2,128)(2,1)S(1)}, bf16[2,128,256]{2,0,1:T(2,128)(2,1)S(1)}, u32[]{:S(2)}, u32[]{:S(2)}) %collective-permute-start.1) | collective-permute-done | bytes 131104 | tf_op jit(solution)/shard_map/ppermute | solution.py:184
  17.4 3.3 %all-to-all-done = bf16[8,128,256]{2,1,0:T(8,128)(2,1)S(1)} async-done(((bf16[8,128,256]{2,1,0:T(8,128)(2,1)}), bf16[8,128,256]{2,1,0:T(8,128)(2,1)S(1)}, u32[]{:S(2)}, u32[]{:S(2)}) %all-to-all-start) | async-done | bytes 524320 | tf_op jit(solution)/shard_map/all_to_all | solution.py:187
  20.6 0.8 broadcast_in_dim.30
  21.5 4.8 %all-to-all-start.1 = ((bf16[8,128,256]{2,1,0:T(8,128)(2,1)}), bf16[8,128,256]{2,1,0:T(8,128)(2,1)S(1)}, u32[]{:S(2)}, u32[]{:S(2)}) async-start(bf16[8,128,256]{2,1,0:T(8,128)(2,1)} %bitcast.10), calls=%async_computation.1 | async-start | bytes 1048576 | tf_op jit(solution)/shard_map/all_to_all | solution.py:187
  26.3 7.7 %all-to-all-done.1 = bf16[8,128,256]{2,1,0:T(8,128)(2,1)S(1)} async-done(((bf16[8,128,256]{2,1,0:T(8,128)(2,1)}), bf16[8,128,256]{2,1,0:T(8,128)(2,1)S(1)}, u32[]{:S(2)}, u32[]{:S(2)}) %all-to-all-start.1) | async-done | bytes 524320 | tf_op jit(solution)/shard_map/all_to_all | solution.py:187
  33.9 0.1 copy.58
  34.0 0.1 copy.49
  34.1 0.5 copy.47
  34.6 1.1 %copy.59 = bf16[32,8,8,128]{3,2,1,0:T(8,128)(2,1)S(1)} copy(bf16[32,8,8,128]{3,1,2,0:T(8,128)(2,1)} %bitcast.66) | data formatting | bytes 1048576
  35.7 0.1 copy.50
  35.8 1.2 %copy.48 = bf16[2,128,8,128]{1,2,3,0:T(8,128)(2,1)} copy(bf16[2,128,8,128]{3,2,1,0:T(8,128)(2,1)S(1)} %bitcast.57) | data formatting | bytes 1048576 | tf_op jit(solution)/shard_map/reshape | solution.py:216
  37.1 0.7 copy-done.9
  37.8 0.1 copy.46
  37.9 0.7 copy-done.10
  38.5 0.1 compare_select_fusion
  38.6 0.6 gather_fusion
  39.2 0.6 gather_fusion.1
  39.8 0.2 reshape.69.qt_ref
  40.0 1.3 %reshape.71.dot_ref = bf16[2,128,1024]{2,1,0:T(8,128)(2,1)S(1)} reshape(bf16[2,128,8,128]{3,2,1,0:T(8,128)(2,1)} %bitcast.60) | data formatting | bytes 1048576 | tf_op jit(solution)/shard_map/reshape | solution.py:218
  41.3 0.2 select_reduce_fusion.slots
  41.5 17.1 %attend.1 = (f32[2,128,1024]{2,1,0:T(8,128)S(1)}, f32[1024,256]{1,0:T(8,128)S(1)}, bf16[1024,256]{1,0:T(8,128)(2,1)S(1)}, f32[1024,256]{1,0:T(8,128)S(1)}, bf16[1024,256]{1,0:T(8,128)(2,1)S(1)}) custom-call(s32[2]{0:T(128)S(1)} %gather_fusion, s32[2,24]{1,0:T(2,128)S(1)} %select_reduce_fusion.slots, bf16[2,128,1024]{2,1,0:T(8,128)(2,1)S(1)} %reshape.69.qt_ref, ...), custom_call_target="tpu_custom_call" | custom-call | tf_op jit(solution)/shard_map/attend/pallas_call | solution.py:135
  58.6 0.8 copy-done.5
  59.4 15.4 %collective-permute-start.4 = (bf16[1024,256]{1,0:T(8,128)(2,1)S(1)}, bf16[1024,256]{1,0:T(8,128)(2,1)S(1)}, u32[]{:S(2)}, u32[]{:S(2)}) collective-permute-start(bf16[1024,256]{1,0:T(8,128)(2,1)S(1)} %get-tuple-element.12), channel_id=1, source_target_pairs={{0,2},{2,0},{4,6},{6,4},{8,10},{10,8},{12,14},{14,12},{16,18},{18,... | collective-permute-start | bytes 1572872 | tf_op jit(solution)/shard_map/ppermute | solution.py:181
  74.8 1.5 %collective-permute-done.4 = bf16[1024,256]{1,0:T(8,128)(2,1)S(1)} collective-permute-done((bf16[1024,256]{1,0:T(8,128)(2,1)S(1)}, bf16[1024,256]{1,0:T(8,128)(2,1)S(1)}, u32[]{:S(2)}, u32[]{:S(2)}) %collective-permute-start.4) | collective-permute-done | bytes 524320 | tf_op jit(solution)/shard_map/ppermute | solution.py:181
  76.3 1.0 add_convert_fusion
  77.3 3.6 %all-to-all-start.3 = ((bf16[8,128,256]{2,1,0:T(8,128)(2,1)}), bf16[8,128,256]{2,1,0:T(8,128)(2,1)S(1)}, u32[]{:S(2)}, u32[]{:S(2)}) async-start(bf16[8,128,256]{2,1,0:T(8,128)(2,1)} %bitcast.15), calls=%async_computation.3 | async-start | bytes 1048576 | tf_op jit(solution)/shard_map/all_to_all | solution.py:187
  80.9 0.4 collective-permute-start.3
  81.4 1.5 %collective-permute-done.3 = bf16[1024,256]{1,0:T(8,128)(2,1)S(1)} collective-permute-done((bf16[1024,256]{1,0:T(8,128)(2,1)S(1)}, bf16[1024,256]{1,0:T(8,128)(2,1)S(1)}, u32[]{:S(2)}, u32[]{:S(2)}) %collective-permute-start.3) | collective-permute-done | bytes 524320 | tf_op jit(solution)/shard_map/ppermute | solution.py:181
  82.9 1.0 add_convert_fusion.1
  83.9 6.7 %all-to-all-done.3 = bf16[8,128,256]{2,1,0:T(8,128)(2,1)S(1)} async-done(((bf16[8,128,256]{2,1,0:T(8,128)(2,1)}), bf16[8,128,256]{2,1,0:T(8,128)(2,1)S(1)}, u32[]{:S(2)}, u32[]{:S(2)}) %all-to-all-start.3) | async-done | bytes 524320 | tf_op jit(solution)/shard_map/all_to_all | solution.py:187
  90.6 3.5 %all-to-all-start.2 = ((bf16[8,128,256]{2,1,0:T(8,128)(2,1)}), bf16[8,128,256]{2,1,0:T(8,128)(2,1)S(1)}, u32[]{:S(2)}, u32[]{:S(2)}) async-start(bf16[8,128,256]{2,1,0:T(8,128)(2,1)} %bitcast.13), calls=%async_computation.2 | async-start | bytes 1048576 | tf_op jit(solution)/shard_map/all_to_all | solution.py:187
  94.1 0.1 multiply_convert_fusion
  94.2 0.1 copy.60
  94.3 0.5 copy.53
  94.8 0.9 copy.63
  95.7 0.1 reduce_sum.32
  95.8 3.2 %collective-permute-start.5 = (bf16[2,128,256]{2,1,0:T(8,128)(2,1)S(1)}, bf16[2,128,256]{2,1,0:T(8,128)(2,1)S(1)}, u32[]{:S(2)}, u32[]{:S(2)}) collective-permute-start(bf16[2,128,256]{2,1,0:T(8,128)(2,1)S(1)} %reduce_sum.32), channel_id=1, source_target_pairs={{0,16},{2,18},{4,20},{6,22},{8,24},{10,26},{12,28},{14,30},{16,0},... | collective-permute-start | bytes 393224 | tf_op jit(solution)/shard_map/ppermute | solution.py:184
  99.0 6.6 %all-to-all-done.2 = bf16[8,128,256]{2,1,0:T(8,128)(2,1)S(1)} async-done(((bf16[8,128,256]{2,1,0:T(8,128)(2,1)}), bf16[8,128,256]{2,1,0:T(8,128)(2,1)S(1)}, u32[]{:S(2)}, u32[]{:S(2)}) %all-to-all-start.2) | async-done | bytes 524320 | tf_op jit(solution)/shard_map/all_to_all | solution.py:187
  105.5 0.1 convert_reduce_fusion
  105.7 0.1 copy.54
  105.8 0.7 copy.56
  106.6 0.1 copy.55
  106.7 0.7 copy.57
  (33 shorter events, 0.2 us)
Async XLA Ops:
  0.6 38.0 %copy-start = (s32[32]{0:T(128)S(1)}, s32[32]{0:T(128)}, u32[]{:S(2)}) copy-start(s32[32]{0:T(128)} %param.12) | copy-start | bytes 388
  0.6 0.9 copy-start.8
  2.6 18.1 %all-to-all-start = ((bf16[8,128,256]{2,1,0:T(8,128)(2,1)}), bf16[8,128,256]{2,1,0:T(8,128)(2,1)S(1)}, u32[]{:S(2)}, u32[]{:S(2)}) async-start(bf16[8,128,256]{2,1,0:T(8,128)(2,1)} %bitcast.8), calls=%async_computation | async-start | bytes 1048576 | tf_op jit(solution)/shard_map/all_to_all | solution.py:187
  8.8 8.6 %collective-permute-start.1 = (bf16[2,128,256]{2,0,1:T(2,128)(2,1)S(1)}, bf16[2,128,256]{2,0,1:T(2,128)(2,1)S(1)}, u32[]{:S(2)}, u32[]{:S(2)}) collective-permute-start(bf16[2,128,256]{2,0,1:T(2,128)(2,1)S(1)} %pad_maximum_fusion), channel_id=1, source_target_pairs={{0,16},{2,18},{4,20},{6,22},{8,24},{10,26},{12,28},{14,30},{16,0},... | collective-permute-start | bytes 393224 | tf_op jit(solution)/shard_map/ppermute | solution.py:184
  21.5 12.5 %copy-start.7 = (bf16[256,1024]{1,0:T(8,128)(2,1)S(1)}, bf16[256,1024]{1,0:T(8,128)(2,1)}, u32[]{:S(2)}) copy-start(bf16[256,1024]{1,0:T(8,128)(2,1)} %param.7) | copy-start | bytes 1572868
  21.5 12.5 %all-to-all-start.1 = ((bf16[8,128,256]{2,1,0:T(8,128)(2,1)}), bf16[8,128,256]{2,1,0:T(8,128)(2,1)S(1)}, u32[]{:S(2)}, u32[]{:S(2)}) async-start(bf16[8,128,256]{2,1,0:T(8,128)(2,1)} %bitcast.10), calls=%async_computation.1 | async-start | bytes 1048576 | tf_op jit(solution)/shard_map/all_to_all | solution.py:187
  26.2 15.3 %collective-permute-start = (bf16[1024,256]{1,0:T(8,128)(2,1)S(1)}, bf16[1024,256]{1,0:T(8,128)(2,1)}, u32[]{:S(2)}, u32[]{:S(2)}) collective-permute-start(bf16[1024,256]{1,0:T(8,128)(2,1)S(1)} %bitcast.48), channel_id=1, source_target_pairs={{0,2},{2,0},{4,6},{6,4},{8,10},{10,8},{12,14},{14,12},{16,18},{18,... | collective-permute-start | bytes 1572872 | tf_op jit(solution)/shard_map/ppermute | solution.py:181
  33.9 7.6 %collective-permute-start.2 = (bf16[1024,256]{1,0:T(8,128)(2,1)S(1)}, bf16[1024,256]{1,0:T(8,128)(2,1)}, u32[]{:S(2)}, u32[]{:S(2)}) collective-permute-start(bf16[1024,256]{1,0:T(8,128)(2,1)S(1)} %bitcast.50), channel_id=1, source_target_pairs={{0,2},{2,0},{4,6},{6,4},{8,10},{10,8},{12,14},{14,12},{16,18},{18,... | collective-permute-start | bytes 1572872 | tf_op jit(solution)/shard_map/ppermute | solution.py:181
  37.1 0.7 copy-start.9
  37.9 0.7 copy-start.10
  58.6 0.8 copy-start.5
  59.4 17.9 %copy-start.1 = (f32[2,128,1024]{2,1,0:T(8,128)}, f32[2,128,1024]{2,1,0:T(8,128)S(1)}, u32[]{:S(2)}) copy-start(f32[2,128,1024]{2,1,0:T(8,128)S(1)} %get-tuple-element.8) | copy-start | bytes 3145732
  59.4 17.9 %copy-start.3 = (f32[1024,256]{1,0:T(8,128)}, f32[1024,256]{1,0:T(8,128)S(1)}, u32[]{:S(2)}) copy-start(f32[1024,256]{1,0:T(8,128)S(1)} %get-tuple-element.9) | copy-start | bytes 3145732
  59.4 16.9 %collective-permute-start.4 = (bf16[1024,256]{1,0:T(8,128)(2,1)S(1)}, bf16[1024,256]{1,0:T(8,128)(2,1)S(1)}, u32[]{:S(2)}, u32[]{:S(2)}) collective-permute-start(bf16[1024,256]{1,0:T(8,128)(2,1)S(1)} %get-tuple-element.12), channel_id=1, source_target_pairs={{0,2},{2,0},{4,6},{6,4},{8,10},{10,8},{12,14},{14,12},{16,18},{18,... | collective-permute-start | bytes 1572872 | tf_op jit(solution)/shard_map/ppermute | solution.py:181
  76.3 4.6 %copy-start.6 = (bf16[1024,256]{1,0:T(8,128)(2,1)S(1)}, bf16[1024,256]{1,0:T(8,128)(2,1)}, u32[]{:S(2)}) copy-start(bf16[1024,256]{1,0:T(8,128)(2,1)} %copy-done.5) | copy-start | bytes 1572868
  77.3 5.6 %copy-start.4 = (f32[1024,256]{1,0:T(8,128)S(1)}, f32[1024,256]{1,0:T(8,128)}, u32[]{:S(2)}) copy-start(f32[1024,256]{1,0:T(8,128)} %copy-done.3) | copy-start | bytes 3145732
  77.3 13.3 %all-to-all-start.3 = ((bf16[8,128,256]{2,1,0:T(8,128)(2,1)}), bf16[8,128,256]{2,1,0:T(8,128)(2,1)S(1)}, u32[]{:S(2)}, u32[]{:S(2)}) async-start(bf16[8,128,256]{2,1,0:T(8,128)(2,1)} %bitcast.15), calls=%async_computation.3 | async-start | bytes 1048576 | tf_op jit(solution)/shard_map/all_to_all | solution.py:187
  80.9 2.0 %collective-permute-start.3 = (bf16[1024,256]{1,0:T(8,128)(2,1)S(1)}, bf16[1024,256]{1,0:T(8,128)(2,1)S(1)}, u32[]{:S(2)}, u32[]{:S(2)}) collective-permute-start(bf16[1024,256]{1,0:T(8,128)(2,1)S(1)} %copy-done.6), channel_id=1, source_target_pairs={{0,2},{2,0},{4,6},{6,4},{8,10},{10,8},{12,14},{14,12},{16,18},{18,... | collective-permute-start | bytes 1572872 | tf_op jit(solution)/shard_map/ppermute | solution.py:181
  83.9 10.2 %copy-start.2 = (f32[2,128,1024]{2,1,0:T(8,128)S(1)}, f32[2,128,1024]{2,1,0:T(8,128)}, u32[]{:S(2)}) copy-start(f32[2,128,1024]{2,1,0:T(8,128)} %copy-done.1) | copy-start | bytes 3145732
  90.6 14.9 %all-to-all-start.2 = ((bf16[8,128,256]{2,1,0:T(8,128)(2,1)}), bf16[8,128,256]{2,1,0:T(8,128)(2,1)S(1)}, u32[]{:S(2)}, u32[]{:S(2)}) async-start(bf16[8,128,256]{2,1,0:T(8,128)(2,1)} %bitcast.13), calls=%async_computation.2 | async-start | bytes 1048576 | tf_op jit(solution)/shard_map/all_to_all | solution.py:187
  95.8 9.8 %collective-permute-start.5 = (bf16[2,128,256]{2,1,0:T(8,128)(2,1)S(1)}, bf16[2,128,256]{2,1,0:T(8,128)(2,1)S(1)}, u32[]{:S(2)}, u32[]{:S(2)}) collective-permute-start(bf16[2,128,256]{2,1,0:T(8,128)(2,1)S(1)} %reduce_sum.32), channel_id=1, source_target_pairs={{0,16},{2,18},{4,20},{6,22},{8,24},{10,26},{12,28},{14,30},{16,0},... | collective-permute-start | bytes 393224 | tf_op jit(solution)/shard_map/ppermute | solution.py:184

commit v4 on v3

v4 whole, which is shorter than its diff:
```python
import functools

import jax
import jax.numpy as jnp
from jax import lax
from jax.experimental import pallas as pl
from jax.experimental.pallas import tpu as pltpu
from jax.sharding import PartitionSpec as P

HEAD = 128
GROUP = 8
BLOCK = 128
SCALE = HEAD ** (-0.5)
LOG2E = 1.4426950408889634
SCORE_SCALE = SCALE * LOG2E
TILE = 2 * BLOCK
WIDE = GROUP * BLOCK
BF16 = jnp.bfloat16
F32 = jnp.float32
BY_ROWS = (((1,), (1,)), ((), ()))


def by_rows(a, b):
    return lax.dot_general(a, b, BY_ROWS, preferred_element_type=F32)


def plain(a, b):
    return jnp.dot(a, b, preferred_element_type=F32)


def start_copies(sources, targets, sems):
    copies = [pltpu.make_async_copy(a, b, sems.at[n]) for n, (a, b) in enumerate(zip(sources, targets))]
    for copy in copies:
        copy.start()
    return copies


def find_places(me, spans, place, local_blocks):
    n_slots = spans.shape[0]
    half, middles = n_slots // local_blocks // 2, n_slots // local_blocks // 4
    seq_at, turn = me[0], me[1]

    def find(slot, carry):
        owner, block = slot // local_blocks, slot % local_blocks
        apart = owner ^ seq_at
        is_far = apart // half
        near_at = apart % half // 2 * local_blocks + (block ^ turn // BLOCK)
        far_at = owner % half // 2 * local_blocks + block
        part = is_far * 2 + apart % 2
        place[spans[slot]] = part * (middles * local_blocks) + jnp.where(is_far == 1, far_at, near_at)
        return carry

    lax.fori_loop(0, n_slots, find, 0)


def choose(me, lists, counts, spans, place, work, sizes, local_blocks, want_far):
    n_slots = spans.shape[0]
    for i in range(local_blocks):
        at = spans[me[0] * local_blocks + i]

        def clear(e, carry):
            work[i, e] = 0
            return carry

        def keep(e, size):
            here = place[lists[at, e]]
            work[i, size] = here
            return size + (here // (n_slots // 2) == want_far).astype(jnp.int32)

        lax.fori_loop(0, work.shape[1], clear, 0)
        size = lax.fori_loop(0, counts[at], keep, 0)
        work[i, size] = 0
        sizes[i] = size


def heads(ref, i, first, many):
    rows = pl.ds(pl.multiple_of(i * BLOCK, BLOCK), BLOCK)
    return jnp.concatenate([ref[rows, h * HEAD : (h + 1) * HEAD] for h in range(first, first + many)], 0)


def rows_at(place):
    return pl.ds(pl.multiple_of(place * BLOCK, BLOCK), BLOCK)


def gathered(kv_ref, places, lanes):
    return jnp.concatenate([kv_ref[rows_at(p), lanes] for p in places], 0)


def allowed(many, start, count, turn, diagonal):
    key_at = lax.broadcasted_iota(jnp.int32, (many * BLOCK, TILE), 0)
    entry = start + key_at // BLOCK
    mask = entry < count
    if diagonal:
        query_at = lax.broadcasted_iota(jnp.int32, (many * BLOCK, TILE), 1) & (BLOCK - 1)
        here = (key_at & (BLOCK - 1)) ^ (turn & (BLOCK - 1))
        mask = jnp.logical_and(mask, jnp.logical_or(entry > 0, here <= query_at))
    return mask


def sweep(count, step):
    rest = count % 4
    quads = count // 4 + (rest == 3).astype(jnp.int32)

    def body(quad, carry):
        special = jnp.logical_or(quad == 0, 4 * quad + 4 > count)

        @pl.when(special)
        def _():
            step(4 * quad, 4, True)

        @pl.when(jnp.logical_not(special))
        def _():
            step(4 * quad, 4, False)

        return carry

    lax.fori_loop(0, quads, body, 0)

    @pl.when(jnp.logical_or(rest == 1, rest == 2))
    def _():
        step(4 * quads, 2, True)


def first_pass(i, places, mask, q_ref, do_ref, kv_ref, total, delta):
    keys = gathered(kv_ref, places, slice(0, HEAD))
    values = gathered(kv_ref, places, slice(HEAD, 2 * HEAD))
    for h in range(0, GROUP, 2):
        lanes = slice(h * BLOCK, h * BLOCK + TILE)
        expd = jnp.exp2(by_rows(keys, heads(q_ref, i, h, 2)) * SCORE_SCALE)
        if mask is not None:
            expd = jnp.where(mask, expd, 0.0)
        total[i, :, lanes] += jnp.sum(expd.reshape(-1, 8, TILE), 0)
        dweights = by_rows(values, heads(do_ref, i, h, 2))
        delta[i, :, lanes] += jnp.sum((expd * dweights).reshape(-1, 8, TILE), 0)


def near_kernel(me, lists, counts, spans, q_any, do_any, near_any, pair_any, total, delta, *scratch):
    q_ref, do_ref, kv_ref, place, work, sizes, sems = scratch
    local_blocks, part = q_ref.shape[0] // BLOCK, near_any.shape[0]
    copies = start_copies(
        [near_any, pair_any, q_any, do_any],
        [kv_ref.at[:part], kv_ref.at[part:], q_ref, do_ref],
        sems,
    )
    total[...] = jnp.zeros_like(total)
    delta[...] = jnp.zeros_like(delta)
    find_places(me, spans, place, local_blocks)
    choose(me, lists, counts, spans, place, work, sizes, local_blocks, 0)
    for copy in copies:
        copy.wait()

    def one_block(i, carry):
        def step(start, many, masked):
            mask = allowed(many, start, sizes[i], me[1], True) if masked else None
            places = [work[i, start + e] for e in range(many)]
            first_pass(i, places, mask, q_ref, do_ref, kv_ref, total, delta)

        sweep(sizes[i], step)
        return carry

    lax.fori_loop(0, local_blocks, one_block, 0)


def main_kernel(me, lists, counts, spans, q_any, do_any, total_in, delta_in, *refs):
    part_refs, (dqt_ref, *out_refs), scratch = refs[:4], refs[4:9], refs[9:]
    q_ref, do_ref, kv_ref, total, delta, w_scr, ds_scr, acc, place, work, sizes, sems = scratch
    local_blocks, part = q_ref.shape[0] // BLOCK, part_refs[0].shape[0]

    def part_of(p):
        return slice(p * part, (p + 1) * part)

    copies = start_copies(
        [*part_refs, q_any, do_any], [*(kv_ref.at[part_of(p)] for p in range(4)), q_ref, do_ref], sems
    )
    acc[...] = jnp.zeros_like(acc)
    dqt_ref[...] = jnp.zeros_like(dqt_ref)
    total[...] = total_in[...]
    delta[...] = delta_in[...]
    find_places(me, spans, place, local_blocks)
    choose(me, lists, counts, spans, place, work, sizes, local_blocks, 1)
    for copy in copies:
        copy.wait()

    def second_pass(i, places, mask):
        keys = gathered(kv_ref, places, slice(0, HEAD))
        values = gathered(kv_ref, places, slice(HEAD, 2 * HEAD))
        rows = slice(0, len(places) * BLOCK)
        for h in range(0, GROUP, 2):
            lanes = slice(h * BLOCK, h * BLOCK + TILE)
            scores = by_rows(keys, heads(q_ref, i, h, 2))
            weights = jnp.exp2(scores * SCORE_SCALE - total[i, 0:1, lanes])
            if mask is not None:
                weights = jnp.where(mask, weights, 0.0)
            dweights = by_rows(values, heads(do_ref, i, h, 2))
            w_scr[rows, lanes] = weights.astype(BF16)
            ds_scr[rows, lanes] = (weights * (dweights - delta[i, 0:1, lanes])).astype(BF16)
        dqt_ref[i] += plain(keys.T, ds_scr[rows])
        dk = plain(ds_scr[rows], heads(q_ref, i, 0, GROUP))
        dv = plain(w_scr[rows], heads(do_ref, i, 0, GROUP))
        for n, p in enumerate(places):
            acc[rows_at(p), :HEAD] += dk[n * BLOCK : (n + 1) * BLOCK]
            acc[rows_at(p), HEAD:] += dv[n * BLOCK : (n + 1) * BLOCK]

    def one_block(i, carry):
        at = spans[me[0] * local_blocks + i]
        count = counts[at]

        def far_step(start, many, masked):
            mask = allowed(many, start, sizes[i], me[1], False) if masked else None
            places = [work[i, start + e] for e in range(many)]
            first_pass(i, places, mask, q_ref, do_ref, kv_ref, total, delta)

        def step(start, many, masked):
            mask = allowed(many, start, count, me[1], True) if masked else None
            second_pass(i, [place[lists[at, start + e]] for e in range(many)], mask)

        sweep(sizes[i], far_step)
        row_total = jnp.sum(total[i], 0, keepdims=True)
        row_delta = jnp.sum(delta[i], 0, keepdims=True) / row_total
        total[i] = jnp.broadcast_to(jnp.log2(row_total), (8, WIDE))
        delta[i] = jnp.broadcast_to(row_delta, (8, WIDE))
        sweep(count, step)
        return carry

    lax.fori_loop(0, local_blocks, one_block, 0)
    for p in range(4):
        out_refs[p][...] = acc[part_of(p)].astype(out_refs[p].dtype)


LIMIT = 32 << 20
SMEM = pl.BlockSpec(memory_space=pltpu.SMEM)
VMEM = pl.BlockSpec(memory_space=pltpu.VMEM)
ANY = pl.BlockSpec(memory_space=pl.ANY)


def lists_scratch(lists, spans, local_blocks):
    return [
        pltpu.SMEM(spans.shape, jnp.int32),
        pltpu.SMEM((local_blocks, lists.shape[1] + 8), jnp.int32),
        pltpu.SMEM((local_blocks,), jnp.int32),
    ]


def near_sums(me, lists, counts, spans, q, do, near, pair):
    local_blocks, rows = q.shape[0] // BLOCK, 2 * near.shape[0]
    return pl.pallas_call(
        near_kernel,
        in_specs=[SMEM] * 4 + [ANY] * 4,
        out_specs=[VMEM] * 2,
        out_shape=[jax.ShapeDtypeStruct((local_blocks, 8, WIDE), F32)] * 2,
        scratch_shapes=[
            pltpu.VMEM(q.shape, BF16),
            pltpu.VMEM(do.shape, BF16),
            pltpu.VMEM((rows, 2 * HEAD), BF16),
            *lists_scratch(lists, spans, local_blocks),
            pltpu.SemaphoreType.DMA((4,)),
        ],
        compiler_params=pltpu.CompilerParams(vmem_limit_bytes=LIMIT),
        cost_estimate=pl.CostEstimate(flops=1 << 20, bytes_accessed=1 << 10, transcendentals=0),
        name="near",
    )(me, lists, counts, spans, q, do, near, pair)


def attend(me, lists, counts, spans, q, do, total, delta, parts):
    local_blocks, rows = q.shape[0] // BLOCK, 4 * parts[0].shape[0]
    return pl.pallas_call(
        main_kernel,
        in_specs=[SMEM] * 4 + [ANY] * 2 + [VMEM] * 2 + [ANY] * 4,
        out_specs=[VMEM] * 5,
        out_shape=[jax.ShapeDtypeStruct((local_blocks, HEAD, WIDE), F32)]
        + [jax.ShapeDtypeStruct(x.shape, BF16 if p & 1 else F32) for p, x in enumerate(parts)],
        scratch_shapes=[
            pltpu.VMEM(q.shape, BF16),
            pltpu.VMEM(do.shape, BF16),
            pltpu.VMEM((rows, 2 * HEAD), BF16),
            pltpu.VMEM((local_blocks, 8, WIDE), F32),
            pltpu.VMEM((local_blocks, 8, WIDE), F32),
            pltpu.VMEM((4 * BLOCK, WIDE), BF16),
            pltpu.VMEM((4 * BLOCK, WIDE), BF16),
            pltpu.VMEM((rows, 2 * HEAD), F32),
            *lists_scratch(lists, spans, local_blocks),
            pltpu.SemaphoreType.DMA((6,)),
        ],
        compiler_params=pltpu.CompilerParams(vmem_limit_bytes=LIMIT),
        name="attend",
    )(me, lists, counts, spans, q, do, total, delta, *parts)


def shards(
    queries,
    key_vector_rows,
    value_vector_rows,
    output_gradient,
    key_lists,
    block_counts,
    span_table,
):
    seq_devices, kv_devices = lax.axis_size("seq"), lax.axis_size("kvh")
    seq_at, kv_at = lax.axis_index("seq"), lax.axis_index("kvh")
    per_kvh = key_vector_rows.shape[0]
    half, middles = seq_devices // 2, seq_devices // 4
    near_devices = middles * kv_devices
    near_groups = [
        [
            (top * half + middle * 2 + core) * kv_devices + head
            for middle in range(middles)
            for head in range(kv_devices)
        ]
        for top in range(2)
        for core in range(2)
    ]

    def swap_seq(x, step):
        return lax.ppermute(x, "seq", [(s, s ^ step) for s in range(seq_devices)])

    def swap_kv(x, step):
        return lax.ppermute(x, "kvh", [(h, h ^ step) for h in range(kv_devices)])

    def exchange_near(x):
        x = x.reshape(near_devices, per_kvh, 2 * HEAD)
        return lax.all_to_all(x, ("seq", "kvh"), 0, 0, axis_index_groups=near_groups)

    own = jnp.stack(
        [
            jnp.concatenate([x[:, h * HEAD : (h + 1) * HEAD] for x in (key_vector_rows, value_vector_rows)], 1)
            for h in range(kv_devices)
        ]
    )
    far = swap_seq(own, half)
    mine = [lax.dynamic_index_in_dim(own, kv_at ^ j, 0, False) for j in range(kv_devices)]
    span = jnp.concatenate([mine[0]] + [swap_kv(mine[j], j) for j in range(1, kv_devices)], 0)
    near_part = jnp.concatenate([span] + [swap_seq(span, 2 * m) for m in range(1, middles)], 0)
    near_pair = swap_seq(near_part, 1)
    far_part = exchange_near(jnp.broadcast_to(far[None], (middles, *far.shape)))
    far_part = far_part.reshape(near_part.shape)

    me = jnp.stack([seq_at, kv_at * per_kvh]).astype(jnp.int32)
    common = (me, key_lists, block_counts, span_table, queries, output_gradient)
    total, delta = near_sums(*common, near_part, near_pair)
    total, far_part = lax.optimization_barrier((total, far_part))
    far_pair = swap_seq(far_part, 1)
    dqt, *partials = attend(*common, total, delta, [near_part, near_pair, far_part, far_pair])
    dq = jnp.transpose(dqt.reshape(-1, HEAD, GROUP, BLOCK), (0, 3, 2, 1)) * SCALE
    grad_queries = dq.reshape(queries.shape).astype(BF16)

    far_chip = (partials[2] + swap_seq(partials[3], 1).astype(F32)).astype(BF16)
    far_sums = exchange_near(far_chip).reshape(middles, kv_devices, per_kvh, 2 * HEAD)
    far_sums = jnp.sum(far_sums.astype(F32), 0).astype(BF16)

    near_recv = swap_seq(partials[1], 1)
    span_rows = kv_devices * per_kvh

    def near_chip(m):
        rows = slice(m * span_rows, (m + 1) * span_rows)
        return partials[0][rows] + near_recv[rows].astype(F32)

    others = [swap_seq(near_chip(m).astype(BF16), 2 * m) for m in range(1, middles)]
    *others, _ = lax.optimization_barrier((*others, far_sums))
    far_sums = swap_seq(far_sums, half).astype(F32)
    span_sums = near_chip(0)
    for other in others:
        span_sums = span_sums + other.astype(F32)
    pieces = [span_sums[j * per_kvh : (j + 1) * per_kvh] for j in range(kv_devices)]
    pieces = pieces[:1] + [swap_kv(pieces[j].astype(BF16), j).astype(F32) for j in range(1, kv_devices)]
    pieces = jnp.stack(pieces)
    sums = [
        lax.dynamic_index_in_dim(pieces, kv_at ^ h, 0, False) + far_sums[h] for h in range(kv_devices)
    ]
    key_gradient = jnp.concatenate([x[:, :HEAD] * SCALE for x in sums], 1).astype(BF16)
    value_gradient = jnp.concatenate([x[:, HEAD:] for x in sums], 1).astype(BF16)
    return grad_queries, key_gradient, value_gradient


def solution(mesh):
    placed = (
        P("seq", "kvh"),
        P(("seq", "kvh"), None),
        P(("seq", "kvh"), None),
        P("seq", "kvh"),
        P(),
        P(),
        P(),
    )
    return jax.shard_map(
        shards,
        mesh=mesh,
        in_specs=placed,
        out_specs=(P("seq", "kvh"), P(("seq", "kvh"), None), P(("seq", "kvh"), None)),
        check_vma=False,
    )
```

time: 107 us -> 88.7 us (0.83); the launches traced: 107 us -> 87.4 us
  local copies, waits for them, and re-layouts: 13.9 us -> 4.98 us
  waiting for transfers between devices: 33.3 us -> 24.7 us
  starting transfers between devices: 39.7 us -> 35.9 us
  other arithmetic: 2.61 us -> 5.83 us
  Pallas kernels: 17.1 us -> 15.1 us
    all_to_all x4 -> x2, waiting for transfers between devices: 24.2 us -> 5.6 us  [exchange_near(): lax.all_to_all(x, ('seq', 'kvh'), 0, 0, axis_index_groups=near_groups)]
    ppermute x6 -> x14, waiting for transfers between devices: 9.07 us -> 19.1 us  [the longest x12 15.5 us: swap_seq(): return lax.ppermute(x, 'seq', [(s, s ^ step) for s in range(seq_devices)])]
    all_to_all x4 -> x2, starting transfers between devices: 18.1 us -> 10.4 us  [exchange_near(): lax.all_to_all(x, ('seq', 'kvh'), 0, 0, axis_index_groups=near_groups)]
    reshape x8 -> x0, local copies, waits for them, and re-layouts: 4.29 us -> none  [the longest x4 1.88 us: by_head(): x = x.reshape(local_blocks, BLOCK, GROUP, HEAD)]
    ppermute x6 -> x14, starting transfers between devices: 21.6 us -> 25.5 us  [the longest x12 21.9 us: swap_seq(): return lax.ppermute(x, 'seq', [(s, s ^ step) for s in range(seq_devices)])]
    unnamed x29 -> x26, local copies, waits for them, and re-layouts: 5.97 us -> 2.8 us
    pallas_call x1 -> x2, Pallas kernels: 17.1 us -> 15.1 us  [the longest x1 11 us: attend(): pl.pallas_call(main_kernel, in_specs=[SMEM] * 4 + [ANY] * 2 + [VMEM] * 2...]
    gather x2 -> x0, local copies, waits for them, and re-layouts: 1.2 us -> none  [the longest x1 0.64 us: shards(): counts = block_counts[positions]]
  transfers between devices with their start and end apart: 10 -> 16, of which waited for: 7 -> 11; matrix products, arithmetic and copies ran while one was open for 8% -> 7% of each run, Pallas kernels for 0% -> 5%
where the time goes in v4:
time: 88.7 us; the launch traced here: 87.4 us
  starting transfers between devices  35.9 us (40%)
  waiting for transfers between devices  24.7 us (28%)
  Pallas kernels  15.1 us (17%)
  other arithmetic  5.83 us (7%)
  local copies, waits for them, and re-layouts  4.98 us (6%)
  between operations  0.95 us (1%)
    ppermute x12, starting transfers between devices, swap_seq(): return lax.ppermute(x, 'seq', [(s, s ^ step) for s in range(seq_devices)])  21.9 us
    ppermute x12, waiting for transfers between devices, swap_seq(): return lax.ppermute(x, 'seq', [(s, s ^ step) for s in range(seq_devices)])  15.5 us
    pallas_call x1, Pallas kernels, attend(): pl.pallas_call(main_kernel, in_specs=[SMEM] * 4 + [ANY] * 2 + [VMEM] * 2...  11 us
    all_to_all x2, starting transfers between devices, exchange_near(): lax.all_to_all(x, ('seq', 'kvh'), 0, 0, axis_index_groups=near_groups)  10.4 us
    all_to_all x2, waiting for transfers between devices, exchange_near(): lax.all_to_all(x, ('seq', 'kvh'), 0, 0, axis_index_groups=near_groups)  5.6 us
    pallas_call x1, Pallas kernels, near_sums(): pl.pallas_call(near_kernel, in_specs=[SMEM] * 4 + [ANY] * 4, out_specs=[V...  4.08 us
    ppermute x2, waiting for transfers between devices, swap_kv(): return lax.ppermute(x, 'kvh', [(h, h ^ step) for h in range(kv_devices)])  3.63 us
    ppermute x2, starting transfers between devices, swap_kv(): return lax.ppermute(x, 'kvh', [(h, h ^ step) for h in range(kv_devices)])  3.62 us
  transfers between devices with their start and end apart: 16, of which 11 were waited for; matrix products, arithmetic and copies ran while one was open for 7% of the time, Pallas kernels for 5%

profile of v4, /device:TPU:0, one launch (start us, length us, event | category | flops | bytes accessed | tf_op | source)
XLA Modules:
  0.0 87.4 jit_solution(15699189491192926290)
XLA Ops:
  0.6 0.8 fusion.13
  1.5 0.0 copy-done.8
  1.6 3.0 %collective-permute-start = (bf16[128,256]{1,0:T(8,128)(2,1)S(1)}, bf16[128,256]{1,0:T(8,128)(2,1)S(1)}, u32[]{:S(2)}, u32[]{:S(2)}) collective-permute-start(bf16[128,256]{1,0:T(8,128)(2,1)S(1)} %fusion.9), channel_id=1, source_target_pairs={{0,1},{1,0},{2,3},{3,2},{4,5},{5,4},{6,7},{7,6},{8,9},{9,8},{10,11... | collective-permute-start | bytes 196616 | tf_op jit(solution)/shard_map/ppermute | solution.py:317
  4.6 2.7 %collective-permute-start.5 = (bf16[2,128,256]{2,1,0:T(8,128)(2,1)S(1)}, bf16[2,128,256]{2,1,0:T(8,128)(2,1)S(1)}, u32[]{:S(2)}, u32[]{:S(2)}) collective-permute-start(bf16[2,128,256]{2,1,0:T(8,128)(2,1)S(1)} %pad_maximum_fusion), channel_id=1, source_target_pairs={{0,16},{2,18},{4,20},{6,22},{8,24},{10,26},{12,28},{14,30},{16,0},... | collective-permute-start | bytes 393224 | tf_op jit(solution)/shard_map/ppermute | solution.py:314
  7.3 1.6 %collective-permute-start.1 = (bf16[256,256]{1,0:T(8,128)(2,1)S(1)}, bf16[256,256]{1,0:T(8,128)(2,1)S(1)}, u32[]{:S(2)}, u32[]{:S(2)}) collective-permute-start(bf16[256,256]{1,0:T(8,128)(2,1)S(1)} %pad_maximum_fusion.1), channel_id=1, source_target_pairs={{0,4},{2,6},{4,0},{6,2},{8,12},{10,14},{12,8},{14,10},{16,20},{18,... | collective-permute-start | bytes 393224 | tf_op jit(solution)/shard_map/ppermute | solution.py:314
  8.9 1.5 %collective-permute-start.3 = (bf16[256,256]{1,0:T(8,128)(2,1)S(1)}, bf16[256,256]{1,0:T(8,128)(2,1)S(1)}, u32[]{:S(2)}, u32[]{:S(2)}) collective-permute-start(bf16[256,256]{1,0:T(8,128)(2,1)S(1)} %pad_maximum_fusion.1), channel_id=1, source_target_pairs={{0,12},{2,14},{4,8},{6,10},{8,4},{10,6},{12,0},{14,2},{16,28},{18,... | collective-permute-start | bytes 393224 | tf_op jit(solution)/shard_map/ppermute | solution.py:314
  10.5 0.4 collective-permute-start.2
  10.8 2.6 %collective-permute-done.5 = bf16[2,128,256]{2,1,0:T(8,128)(2,1)S(1)} collective-permute-done((bf16[2,128,256]{2,1,0:T(8,128)(2,1)S(1)}, bf16[2,128,256]{2,1,0:T(8,128)(2,1)S(1)}, u32[]{:S(2)}, u32[]{:S(2)}) %collective-permute-start.5) | collective-permute-done | bytes 131104 | tf_op jit(solution)/shard_map/ppermute | solution.py:314
  13.4 0.8 broadcast_in_dim.2
  14.2 3.6 %all-to-all-start = ((bf16[8,128,256]{2,1,0:T(8,128)(2,1)}), bf16[8,128,256]{2,1,0:T(8,128)(2,1)S(1)}, u32[]{:S(2)}, u32[]{:S(2)}) async-start(bf16[8,128,256]{2,1,0:T(8,128)(2,1)} %bitcast.6), calls=%async_computation | async-start | bytes 1048576 | tf_op jit(solution)/shard_map/all_to_all | solution.py:321
  17.9 0.0 copy-start
  18.0 0.1 collective-permute-start.4
  18.1 0.7 copy-done.9
  18.7 0.1 copy.11.lists
  18.8 0.1 pad_add_fusion.me
  18.9 1.1 %collective-permute-done.4.pair_any.refs_1_ = bf16[1024,256]{1,0:T(8,128)(2,1)S(1)} collective-permute-done((bf16[1024,256]{1,0:T(8,128)(2,1)S(1)}, bf16[1024,256]{1,0:T(8,128)(2,1)S(1)}, u32[]{:S(2)}, u32[]{:S(2)}) %collective-permute-start.4) | collective-permute-done | bytes 524320 | tf_op jit(solution)/shard_map/ppermute | solution.py:314
  20.0 4.1 %near.1 = (f32[2,8,1024]{2,1,0:T(8,128)S(1)}, f32[2,8,1024]{2,1,0:T(8,128)S(1)}) custom-call(s32[2]{0:T(128)S(1)} %pad_add_fusion.me, s32[32,24]{1,0:T(8,128)S(1)} %copy.11.lists, s32[32]{0:T(128)S(1)} %copy-done.6, s32[32]{0:T(128)S(1)} %copy-done.7, bf16[256,1024]{1,0:T(8,128)(2,1)S(1)} %copy-done, bf16[256,1024]{1,0:T(8,128)(2,1)S(1)} %copy-done.1, ...), custom_call_target="tpu_custom_call" | custom-call | flops 1048576 | bytes 1024 | tf_op jit(solution)/shard_map/near/pallas_call | solution.py:246
  24.1 2.4 %all-to-all-done = bf16[8,128,256]{2,1,0:T(8,128)(2,1)S(1)} async-done(((bf16[8,128,256]{2,1,0:T(8,128)(2,1)}), bf16[8,128,256]{2,1,0:T(8,128)(2,1)S(1)}, u32[]{:S(2)}, u32[]{:S(2)}) %all-to-all-start) | async-done | bytes 524320 | tf_op jit(solution)/shard_map/all_to_all | solution.py:321
  26.5 0.2 collective-permute-start.6
  26.7 1.7 %collective-permute-done.6.refs_3_ = bf16[1024,256]{1,0:T(8,128)(2,1)S(1)} collective-permute-done((bf16[1024,256]{1,0:T(8,128)(2,1)S(1)}, bf16[1024,256]{1,0:T(8,128)(2,1)S(1)}, u32[]{:S(2)}, u32[]{:S(2)}) %collective-permute-start.6) | collective-permute-done | bytes 524320 | tf_op jit(solution)/shard_map/ppermute | solution.py:314
  28.4 11.0 %attend.1 = (f32[2,128,1024]{2,1,0:T(8,128)S(1)}, f32[1024,256]{1,0:T(8,128)S(1)}, bf16[1024,256]{1,0:T(8,128)(2,1)S(1)}, f32[1024,256]{1,0:T(8,128)S(1)}, bf16[1024,256]{1,0:T(8,128)(2,1)S(1)}) custom-call(s32[2]{0:T(128)S(1)} %pad_add_fusion.me, s32[32,24]{1,0:T(8,128)S(1)} %copy.11.lists, s32[32]{0:T(128)S(1)} %copy-done.6, s32[32]{0:T(128)S(1)} %copy-done.7, ...), custom_call_target="tpu_custom_call" | custom-call | tf_op jit(solution)/shard_map/attend/pallas_call | solution.py:266
  39.4 11.6 %collective-permute-start.11 = (bf16[1024,256]{1,0:T(8,128)(2,1)S(1)}, bf16[1024,256]{1,0:T(8,128)(2,1)S(1)}, u32[]{:S(2)}, u32[]{:S(2)}) collective-permute-start(bf16[1024,256]{1,0:T(8,128)(2,1)S(1)} %get-tuple-element.23), channel_id=1, source_target_pairs={{0,2},{2,0},{4,6},{6,4},{8,10},{10,8},{12,14},{14,12},{16,18},{18,... | collective-permute-start | bytes 1572872 | tf_op jit(solution)/shard_map/ppermute | solution.py:314
  51.0 0.1 collective-permute-start.7
  51.1 1.5 %collective-permute-done.11 = bf16[1024,256]{1,0:T(8,128)(2,1)S(1)} collective-permute-done((bf16[1024,256]{1,0:T(8,128)(2,1)S(1)}, bf16[1024,256]{1,0:T(8,128)(2,1)S(1)}, u32[]{:S(2)}, u32[]{:S(2)}) %collective-permute-start.11) | collective-permute-done | bytes 524320 | tf_op jit(solution)/shard_map/ppermute | solution.py:314
  52.6 0.9 %add_convert_fusion = bf16[1024,256]{1,0:T(8,128)(2,1)} fusion(f32[1024,256]{1,0:T(8,128)S(1)} %get-tuple-element.22, bf16[1024,256]{1,0:T(8,128)(2,1)S(1)} %collective-permute-done.11), kind=kLoop, calls=%fused_computation | loop fusion | flops 786432 | bytes 2097152 | tf_op jit(solution)/shard_map/convert_element_type | solution.py:346
  53.5 6.7 %all-to-all-start.1 = ((bf16[8,128,256]{2,1,0:T(8,128)(2,1)}), bf16[8,128,256]{2,1,0:T(8,128)(2,1)}, u32[]{:S(2)}, u32[]{:S(2)}) async-start(bf16[8,128,256]{2,1,0:T(8,128)(2,1)} %bitcast.9), calls=%async_computation.1 | async-start | bytes 1048576 | tf_op jit(solution)/shard_map/all_to_all | solution.py:321
  60.3 0.1 multiply_convert_fusion
  60.4 0.1 copy.13
  60.5 1.0 %copy-done.5 = f32[1024,256]{1,0:T(8,128)S(1)} copy-done((f32[1024,256]{1,0:T(8,128)S(1)}, f32[1024,256]{1,0:T(8,128)}, u32[]{:S(2)}) %copy-start.5) | copy-done | bytes 1048600
  61.5 1.1 %add_convert_fusion.1 = (bf16[256,256]{1,0:T(8,128)(2,1)S(1)}, bf16[256,256]{1,0:T(8,128)(2,1)S(1)}, bf16[256,256]{1,0:T(8,128)(2,1)S(1)}) fusion(f32[1024,256]{1,0:T(8,128)S(1)} %copy-done.5, bf16[1024,256]{1,0:T(8,128)(2,1)} %collective-permute-done.7), kind=kLoop, calls=%fused_computation.9 | loop fusion | flops 589824 | bytes 1572864 | tf_op jit(solution)/shard_map/convert_element_type | solution.py:357
  62.6 3.0 %collective-permute-start.10 = (bf16[256,256]{1,0:T(8,128)(2,1)S(1)}, bf16[256,256]{1,0:T(8,128)(2,1)S(1)}, u32[]{:S(2)}, u32[]{:S(2)}) collective-permute-start(bf16[256,256]{1,0:T(8,128)(2,1)S(1)} %get-tuple-element.29), channel_id=1, source_target_pairs={{0,12},{2,14},{4,8},{6,10},{8,4},{10,6},{12,0},{14,2},{16,28},{18,... | collective-permute-start | bytes 393224 | tf_op jit(solution)/shard_map/ppermute | solution.py:314
  65.6 0.6 collective-permute-start.9
  66.1 0.1 collective-permute-start.8
  66.3 0.5 copy.12
  66.7 0.9 %copy.16 = bf16[32,8,8,128]{3,1,2,0:T(8,128)(2,1)} copy(bf16[32,8,8,128]{3,2,1,0:T(8,128)(2,1)S(1)} %bitcast.41) | data formatting | bytes 1048576
  67.6 3.2 %all-to-all-done.1 = bf16[8,128,256]{2,1,0:T(8,128)(2,1)} async-done(((bf16[8,128,256]{2,1,0:T(8,128)(2,1)}), bf16[8,128,256]{2,1,0:T(8,128)(2,1)}, u32[]{:S(2)}, u32[]{:S(2)}) %all-to-all-start.1) | async-done | bytes 524320 | tf_op jit(solution)/shard_map/all_to_all | solution.py:321
  70.8 1.1 %reduce_sum.12 = bf16[2,128,256]{2,1,0:T(8,128)(2,1)S(1)} reduce(bf16[4,2,128,256]{3,2,1,0:T(8,128)(2,1)} %bitcast.10, bf16[]{:T(256)} %constant.31.clone.1), dimensions={0}, to_apply=%region_0.1 | reduce | flops 196608 | bytes 655362 | tf_op jit(solution)/shard_map/reduce_sum | solution.py:348
  72.0 1.7 %collective-permute-done.10 = bf16[256,256]{1,0:T(8,128)(2,1)S(1)} collective-permute-done((bf16[256,256]{1,0:T(8,128)(2,1)S(1)}, bf16[256,256]{1,0:T(8,128)(2,1)S(1)}, u32[]{:S(2)}, u32[]{:S(2)}) %collective-permute-start.10) | collective-permute-done | bytes 131104 | tf_op jit(solution)/shard_map/ppermute | solution.py:314
  73.7 0.6 collective-permute-done.9
  74.3 1.2 %collective-permute-done.8 = bf16[256,256]{1,0:T(8,128)(2,1)S(1)} collective-permute-done((bf16[256,256]{1,0:T(8,128)(2,1)S(1)}, bf16[256,256]{1,0:T(8,128)(2,1)S(1)}, u32[]{:S(2)}, u32[]{:S(2)}) %collective-permute-start.8) | collective-permute-done | bytes 131104 | tf_op jit(solution)/shard_map/ppermute | solution.py:314
  75.6 1.0 %convert_add_fusion = f32[256,256]{1,0:T(8,128)S(1)} fusion(bf16[256,256]{1,0:T(8,128)(2,1)S(1)} %collective-permute-done.10, bf16[256,256]{1,0:T(8,128)(2,1)S(1)} %collective-permute-done.9, bf16[256,256]{1,0:T(8,128)(2,1)S(1)} %collective-permute-done.8, f32[1024,256]{1,0:T(8,128)S(1)} %copy-done.5, bf16[1024,256]{1,0:T(8,128)(2,1)} %collective-permute-done.7), kind=kLoop, calls=%fused_computation.8 | loop fusion | flops 524288 | bytes 1048576 | tf_op jit(solution)/shard_map/add | solution.py:362
  76.6 0.6 collective-permute-start.12
  77.2 0.1 collective-permute-start.13
  77.3 3.6 %collective-permute-done.12 = bf16[128,256]{1,0:T(8,128)(2,1)S(1)} collective-permute-done((bf16[128,256]{1,0:T(8,128)(2,1)S(1)}, bf16[128,256]{1,0:T(8,128)(2,1)S(1)}, u32[]{:S(2)}, u32[]{:S(2)}) %collective-permute-start.12) | collective-permute-done | bytes 65568 | tf_op jit(solution)/shard_map/ppermute | solution.py:317
  80.9 5.1 %collective-permute-done.13 = bf16[2,128,256]{2,1,0:T(8,128)(2,1)S(1)} collective-permute-done((bf16[2,128,256]{2,1,0:T(8,128)(2,1)S(1)}, bf16[2,128,256]{2,1,0:T(8,128)(2,1)S(1)}, u32[]{:S(2)}, u32[]{:S(2)}) %collective-permute-start.13) | collective-permute-done | bytes 131104 | tf_op jit(solution)/shard_map/ppermute | solution.py:314
  86.0 0.1 fusion.5
  86.2 0.6 pad_maximum_fusion.2
  86.8 0.6 pad_maximum_fusion.3
  (40 shorter events, 0.3 us)
Async XLA Ops:
  0.6 0.8 copy-start.8
  1.6 5.7 %collective-permute-start = (bf16[128,256]{1,0:T(8,128)(2,1)S(1)}, bf16[128,256]{1,0:T(8,128)(2,1)S(1)}, u32[]{:S(2)}, u32[]{:S(2)}) collective-permute-start(bf16[128,256]{1,0:T(8,128)(2,1)S(1)} %fusion.9), channel_id=1, source_target_pairs={{0,1},{1,0},{2,3},{3,2},{4,5},{5,4},{6,7},{7,6},{8,9},{9,8},{10,11... | collective-permute-start | bytes 196616 | tf_op jit(solution)/shard_map/ppermute | solution.py:317
  4.6 8.8 %collective-permute-start.5 = (bf16[2,128,256]{2,1,0:T(8,128)(2,1)S(1)}, bf16[2,128,256]{2,1,0:T(8,128)(2,1)S(1)}, u32[]{:S(2)}, u32[]{:S(2)}) collective-permute-start(bf16[2,128,256]{2,1,0:T(8,128)(2,1)S(1)} %pad_maximum_fusion), channel_id=1, source_target_pairs={{0,16},{2,18},{4,20},{6,22},{8,24},{10,26},{12,28},{14,30},{16,0},... | collective-permute-start | bytes 393224 | tf_op jit(solution)/shard_map/ppermute | solution.py:314
  7.3 10.6 %collective-permute-start.1 = (bf16[256,256]{1,0:T(8,128)(2,1)S(1)}, bf16[256,256]{1,0:T(8,128)(2,1)S(1)}, u32[]{:S(2)}, u32[]{:S(2)}) collective-permute-start(bf16[256,256]{1,0:T(8,128)(2,1)S(1)} %pad_maximum_fusion.1), channel_id=1, source_target_pairs={{0,4},{2,6},{4,0},{6,2},{8,12},{10,14},{12,8},{14,10},{16,20},{18,... | collective-permute-start | bytes 393224 | tf_op jit(solution)/shard_map/ppermute | solution.py:314
  8.9 9.0 %collective-permute-start.3 = (bf16[256,256]{1,0:T(8,128)(2,1)S(1)}, bf16[256,256]{1,0:T(8,128)(2,1)S(1)}, u32[]{:S(2)}, u32[]{:S(2)}) collective-permute-start(bf16[256,256]{1,0:T(8,128)(2,1)S(1)} %pad_maximum_fusion.1), channel_id=1, source_target_pairs={{0,12},{2,14},{4,8},{6,10},{8,4},{10,6},{12,0},{14,2},{16,28},{18,... | collective-permute-start | bytes 393224 | tf_op jit(solution)/shard_map/ppermute | solution.py:314
  10.5 7.5 %collective-permute-start.2 = (bf16[256,256]{1,0:T(8,128)(2,1)S(1)}, bf16[256,256]{1,0:T(8,128)(2,1)S(1)}, u32[]{:S(2)}, u32[]{:S(2)}) collective-permute-start(bf16[256,256]{1,0:T(8,128)(2,1)S(1)} %pad_maximum_fusion.1), channel_id=1, source_target_pairs={{0,8},{2,10},{4,12},{6,14},{8,0},{10,2},{12,4},{14,6},{16,24},{18,... | collective-permute-start | bytes 393224 | tf_op jit(solution)/shard_map/ppermute | solution.py:314
  14.2 5.7 %copy-start.1 = (bf16[256,1024]{1,0:T(8,128)(2,1)S(1)}, bf16[256,1024]{1,0:T(8,128)(2,1)}, u32[]{:S(2)}) copy-start(bf16[256,1024]{1,0:T(8,128)(2,1)} %do_any.3) | copy-start | bytes 1572868
  14.2 12.2 %all-to-all-start = ((bf16[8,128,256]{2,1,0:T(8,128)(2,1)}), bf16[8,128,256]{2,1,0:T(8,128)(2,1)S(1)}, u32[]{:S(2)}, u32[]{:S(2)}) async-start(bf16[8,128,256]{2,1,0:T(8,128)(2,1)} %bitcast.6), calls=%async_computation | async-start | bytes 1048576 | tf_op jit(solution)/shard_map/all_to_all | solution.py:321
  17.9 2.1 %copy-start = (bf16[256,1024]{1,0:T(8,128)(2,1)S(1)}, bf16[256,1024]{1,0:T(8,128)(2,1)}, u32[]{:S(2)}) copy-start(bf16[256,1024]{1,0:T(8,128)(2,1)} %q_any.3) | copy-start | bytes 1572868
  18.0 0.8 copy-start.9
  18.0 2.0 %collective-permute-start.4 = (bf16[1024,256]{1,0:T(8,128)(2,1)S(1)}, bf16[1024,256]{1,0:T(8,128)(2,1)S(1)}, u32[]{:S(2)}, u32[]{:S(2)}) collective-permute-start(bf16[1024,256]{1,0:T(8,128)(2,1)S(1)} %constant_dynamic-update-slice_fusion.near_any.refs_0_), channel_id=1, source_target_pairs={{0,2},{2,0},{4,6},{6,4},{8,10},{10,8},{12,14},{14,12},{16,18},{18,... | collective-permute-start | bytes 1572872 | tf_op jit(solution)/shard_map/ppermute | solution.py:314
  18.8 1.2 %copy-start.6 = (s32[32]{0:T(128)S(1)}, s32[32]{0:T(128)}, u32[]{:S(2)}) copy-start(s32[32]{0:T(128)} %counts.3) | copy-start | bytes 388
  18.8 1.2 %copy-start.7 = (s32[32]{0:T(128)S(1)}, s32[32]{0:T(128)}, u32[]{:S(2)}) copy-start(s32[32]{0:T(128)} %spans.3) | copy-start | bytes 388
  26.5 1.9 %collective-permute-start.6 = (bf16[1024,256]{1,0:T(8,128)(2,1)S(1)}, bf16[1024,256]{1,0:T(8,128)(2,1)S(1)}, u32[]{:S(2)}, u32[]{:S(2)}) collective-permute-start(bf16[1024,256]{1,0:T(8,128)(2,1)S(1)} %bitcast.37), channel_id=1, source_target_pairs={{0,2},{2,0},{4,6},{6,4},{8,10},{10,8},{12,14},{14,12},{16,18},{18,... | collective-permute-start | bytes 1572872 | tf_op jit(solution)/shard_map/ppermute | solution.py:314
  39.4 14.1 %copy-start.2 = (f32[2,128,1024]{2,1,0:T(8,128)}, f32[2,128,1024]{2,1,0:T(8,128)S(1)}, u32[]{:S(2)}) copy-start(f32[2,128,1024]{2,1,0:T(8,128)S(1)} %get-tuple-element.19) | copy-start | bytes 3145732
  39.4 14.1 %copy-start.4 = (f32[1024,256]{1,0:T(8,128)}, f32[1024,256]{1,0:T(8,128)S(1)}, u32[]{:S(2)}) copy-start(f32[1024,256]{1,0:T(8,128)S(1)} %get-tuple-element.20) | copy-start | bytes 3145732
  39.4 13.2 %collective-permute-start.11 = (bf16[1024,256]{1,0:T(8,128)(2,1)S(1)}, bf16[1024,256]{1,0:T(8,128)(2,1)S(1)}, u32[]{:S(2)}, u32[]{:S(2)}) collective-permute-start(bf16[1024,256]{1,0:T(8,128)(2,1)S(1)} %get-tuple-element.23), channel_id=1, source_target_pairs={{0,2},{2,0},{4,6},{6,4},{8,10},{10,8},{12,14},{14,12},{16,18},{18,... | collective-permute-start | bytes 1572872 | tf_op jit(solution)/shard_map/ppermute | solution.py:314
  51.0 9.4 %collective-permute-start.7 = (bf16[1024,256]{1,0:T(8,128)(2,1)S(1)}, bf16[1024,256]{1,0:T(8,128)(2,1)}, u32[]{:S(2)}, u32[]{:S(2)}) collective-permute-start(bf16[1024,256]{1,0:T(8,128)(2,1)S(1)} %get-tuple-element.21), channel_id=1, source_target_pairs={{0,2},{2,0},{4,6},{6,4},{8,10},{10,8},{12,14},{14,12},{16,18},{18,... | collective-permute-start | bytes 1572872 | tf_op jit(solution)/shard_map/ppermute | solution.py:314
  53.5 6.7 %copy-start.3 = (f32[2,128,1024]{2,1,0:T(8,128)S(1)}, f32[2,128,1024]{2,1,0:T(8,128)}, u32[]{:S(2)}) copy-start(f32[2,128,1024]{2,1,0:T(8,128)} %copy-done.2) | copy-start | bytes 3145732
  53.5 17.3 %all-to-all-start.1 = ((bf16[8,128,256]{2,1,0:T(8,128)(2,1)}), bf16[8,128,256]{2,1,0:T(8,128)(2,1)}, u32[]{:S(2)}, u32[]{:S(2)}) async-start(bf16[8,128,256]{2,1,0:T(8,128)(2,1)} %bitcast.9), calls=%async_computation.1 | async-start | bytes 1048576 | tf_op jit(solution)/shard_map/all_to_all | solution.py:321
  60.3 1.2 %copy-start.5 = (f32[1024,256]{1,0:T(8,128)S(1)}, f32[1024,256]{1,0:T(8,128)}, u32[]{:S(2)}) copy-start(f32[1024,256]{1,0:T(8,128)} %copy-done.4) | copy-start | bytes 3145732
  62.6 11.1 %collective-permute-start.10 = (bf16[256,256]{1,0:T(8,128)(2,1)S(1)}, bf16[256,256]{1,0:T(8,128)(2,1)S(1)}, u32[]{:S(2)}, u32[]{:S(2)}) collective-permute-start(bf16[256,256]{1,0:T(8,128)(2,1)S(1)} %get-tuple-element.29), channel_id=1, source_target_pairs={{0,12},{2,14},{4,8},{6,10},{8,4},{10,6},{12,0},{14,2},{16,28},{18,... | collective-permute-start | bytes 393224 | tf_op jit(solution)/shard_map/ppermute | solution.py:314
  65.6 8.7 %collective-permute-start.9 = (bf16[256,256]{1,0:T(8,128)(2,1)S(1)}, bf16[256,256]{1,0:T(8,128)(2,1)S(1)}, u32[]{:S(2)}, u32[]{:S(2)}) collective-permute-start(bf16[256,256]{1,0:T(8,128)(2,1)S(1)} %get-tuple-element.30), channel_id=1, source_target_pairs={{0,8},{2,10},{4,12},{6,14},{8,0},{10,2},{12,4},{14,6},{16,24},{18,... | collective-permute-start | bytes 393224 | tf_op jit(solution)/shard_map/ppermute | solution.py:314
  66.1 9.4 %collective-permute-start.8 = (bf16[256,256]{1,0:T(8,128)(2,1)S(1)}, bf16[256,256]{1,0:T(8,128)(2,1)S(1)}, u32[]{:S(2)}, u32[]{:S(2)}) collective-permute-start(bf16[256,256]{1,0:T(8,128)(2,1)S(1)} %get-tuple-element.31), channel_id=1, source_target_pairs={{0,4},{2,6},{4,0},{6,2},{8,12},{10,14},{12,8},{14,10},{16,20},{18,... | collective-permute-start | bytes 393224 | tf_op jit(solution)/shard_map/ppermute | solution.py:314
  76.6 4.3 %collective-permute-start.12 = (bf16[128,256]{1,0:T(8,128)(2,1)S(1)}, bf16[128,256]{1,0:T(8,128)(2,1)S(1)}, u32[]{:S(2)}, u32[]{:S(2)}) collective-permute-start(bf16[128,256]{1,0:T(8,128)(2,1)S(1)} %slice.115), channel_id=1, source_target_pairs={{0,1},{1,0},{2,3},{3,2},{4,5},{5,4},{6,7},{7,6},{8,9},{9,8},{10,11... | collective-permute-start | bytes 196616 | tf_op jit(solution)/shard_map/ppermute | solution.py:317
  77.2 8.8 %collective-permute-start.13 = (bf16[2,128,256]{2,1,0:T(8,128)(2,1)S(1)}, bf16[2,128,256]{2,1,0:T(8,128)(2,1)S(1)}, u32[]{:S(2)}, u32[]{:S(2)}) collective-permute-start(bf16[2,128,256]{2,1,0:T(8,128)(2,1)S(1)} %reduce_sum.12), channel_id=1, source_target_pairs={{0,16},{2,18},{4,20},{6,22},{8,24},{10,26},{12,28},{14,30},{16,0},... | collective-permute-start | bytes 393224 | tf_op jit(solution)/shard_map/ppermute | solution.py:314

commit v5 on v4

v5 whole, which is shorter than its diff:
```python
import functools

import jax
import jax.numpy as jnp
from jax import lax
from jax.experimental import pallas as pl
from jax.experimental.pallas import tpu as pltpu
from jax.sharding import PartitionSpec as P

HEAD = 128
GROUP = 8
BLOCK = 128
SCALE = HEAD ** (-0.5)
LOG2E = 1.4426950408889634
SCORE_SCALE = SCALE * LOG2E
TILE = 2 * BLOCK
WIDE = GROUP * BLOCK
BF16 = jnp.bfloat16
F32 = jnp.float32
BY_ROWS = (((1,), (1,)), ((), ()))


def by_rows(a, b):
    return lax.dot_general(a, b, BY_ROWS, preferred_element_type=F32)


def plain(a, b):
    return jnp.dot(a, b, preferred_element_type=F32)


def start_copies(sources, targets, sems):
    copies = [pltpu.make_async_copy(a, b, sems.at[n]) for n, (a, b) in enumerate(zip(sources, targets))]
    for copy in copies:
        copy.start()
    return copies


def here(part):
    return lax.axis_index("seq"), lax.axis_index("kvh") * part


def lists_kernel(part, lists, counts, spans, work, place):
    n_slots, local_blocks = spans.shape[0], (work.shape[0] - 1) // 3
    seq_at, turn = here(part)
    seq_bits = (n_slots // local_blocks).bit_length() - 1
    block_bits, half_bit = local_blocks.bit_length() - 1, seq_bits - 1
    part_bits = half_bit - 1 + block_bits

    def find(slot, carry):
        owner, block = slot >> block_bits, slot & (local_blocks - 1)
        apart = owner ^ seq_at
        is_far = apart >> half_bit
        middle = (jnp.where(is_far == 1, owner, apart) >> 1) & ((1 << (half_bit - 1)) - 1)
        block = jnp.where(is_far == 1, block, block ^ (turn >> 7))
        place[spans[slot]] = (((is_far << 1) | (apart & 1)) << part_bits) | (middle << block_bits) | block
        return carry

    lax.fori_loop(0, n_slots, find, 0, unroll=8)
    for i in range(local_blocks):
        at = spans[seq_at * local_blocks + i]
        near, far, every = (kind * local_blocks + i for kind in range(3))

        def clear(e, carry):
            for row in (near, far, every):
                work[row, e] = 0
            return carry

        def keep(e, sizes):
            found = place[lists[e, at]]
            is_far = found >> (part_bits + 1)
            work[near, sizes[0]] = found
            work[far, sizes[1]] = found
            work[every, e] = found
            return sizes[0] + 1 - is_far, sizes[1] + is_far

        lax.fori_loop(0, work.shape[1], clear, 0, unroll=8)
        near_size, far_size = lax.fori_loop(0, counts[at], keep, (0, 0))
        work[near, near_size] = 0
        work[far, far_size] = 0
        for kind, size in enumerate((near_size, far_size, counts[at])):
            work[3 * local_blocks, kind * local_blocks + i] = size


def heads(ref, i, first, many):
    rows = pl.ds(pl.multiple_of(i * BLOCK, BLOCK), BLOCK)
    return jnp.concatenate([ref[rows, h * HEAD : (h + 1) * HEAD] for h in range(first, first + many)], 0)


def rows_at(place):
    return pl.ds(pl.multiple_of(place * BLOCK, BLOCK), BLOCK)


def gathered(kv_ref, places, lanes):
    return jnp.concatenate([kv_ref[rows_at(p), lanes] for p in places], 0)


def allowed(many, count, turn, diagonal):
    if count is None:
        return None
    key_at = lax.broadcasted_iota(jnp.int32, (many * BLOCK, TILE), 0)
    entry = key_at // BLOCK
    mask = entry < count
    if diagonal:
        query_at = lax.broadcasted_iota(jnp.int32, (many * BLOCK, TILE), 1) & (BLOCK - 1)
        here = (key_at & (BLOCK - 1)) ^ (turn & (BLOCK - 1))
        mask = jnp.logical_and(mask, jnp.logical_or(entry > 0, here <= query_at))
    return mask


def split(count):
    first = (count + 3) % 4 + 1
    return first, (count - first) // 4


def sweep(count, step):
    first, quads = split(count)

    @pl.when(jnp.logical_and(count > 0, first <= 2))
    def _():
        step(0, 2, first)

    @pl.when(jnp.logical_and(count > 0, first > 2))
    def _():
        step(0, 4, first)

    def body(n, carry):
        step(first + 8 * n, 8, None)
        return carry

    lax.fori_loop(0, quads // 2, body, 0)

    @pl.when(jnp.logical_and(count > 0, quads % 2 == 1))
    def _():
        step(first + 4 * (quads - 1), 4, None)


def first_pass(i, places, mask, q_ref, do_ref, kv_ref, total, delta):
    keys = gathered(kv_ref, places, slice(0, HEAD))
    values = gathered(kv_ref, places, slice(HEAD, 2 * HEAD))
    for h in range(0, GROUP, 2):
        lanes = slice(h * BLOCK, h * BLOCK + TILE)
        expd = jnp.exp2(by_rows(keys, heads(q_ref, i, h, 2)) * SCORE_SCALE)
        if mask is not None:
            expd = jnp.where(mask, expd, 0.0)
        total[i, :, lanes] += jnp.sum(expd.reshape(-1, 8, TILE), 0)
        dweights = by_rows(values, heads(do_ref, i, h, 2))
        delta[i, :, lanes] += jnp.sum((expd * dweights).reshape(-1, 8, TILE), 0)


def near_kernel(part_rows, work, q_any, do_any, near_any, pair_any, total, delta, *scratch):
    q_ref, do_ref, kv_ref, sems = scratch
    local_blocks, part = q_ref.shape[0] // BLOCK, near_any.shape[0]
    _, turn = here(part_rows)
    copies = start_copies(
        [near_any, pair_any, q_any, do_any],
        [kv_ref.at[:part], kv_ref.at[part:], q_ref, do_ref],
        sems,
    )
    total[...] = jnp.zeros_like(total)
    delta[...] = jnp.zeros_like(delta)
    for copy in copies:
        copy.wait()

    def one_block(i, carry):
        def step(start, many, used):
            mask = allowed(many, used, turn, True)
            places = [work[i, start + e] for e in range(many)]
            first_pass(i, places, mask, q_ref, do_ref, kv_ref, total, delta)

        sweep(work[3 * local_blocks, i], step)
        return carry

    lax.fori_loop(0, local_blocks, one_block, 0)


def main_kernel(part_rows, work, q_any, do_any, total_in, delta_in, *refs):
    part_refs, (dqt_ref, *out_refs), scratch = refs[:4], refs[4:9], refs[9:]
    q_ref, do_ref, kv_ref, total, delta, w_scr, ds_scr, acc, sems = scratch
    local_blocks, part = q_ref.shape[0] // BLOCK, part_refs[0].shape[0]
    seq_at, turn = here(part_rows)

    def part_of(p):
        return slice(p * part, (p + 1) * part)

    copies = start_copies(
        [*part_refs, q_any, do_any], [*(kv_ref.at[part_of(p)] for p in range(4)), q_ref, do_ref], sems
    )
    acc[...] = jnp.zeros_like(acc)
    dqt_ref[...] = jnp.zeros_like(dqt_ref)
    total[...] = total_in[...]
    delta[...] = delta_in[...]
    for copy in copies:
        copy.wait()

    def weigh(i, places, mask):
        keys = gathered(kv_ref, places, slice(0, HEAD))
        values = gathered(kv_ref, places, slice(HEAD, 2 * HEAD))
        rows = slice(0, len(places) * BLOCK)
        for h in range(0, GROUP, 2):
            lanes = slice(h * BLOCK, h * BLOCK + TILE)
            scores = by_rows(keys, heads(q_ref, i, h, 2))
            weights = jnp.exp2(scores * SCORE_SCALE - total[i, 0:1, lanes])
            if mask is not None:
                weights = jnp.where(mask, weights, 0.0)
            dweights = by_rows(values, heads(do_ref, i, h, 2))
            w_scr[rows, lanes] = weights.astype(BF16)
            ds_scr[rows, lanes] = (weights * (dweights - delta[i, 0:1, lanes])).astype(BF16)

    def spread(i, places):
        keys = gathered(kv_ref, places, slice(0, HEAD))
        rows = slice(0, len(places) * BLOCK)
        dk = plain(ds_scr[rows], heads(q_ref, i, 0, GROUP))
        dv = plain(w_scr[rows], heads(do_ref, i, 0, GROUP))
        dqt_ref[i] += plain(keys.T, ds_scr[rows])
        for n, p in enumerate(places):
            acc[rows_at(p), :HEAD] += dk[n * BLOCK : (n + 1) * BLOCK]
            acc[rows_at(p), HEAD:] += dv[n * BLOCK : (n + 1) * BLOCK]

    def one_block(i, carry):
        count = work[3 * local_blocks, 2 * local_blocks + i]

        def far_step(start, many, used):
            mask = allowed(many, used, turn, False)
            places = [work[local_blocks + i, start + e] for e in range(many)]
            first_pass(i, places, mask, q_ref, do_ref, kv_ref, total, delta)

        def places(start, many):
            return [work[2 * local_blocks + i, start + e] for e in range(many)]

        def begin(many):
            weigh(i, places(0, many), allowed(many, first, turn, True))
            spread(i, places(0, many))

        def body(n, carry):
            spread(i, places(first + 4 * n - 4, 4))
            weigh(i, places(first + 4 * n, 4), None)
            return carry

        sweep(work[3 * local_blocks, local_blocks + i], far_step)
        row_total = jnp.sum(total[i], 0, keepdims=True)
        row_delta = jnp.sum(delta[i], 0, keepdims=True) / row_total
        total[i] = jnp.broadcast_to(jnp.log2(row_total), (8, WIDE))
        delta[i] = jnp.broadcast_to(row_delta, (8, WIDE))
        first, quads = split(count)
        pl.when(first <= 2)(lambda: begin(2))
        pl.when(first > 2)(lambda: begin(4))

        @pl.when(quads > 0)
        def _():
            weigh(i, places(first, 4), None)
            lax.fori_loop(1, quads, body, 0)
            spread(i, places(first + 4 * quads - 4, 4))

        return carry

    lax.fori_loop(0, local_blocks, one_block, 0)
    for p in range(2):
        out_refs[p][...] = acc[part_of(p)].astype(BF16)
    span = q_ref.shape[0]
    middle = (seq_at >> 1) & (part // span - 1)
    for p in range(2, 4):
        for at in range(0, part, part_rows):
            m, row = at // span, at % span
            start = p * part + (m ^ middle) * span + (row ^ turn)
            rows = pl.ds(pl.multiple_of(start, part_rows), part_rows)
            out_refs[p][at : at + part_rows] = acc[rows].astype(BF16)


LIMIT = 32 << 20
SMEM = pl.BlockSpec(memory_space=pltpu.SMEM)
VMEM = pl.BlockSpec(memory_space=pltpu.VMEM)
ANY = pl.BlockSpec(memory_space=pl.ANY)


def resolve(lists, counts, spans, local_blocks, part):
    return pl.pallas_call(
        functools.partial(lists_kernel, part),
        in_specs=[SMEM] * 3,
        out_specs=SMEM,
        out_shape=jax.ShapeDtypeStruct((3 * local_blocks + 1, lists.shape[0] + 8), jnp.int32),
        scratch_shapes=[pltpu.SMEM(spans.shape, jnp.int32)],
        name="lists",
    )(lists, counts, spans)


def near_sums(part_rows, work, q, do, near, pair):
    local_blocks, rows = q.shape[0] // BLOCK, 2 * near.shape[0]
    return pl.pallas_call(
        functools.partial(near_kernel, part_rows),
        in_specs=[SMEM] + [ANY] * 4,
        out_specs=[VMEM] * 2,
        out_shape=[jax.ShapeDtypeStruct((local_blocks, 8, WIDE), F32)] * 2,
        scratch_shapes=[
            pltpu.VMEM(q.shape, BF16),
            pltpu.VMEM(do.shape, BF16),
            pltpu.VMEM((rows, 2 * HEAD), BF16),
            pltpu.SemaphoreType.DMA((4,)),
        ],
        compiler_params=pltpu.CompilerParams(vmem_limit_bytes=LIMIT),
        cost_estimate=pl.CostEstimate(flops=1 << 20, bytes_accessed=1 << 10, transcendentals=0),
        name="near",
    )(work, q, do, near, pair)


def attend(part_rows, work, q, do, total, delta, parts):
    local_blocks, rows = q.shape[0] // BLOCK, 4 * parts[0].shape[0]
    return pl.pallas_call(
        functools.partial(main_kernel, part_rows),
        in_specs=[SMEM] + [ANY] * 2 + [VMEM] * 2 + [ANY] * 4,
        out_specs=[VMEM] * 5,
        out_shape=[jax.ShapeDtypeStruct((local_blocks, HEAD, WIDE), F32)]
        + [jax.ShapeDtypeStruct(x.shape, BF16) for x in parts],
        scratch_shapes=[
            pltpu.VMEM(q.shape, BF16),
            pltpu.VMEM(do.shape, BF16),
            pltpu.VMEM((rows, 2 * HEAD), BF16),
            pltpu.VMEM((local_blocks, 8, WIDE), F32),
            pltpu.VMEM((local_blocks, 8, WIDE), F32),
            pltpu.VMEM((4 * BLOCK, WIDE), BF16),
            pltpu.VMEM((4 * BLOCK, WIDE), BF16),
            pltpu.VMEM((rows, 2 * HEAD), F32),
            pltpu.SemaphoreType.DMA((6,)),
        ],
        compiler_params=pltpu.CompilerParams(vmem_limit_bytes=LIMIT),
        name="attend",
    )(work, q, do, total, delta, *parts)


def shards(
    queries,
    key_vector_rows,
    value_vector_rows,
    output_gradient,
    key_lists,
    block_counts,
    span_table,
):
    seq_devices, kv_devices = lax.axis_size("seq"), lax.axis_size("kvh")
    seq_at, kv_at = lax.axis_index("seq"), lax.axis_index("kvh")
    per_kvh = key_vector_rows.shape[0]
    half, middles = seq_devices // 2, seq_devices // 4
    span_rows = kv_devices * per_kvh
    near_groups = [
        [
            (top * half + middle * 2 + core) * kv_devices + head
            for middle in range(middles)
            for head in range(kv_devices)
        ]
        for top in range(2)
        for core in range(2)
    ]

    def swap(x, seq_step, kv_step):
        if seq_step == 0 and kv_step == 0:
            return x
        pairs = [
            (s * kv_devices + h, (s ^ seq_step) * kv_devices + (h ^ kv_step))
            for s in range(seq_devices)
            for h in range(kv_devices)
        ]
        return lax.ppermute(x, ("seq", "kvh"), pairs)

    def exchange_near(x):
        x = x.reshape(middles * kv_devices, per_kvh, 2 * HEAD)
        return lax.all_to_all(x, ("seq", "kvh"), 0, 0, axis_index_groups=near_groups)

    work = resolve(key_lists.T, block_counts, span_table, queries.shape[0] // BLOCK, per_kvh)
    own = jnp.stack(
        [
            jnp.concatenate([x[:, h * HEAD : (h + 1) * HEAD] for x in (key_vector_rows, value_vector_rows)], 1)
            for h in range(kv_devices)
        ]
    )
    far = swap(own, half, 0)
    mine = [lax.dynamic_index_in_dim(own, kv_at ^ j, 0, False) for j in range(kv_devices)]
    near_span = jnp.concatenate([swap(mine[j], 0, j) for j in range(kv_devices)], 0)
    near_part = jnp.concatenate([swap(near_span, 2 * m, 0) for m in range(middles)], 0)
    near_pair = swap(near_part, 1, 0)
    far, work = lax.optimization_barrier((far, work))
    far_part = exchange_near(jnp.broadcast_to(far[None], (middles, *far.shape)))
    far_part = far_part.reshape(near_part.shape)

    common = (per_kvh, work, queries, output_gradient)
    total, delta = near_sums(*common, near_part, near_pair)
    total, far_part = lax.optimization_barrier((total, far_part))
    far_pair = swap(far_part, 1, 0)
    dqt, *partials = attend(*common, total, delta, [near_part, near_pair, far_part, far_pair])
    dq = jnp.transpose(dqt.reshape(-1, HEAD, GROUP, BLOCK), (0, 3, 2, 1)) * SCALE
    grad_queries = dq.reshape(queries.shape).astype(BF16)

    def chip_rows(kept, received, m):
        rows = slice(m * span_rows, (m + 1) * span_rows)
        return kept[rows].astype(F32) + received[rows].astype(F32)

    def sent_to_middles(kept, received):
        return [swap(chip_rows(kept, received, m).astype(BF16), 2 * m, 0) for m in range(1, middles)]

    def added(kept, received, others):
        return sum([x.astype(F32) for x in others], chip_rows(kept, received, 0))

    def to_owners(span, seq_step):
        pieces = [span[j * per_kvh : (j + 1) * per_kvh] for j in range(kv_devices)]
        return [
            x if seq_step + j == 0 else swap(x.astype(BF16), seq_step, j).astype(F32)
            for j, x in enumerate(pieces)
        ]

    far_received, near_received = swap(partials[3], 1, 0), swap(partials[1], 1, 0)
    far_others = sent_to_middles(partials[2], far_received)
    near_others = sent_to_middles(partials[0], near_received)
    far_sums = to_owners(added(partials[2], far_received, far_others), half)
    near_grads = to_owners(added(partials[0], near_received, near_others), 0)
    sums = jnp.stack([x + y for x, y in zip(near_grads, far_sums)])
    sums = [lax.dynamic_index_in_dim(sums, kv_at ^ h, 0, False) for h in range(kv_devices)]
    key_gradient = jnp.concatenate([x[:, :HEAD] * SCALE for x in sums], 1).astype(BF16)
    value_gradient = jnp.concatenate([x[:, HEAD:] for x in sums], 1).astype(BF16)
    return grad_queries, key_gradient, value_gradient


def solution(mesh):
    placed = (
        P("seq", "kvh"),
        P(("seq", "kvh"), None),
        P(("seq", "kvh"), None),
        P("seq", "kvh"),
        P(),
        P(),
        P(),
    )
    return jax.shard_map(
        shards,
        mesh=mesh,
        in_specs=placed,
        out_specs=(P("seq", "kvh"), P(("seq", "kvh"), None), P(("seq", "kvh"), None)),
        check_vma=False,
    )
```

time: 88.7 us -> 77.4 us (0.87); the launches traced: 87.4 us -> 78.9 us
  waiting for transfers between devices: 24.7 us -> 16.9 us
  Pallas kernels: 15.1 us -> 21.5 us
  other arithmetic: 5.83 us -> 1.96 us
  starting transfers between devices: 35.9 us -> 34.1 us
  local copies, waits for them, and re-layouts: 4.98 us -> 3.55 us
    pallas_call x2 -> x3, Pallas kernels: 15.1 us -> 21.5 us  [the longest x1 16.2 us: attend(): pl.pallas_call(functools.partial(main_kernel, part_rows), in_specs=[SMEM]...]
    all_to_all x2 -> x1, starting transfers between devices: 10.4 us -> 4.86 us  [exchange_near(): lax.all_to_all(x, ('seq', 'kvh'), 0, 0, axis_index_groups=near_groups)]
    ppermute x14 -> x18, waiting for transfers between devices: 19.1 us -> 14.4 us  [swap(): return lax.ppermute(x, ('seq', 'kvh'), pairs)]
    ppermute x14 -> x18, starting transfers between devices: 25.5 us -> 29.2 us  [swap(): return lax.ppermute(x, ('seq', 'kvh'), pairs)]
    all_to_all x2 -> x1, waiting for transfers between devices: 5.6 us -> 2.49 us  [exchange_near(): lax.all_to_all(x, ('seq', 'kvh'), 0, 0, axis_index_groups=near_groups)]
    convert_element_type x3 -> x2, other arithmetic: 2.08 us -> 0.19 us  [sent_to_middles(): chip_rows(kept, received, m).astype(BF16)]
    unnamed x26 -> x17, local copies, waits for them, and re-layouts: 2.8 us -> 1.36 us
    reduce_sum x1 -> x0, other arithmetic: 1.12 us -> none  [shards(): far_sums = jnp.sum(far_sums.astype(F32), 0).astype(BF16)]
  transfers between devices with their start and end apart: 16 -> 19, of which waited for: 11 -> 8; matrix products, arithmetic and copies ran while one was open for 7% -> 4% of each run, Pallas kernels for 5% -> 7%
where the time goes in v5:
time: 77.4 us; the launch traced here: 78.9 us
  starting transfers between devices  34.1 us (44%)
  Pallas kernels  21.5 us (28%)
  waiting for transfers between devices  16.9 us (22%)
  local copies, waits for them, and re-layouts  3.55 us (5%)
  other arithmetic  1.96 us (3%)
  between operations  0.93 us (1%)
    ppermute x18, starting transfers between devices, swap(): return lax.ppermute(x, ('seq', 'kvh'), pairs)  29.2 us
    pallas_call x1, Pallas kernels, attend(): pl.pallas_call(functools.partial(main_kernel, part_rows), in_specs=[SMEM]...  16.2 us
    ppermute x18, waiting for transfers between devices, swap(): return lax.ppermute(x, ('seq', 'kvh'), pairs)  14.4 us
    all_to_all x1, starting transfers between devices, exchange_near(): lax.all_to_all(x, ('seq', 'kvh'), 0, 0, axis_index_groups=near_groups)  4.86 us
    pallas_call x1, Pallas kernels, near_sums(): pl.pallas_call(functools.partial(near_kernel, part_rows), in_specs=[SMEM]...  3.06 us
    all_to_all x1, waiting for transfers between devices, exchange_near(): lax.all_to_all(x, ('seq', 'kvh'), 0, 0, axis_index_groups=near_groups)  2.49 us
    pallas_call x1, Pallas kernels, resolve(): pl.pallas_call(functools.partial(lists_kernel, part), in_specs=[SMEM] * 3...  2.23 us
  transfers between devices with their start and end apart: 19, of which 8 were waited for; matrix products, arithmetic and copies ran while one was open for 4% of the time, Pallas kernels for 7%

profile of v5, /device:TPU:0, one launch (start us, length us, event | category | flops | bytes accessed | tf_op | source)
XLA Modules:
  0.0 78.9 jit_solution(9715689399284043192)
XLA Ops:
  0.6 0.8 %fusion.13 = (bf16[128,128]{1,0:T(8,128)(2,1)S(1)}, bf16[128,128]{1,0:T(8,128)(2,1)S(1)}) fusion(bf16[128,256]{1,0:T(8,128)(2,1)} %param.8), kind=kLoop, calls=%fused_computation.49 | loop fusion | bytes 131072 | tf_op jit(solution)/shard_map/slice | solution.py:370
  1.5 0.0 copy-done.5
  1.6 3.0 %collective-permute-start.1 = (bf16[128,256]{1,0:T(8,128)(2,1)S(1)}, bf16[128,256]{1,0:T(8,128)(2,1)S(1)}, u32[]{:S(2)}, u32[]{:S(2)}) collective-permute-start(bf16[128,256]{1,0:T(8,128)(2,1)S(1)} %fusion.8), channel_id=1, source_target_pairs={{0,1},{1,0},{2,3},{3,2},{4,5},{5,4},{6,7},{7,6},{8,9},{9,8},{10,11... | collective-permute-start | bytes 196616 | tf_op jit(solution)/shard_map/ppermute | solution.py:361
  4.6 2.7 %collective-permute-start = (bf16[2,128,256]{2,1,0:T(8,128)(2,1)S(1)}, bf16[2,128,256]{2,1,0:T(8,128)(2,1)S(1)}, u32[]{:S(2)}, u32[]{:S(2)}) collective-permute-start(bf16[2,128,256]{2,1,0:T(8,128)(2,1)S(1)} %pad_maximum_fusion), channel_id=1, source_target_pairs={{0,16},{1,17},{2,18},{3,19},{4,20},{5,21},{6,22},{7,23},{8,24},{9,... | collective-permute-start | bytes 393224 | tf_op jit(solution)/shard_map/ppermute | solution.py:361
  7.3 0.0 collective-permute-done.1
  7.3 1.6 %collective-permute-start.2 = (bf16[256,256]{1,0:T(8,128)(2,1)S(1)}, bf16[256,256]{1,0:T(8,128)(2,1)S(1)}, u32[]{:S(2)}, u32[]{:S(2)}) collective-permute-start(bf16[256,256]{1,0:T(8,128)(2,1)S(1)} %pad_maximum_fusion.1), channel_id=1, source_target_pairs={{0,4},{1,5},{2,6},{3,7},{4,0},{5,1},{6,2},{7,3},{8,12},{9,13},{10,... | collective-permute-start | bytes 393224 | tf_op jit(solution)/shard_map/ppermute | solution.py:361
  8.9 2.2 %lists.1.work = s32[7,32]{1,0:T(8,128)} custom-call(s32[24,32]{1,0:T(8,128)} %bitcast.39, s32[32]{0:T(128)} %counts.1, s32[32]{0:T(128)} %spans.1), custom_call_target="tpu_custom_call" | custom-call | tf_op jit(solution)/shard_map/lists/pallas_call | solution.py:276
  11.2 1.7 %collective-permute-start.4 = (bf16[256,256]{1,0:T(8,128)(2,1)S(1)}, bf16[256,256]{1,0:T(8,128)(2,1)S(1)}, u32[]{:S(2)}, u32[]{:S(2)}) collective-permute-start(bf16[256,256]{1,0:T(8,128)(2,1)S(1)} %pad_maximum_fusion.1), channel_id=1, source_target_pairs={{0,12},{1,13},{2,14},{3,15},{4,8},{5,9},{6,10},{7,11},{8,4},{9,5},... | collective-permute-start | bytes 393224 | tf_op jit(solution)/shard_map/ppermute | solution.py:361
  12.9 0.3 collective-permute-start.3
  13.2 0.2 collective-permute-done
  13.4 0.8 %broadcast_in_dim.2 = bf16[4,2,128,256]{3,2,1,0:T(8,128)(2,1)} broadcast(bf16[2,128,256]{2,1,0:T(8,128)(2,1)S(1)} %collective-permute-done), dimensions={1,2,3} | broadcast | bytes 655360 | tf_op jit(solution)/shard_map/broadcast_in_dim | solution.py:380
  14.2 4.9 %all-to-all-start = ((bf16[8,128,256]{2,1,0:T(8,128)(2,1)}), bf16[8,128,256]{2,1,0:T(8,128)(2,1)S(1)}, u32[]{:S(2)}, u32[]{:S(2)}) async-start(bf16[8,128,256]{2,1,0:T(8,128)(2,1)} %bitcast.5), calls=%async_computation | async-start | bytes 1048576 | tf_op jit(solution)/shard_map/all_to_all | solution.py:365
  19.1 0.0 collective-permute-done.2
  19.1 0.0 copy-start.4
  19.2 0.1 collective-permute-start.5
  19.3 1.9 %collective-permute-done.5.pair_any.refs_1_ = bf16[1024,256]{1,0:T(8,128)(2,1)S(1)} collective-permute-done((bf16[1024,256]{1,0:T(8,128)(2,1)S(1)}, bf16[1024,256]{1,0:T(8,128)(2,1)S(1)}, u32[]{:S(2)}, u32[]{:S(2)}) %collective-permute-start.5) | collective-permute-done | bytes 524320 | tf_op jit(solution)/shard_map/ppermute | solution.py:361
  21.2 3.1 %near.1 = (f32[2,8,1024]{2,1,0:T(8,128)S(1)}, f32[2,8,1024]{2,1,0:T(8,128)S(1)}) custom-call(s32[7,32]{1,0:T(8,128)S(1)} %copy-done.4, bf16[256,1024]{1,0:T(8,128)(2,1)S(1)} %copy-done, bf16[256,1024]{1,0:T(8,128)(2,1)S(1)} %copy-done.1, bf16[1024,256]{1,0:T(8,128)(2,1)S(1)} %constant_dynamic-update-slice_fusion.near_any.refs_0_, ...), custom_call_target="tpu_custom_call" | custom-call | flops 1048576 | bytes 1024 | tf_op jit(solution)/shard_map/near/pallas_call | solution.py:288
  24.2 2.5 %all-to-all-done = bf16[8,128,256]{2,1,0:T(8,128)(2,1)S(1)} async-done(((bf16[8,128,256]{2,1,0:T(8,128)(2,1)}), bf16[8,128,256]{2,1,0:T(8,128)(2,1)S(1)}, u32[]{:S(2)}, u32[]{:S(2)}) %all-to-all-start) | async-done | bytes 524320 | tf_op jit(solution)/shard_map/all_to_all | solution.py:365
  26.7 1.9 %collective-permute-done.6.refs_3_ = bf16[1024,256]{1,0:T(8,128)(2,1)S(1)} collective-permute-done((bf16[1024,256]{1,0:T(8,128)(2,1)S(1)}, bf16[1024,256]{1,0:T(8,128)(2,1)S(1)}, u32[]{:S(2)}, u32[]{:S(2)}) %collective-permute-start.6) | collective-permute-done | bytes 524320 | tf_op jit(solution)/shard_map/ppermute | solution.py:361
  28.6 16.2 %attend.1 = (f32[2,128,1024]{2,1,0:T(8,128)S(1)}, bf16[1024,256]{1,0:T(8,128)(2,1)S(1)}, bf16[1024,256]{1,0:T(8,128)(2,1)}, bf16[1024,256]{1,0:T(8,128)(2,1)S(1)}, bf16[1024,256]{1,0:T(8,128)(2,1)}) custom-call(s32[7,32]{1,0:T(8,128)S(1)} %copy-done.4, bf16[256,1024]{1,0:T(8,128)(2,1)S(1)} %copy-done, bf16[256,1024]{1,0:T(8,128)(2,1)S(1)} %copy-done.1, ...), custom_call_target="tpu_custom_call" | custom-call | tf_op jit(solution)/shard_map/attend/pallas_call | solution.py:307
  44.9 0.1 collective-permute-start.11
  45.0 0.5 collective-permute-start.7
  45.5 0.1 multiply_convert_fusion
  45.6 0.1 copy-done.2
  45.7 0.1 copy.11
  45.8 0.5 copy.10
  46.3 0.9 %copy.14 = bf16[32,8,8,128]{3,1,2,0:T(8,128)(2,1)} copy(bf16[32,8,8,128]{3,2,1,0:T(8,128)(2,1)S(1)} %bitcast.37) | data formatting | bytes 1048576
  47.2 0.2 copy-done.3
  47.4 0.1 add_convert_fusion.3
  47.5 3.6 %collective-permute-start.12 = (bf16[256,256]{1,0:T(8,128)(2,1)S(1)}, bf16[256,256]{1,0:T(8,128)(2,1)S(1)}, u32[]{:S(2)}, u32[]{:S(2)}) collective-permute-start(bf16[256,256]{1,0:T(8,128)(2,1)S(1)} %get-tuple-element.27), channel_id=1, source_target_pairs={{0,4},{1,5},{2,6},{3,7},{4,0},{5,1},{6,2},{7,3},{8,12},{9,13},{10,... | collective-permute-start | bytes 393224 | tf_op jit(solution)/shard_map/ppermute | solution.py:361
  51.1 4.9 %collective-permute-start.14 = (bf16[256,256]{1,0:T(8,128)(2,1)S(1)}, bf16[256,256]{1,0:T(8,128)(2,1)S(1)}, u32[]{:S(2)}, u32[]{:S(2)}) collective-permute-start(bf16[256,256]{1,0:T(8,128)(2,1)S(1)} %get-tuple-element.28), channel_id=1, source_target_pairs={{0,12},{1,13},{2,14},{3,15},{4,8},{5,9},{6,10},{7,11},{8,4},{9,5},... | collective-permute-start | bytes 393224 | tf_op jit(solution)/shard_map/ppermute | solution.py:361
  56.0 0.0 collective-permute-done.7
  56.0 0.1 add_convert_fusion.6
  56.1 0.9 %collective-permute-start.8 = (bf16[256,256]{1,0:T(8,128)(2,1)S(1)}, bf16[256,256]{1,0:T(8,128)(2,1)S(1)}, u32[]{:S(2)}, u32[]{:S(2)}) collective-permute-start(bf16[256,256]{1,0:T(8,128)(2,1)S(1)} %get-tuple-element.30), channel_id=1, source_target_pairs={{0,4},{1,5},{2,6},{3,7},{4,0},{5,1},{6,2},{7,3},{8,12},{9,13},{10,... | collective-permute-start | bytes 393224 | tf_op jit(solution)/shard_map/ppermute | solution.py:361
  57.0 2.6 %collective-permute-start.10 = (bf16[256,256]{1,0:T(8,128)(2,1)S(1)}, bf16[256,256]{1,0:T(8,128)(2,1)S(1)}, u32[]{:S(2)}, u32[]{:S(2)}) collective-permute-start(bf16[256,256]{1,0:T(8,128)(2,1)S(1)} %get-tuple-element.31), channel_id=1, source_target_pairs={{0,12},{1,13},{2,14},{3,15},{4,8},{5,9},{6,10},{7,11},{8,4},{9,5},... | collective-permute-start | bytes 393224 | tf_op jit(solution)/shard_map/ppermute | solution.py:361
  59.6 4.0 %collective-permute-start.9 = (bf16[256,256]{1,0:T(8,128)(2,1)S(1)}, bf16[256,256]{1,0:T(8,128)(2,1)S(1)}, u32[]{:S(2)}, u32[]{:S(2)}) collective-permute-start(bf16[256,256]{1,0:T(8,128)(2,1)S(1)} %get-tuple-element.32), channel_id=1, source_target_pairs={{0,8},{1,9},{2,10},{3,11},{4,12},{5,13},{6,14},{7,15},{8,0},{9,1},... | collective-permute-start | bytes 393224 | tf_op jit(solution)/shard_map/ppermute | solution.py:361
  63.6 0.1 add_convert_fusion
  63.7 0.6 collective-permute-start.15
  64.4 1.5 %collective-permute-done.10 = bf16[256,256]{1,0:T(8,128)(2,1)S(1)} collective-permute-done((bf16[256,256]{1,0:T(8,128)(2,1)S(1)}, bf16[256,256]{1,0:T(8,128)(2,1)S(1)}, u32[]{:S(2)}, u32[]{:S(2)}) %collective-permute-start.10) | collective-permute-done | bytes 131104 | tf_op jit(solution)/shard_map/ppermute | solution.py:361
  65.9 2.6 %collective-permute-done.9 = bf16[256,256]{1,0:T(8,128)(2,1)S(1)} collective-permute-done((bf16[256,256]{1,0:T(8,128)(2,1)S(1)}, bf16[256,256]{1,0:T(8,128)(2,1)S(1)}, u32[]{:S(2)}, u32[]{:S(2)}) %collective-permute-start.9) | collective-permute-done | bytes 131104 | tf_op jit(solution)/shard_map/ppermute | solution.py:361
  68.5 0.1 convert_add_fusion
  68.6 2.1 %collective-permute-start.16 = (bf16[128,256]{1,0:T(8,128)(2,1)S(1)}, bf16[128,256]{1,0:T(8,128)(2,1)S(1)}, u32[]{:S(2)}, u32[]{:S(2)}) collective-permute-start(bf16[128,256]{1,0:T(8,128)(2,1)S(1)} %slice.161), channel_id=1, source_target_pairs={{0,1},{1,0},{2,3},{3,2},{4,5},{5,4},{6,7},{7,6},{8,9},{9,8},{10,11... | collective-permute-start | bytes 196616 | tf_op jit(solution)/shard_map/ppermute | solution.py:361
  70.7 0.5 collective-permute-start.17
  71.2 1.8 %collective-permute-done.16 = bf16[128,256]{1,0:T(8,128)(2,1)S(1)} collective-permute-done((bf16[128,256]{1,0:T(8,128)(2,1)S(1)}, bf16[128,256]{1,0:T(8,128)(2,1)S(1)}, u32[]{:S(2)}, u32[]{:S(2)}) %collective-permute-start.16) | collective-permute-done | bytes 65568 | tf_op jit(solution)/shard_map/ppermute | solution.py:361
  73.0 4.5 %collective-permute-done.17 = bf16[128,256]{1,0:T(8,128)(2,1)S(1)} collective-permute-done((bf16[128,256]{1,0:T(8,128)(2,1)S(1)}, bf16[128,256]{1,0:T(8,128)(2,1)S(1)}, u32[]{:S(2)}, u32[]{:S(2)}) %collective-permute-start.17) | collective-permute-done | bytes 65568 | tf_op jit(solution)/shard_map/ppermute | solution.py:361
  77.5 0.1 fusion.3
  77.6 0.6 pad_maximum_fusion.2
  78.3 0.6 pad_maximum_fusion.3
  (37 shorter events, 0.3 us)
Async XLA Ops:
  0.6 0.8 %copy-start.5 = (bf16[128,256]{1,0:T(8,128)(2,1)S(1)}, bf16[128,256]{1,0:T(8,128)(2,1)}, u32[]{:S(2)}) copy-start(bf16[128,256]{1,0:T(8,128)(2,1)} %param.9) | copy-start | bytes 196612
  1.6 5.7 %collective-permute-start.1 = (bf16[128,256]{1,0:T(8,128)(2,1)S(1)}, bf16[128,256]{1,0:T(8,128)(2,1)S(1)}, u32[]{:S(2)}, u32[]{:S(2)}) collective-permute-start(bf16[128,256]{1,0:T(8,128)(2,1)S(1)} %fusion.8), channel_id=1, source_target_pairs={{0,1},{1,0},{2,3},{3,2},{4,5},{5,4},{6,7},{7,6},{8,9},{9,8},{10,11... | collective-permute-start | bytes 196616 | tf_op jit(solution)/shard_map/ppermute | solution.py:361
  4.6 8.8 %collective-permute-start = (bf16[2,128,256]{2,1,0:T(8,128)(2,1)S(1)}, bf16[2,128,256]{2,1,0:T(8,128)(2,1)S(1)}, u32[]{:S(2)}, u32[]{:S(2)}) collective-permute-start(bf16[2,128,256]{2,1,0:T(8,128)(2,1)S(1)} %pad_maximum_fusion), channel_id=1, source_target_pairs={{0,16},{1,17},{2,18},{3,19},{4,20},{5,21},{6,22},{7,23},{8,24},{9,... | collective-permute-start | bytes 393224 | tf_op jit(solution)/shard_map/ppermute | solution.py:361
  7.3 11.8 %collective-permute-start.2 = (bf16[256,256]{1,0:T(8,128)(2,1)S(1)}, bf16[256,256]{1,0:T(8,128)(2,1)S(1)}, u32[]{:S(2)}, u32[]{:S(2)}) collective-permute-start(bf16[256,256]{1,0:T(8,128)(2,1)S(1)} %pad_maximum_fusion.1), channel_id=1, source_target_pairs={{0,4},{1,5},{2,6},{3,7},{4,0},{5,1},{6,2},{7,3},{8,12},{9,13},{10,... | collective-permute-start | bytes 393224 | tf_op jit(solution)/shard_map/ppermute | solution.py:361
  11.2 8.0 %collective-permute-start.4 = (bf16[256,256]{1,0:T(8,128)(2,1)S(1)}, bf16[256,256]{1,0:T(8,128)(2,1)S(1)}, u32[]{:S(2)}, u32[]{:S(2)}) collective-permute-start(bf16[256,256]{1,0:T(8,128)(2,1)S(1)} %pad_maximum_fusion.1), channel_id=1, source_target_pairs={{0,12},{1,13},{2,14},{3,15},{4,8},{5,9},{6,10},{7,11},{8,4},{9,5},... | collective-permute-start | bytes 393224 | tf_op jit(solution)/shard_map/ppermute | solution.py:361
  12.9 6.2 %collective-permute-start.3 = (bf16[256,256]{1,0:T(8,128)(2,1)S(1)}, bf16[256,256]{1,0:T(8,128)(2,1)S(1)}, u32[]{:S(2)}, u32[]{:S(2)}) collective-permute-start(bf16[256,256]{1,0:T(8,128)(2,1)S(1)} %pad_maximum_fusion.1), channel_id=1, source_target_pairs={{0,8},{1,9},{2,10},{3,11},{4,12},{5,13},{6,14},{7,15},{8,0},{9,1},... | collective-permute-start | bytes 393224 | tf_op jit(solution)/shard_map/ppermute | solution.py:361
  14.2 7.0 %copy-start.1 = (bf16[256,1024]{1,0:T(8,128)(2,1)S(1)}, bf16[256,1024]{1,0:T(8,128)(2,1)}, u32[]{:S(2)}) copy-start(bf16[256,1024]{1,0:T(8,128)(2,1)} %do_any.3) | copy-start | bytes 1572868
  14.2 12.5 %all-to-all-start = ((bf16[8,128,256]{2,1,0:T(8,128)(2,1)}), bf16[8,128,256]{2,1,0:T(8,128)(2,1)S(1)}, u32[]{:S(2)}, u32[]{:S(2)}) async-start(bf16[8,128,256]{2,1,0:T(8,128)(2,1)} %bitcast.5), calls=%async_computation | async-start | bytes 1048576 | tf_op jit(solution)/shard_map/all_to_all | solution.py:365
  19.1 2.1 %copy-start = (bf16[256,1024]{1,0:T(8,128)(2,1)S(1)}, bf16[256,1024]{1,0:T(8,128)(2,1)}, u32[]{:S(2)}) copy-start(bf16[256,1024]{1,0:T(8,128)(2,1)} %q_any.3) | copy-start | bytes 1572868
  19.1 2.0 %copy-start.4 = (s32[7,32]{1,0:T(8,128)S(1)}, s32[7,32]{1,0:T(8,128)}, u32[]{:S(2)}) copy-start(s32[7,32]{1,0:T(8,128)} %lists.1.work) | copy-start | bytes 2692
  19.2 2.0 %collective-permute-start.5 = (bf16[1024,256]{1,0:T(8,128)(2,1)S(1)}, bf16[1024,256]{1,0:T(8,128)(2,1)S(1)}, u32[]{:S(2)}, u32[]{:S(2)}) collective-permute-start(bf16[1024,256]{1,0:T(8,128)(2,1)S(1)} %constant_dynamic-update-slice_fusion.near_any.refs_0_), channel_id=1, source_target_pairs={{0,2},{1,3},{2,0},{3,1},{4,6},{5,7},{6,4},{7,5},{8,10},{9,11},{10,... | collective-permute-start | bytes 1572872 | tf_op jit(solution)/shard_map/ppermute | solution.py:361
  26.7 1.9 %collective-permute-start.6 = (bf16[1024,256]{1,0:T(8,128)(2,1)S(1)}, bf16[1024,256]{1,0:T(8,128)(2,1)S(1)}, u32[]{:S(2)}, u32[]{:S(2)}) collective-permute-start(bf16[1024,256]{1,0:T(8,128)(2,1)S(1)} %bitcast.33), channel_id=1, source_target_pairs={{0,2},{1,3},{2,0},{3,1},{4,6},{5,7},{6,4},{7,5},{8,10},{9,11},{10,... | collective-permute-start | bytes 1572872 | tf_op jit(solution)/shard_map/ppermute | solution.py:361
  44.9 0.8 copy-start.2
  44.9 2.3 %collective-permute-start.11 = (bf16[1024,256]{1,0:T(8,128)(2,1)}, bf16[1024,256]{1,0:T(8,128)(2,1)S(1)}, u32[]{:S(2)}, u32[]{:S(2)}) collective-permute-start(bf16[1024,256]{1,0:T(8,128)(2,1)} %get-tuple-element.24), channel_id=1, source_target_pairs={{0,2},{1,3},{2,0},{3,1},{4,6},{5,7},{6,4},{7,5},{8,10},{9,11},{10,... | collective-permute-start | bytes 1572872 | tf_op jit(solution)/shard_map/ppermute | solution.py:361
  45.0 11.0 %collective-permute-start.7 = (bf16[1024,256]{1,0:T(8,128)(2,1)}, bf16[1024,256]{1,0:T(8,128)(2,1)S(1)}, u32[]{:S(2)}, u32[]{:S(2)}) collective-permute-start(bf16[1024,256]{1,0:T(8,128)(2,1)} %get-tuple-element.22), channel_id=1, source_target_pairs={{0,2},{1,3},{2,0},{3,1},{4,6},{5,7},{6,4},{7,5},{8,10},{9,11},{10,... | collective-permute-start | bytes 1572872 | tf_op jit(solution)/shard_map/ppermute | solution.py:361
  46.3 1.1 %copy-start.3 = (bf16[1024,256]{1,0:T(8,128)(2,1)S(1)}, bf16[1024,256]{1,0:T(8,128)(2,1)}, u32[]{:S(2)}) copy-start(bf16[1024,256]{1,0:T(8,128)(2,1)} %copy-done.2) | copy-start | bytes 1572868
  47.5 12.1 %collective-permute-start.12 = (bf16[256,256]{1,0:T(8,128)(2,1)S(1)}, bf16[256,256]{1,0:T(8,128)(2,1)S(1)}, u32[]{:S(2)}, u32[]{:S(2)}) collective-permute-start(bf16[256,256]{1,0:T(8,128)(2,1)S(1)} %get-tuple-element.27), channel_id=1, source_target_pairs={{0,4},{1,5},{2,6},{3,7},{4,0},{5,1},{6,2},{7,3},{8,12},{9,13},{10,... | collective-permute-start | bytes 393224 | tf_op jit(solution)/shard_map/ppermute | solution.py:361
  51.1 12.5 %collective-permute-start.14 = (bf16[256,256]{1,0:T(8,128)(2,1)S(1)}, bf16[256,256]{1,0:T(8,128)(2,1)S(1)}, u32[]{:S(2)}, u32[]{:S(2)}) collective-permute-start(bf16[256,256]{1,0:T(8,128)(2,1)S(1)} %get-tuple-element.28), channel_id=1, source_target_pairs={{0,12},{1,13},{2,14},{3,15},{4,8},{5,9},{6,10},{7,11},{8,4},{9,5},... | collective-permute-start | bytes 393224 | tf_op jit(solution)/shard_map/ppermute | solution.py:361
  56.0 7.7 %collective-permute-start.13 = (bf16[256,256]{1,0:T(8,128)(2,1)S(1)}, bf16[256,256]{1,0:T(8,128)(2,1)S(1)}, u32[]{:S(2)}, u32[]{:S(2)}) collective-permute-start(bf16[256,256]{1,0:T(8,128)(2,1)S(1)} %get-tuple-element.29), channel_id=1, source_target_pairs={{0,8},{1,9},{2,10},{3,11},{4,12},{5,13},{6,14},{7,15},{8,0},{9,1},... | collective-permute-start | bytes 393224 | tf_op jit(solution)/shard_map/ppermute | solution.py:361
  56.1 8.3 %collective-permute-start.8 = (bf16[256,256]{1,0:T(8,128)(2,1)S(1)}, bf16[256,256]{1,0:T(8,128)(2,1)S(1)}, u32[]{:S(2)}, u32[]{:S(2)}) collective-permute-start(bf16[256,256]{1,0:T(8,128)(2,1)S(1)} %get-tuple-element.30), channel_id=1, source_target_pairs={{0,4},{1,5},{2,6},{3,7},{4,0},{5,1},{6,2},{7,3},{8,12},{9,13},{10,... | collective-permute-start | bytes 393224 | tf_op jit(solution)/shard_map/ppermute | solution.py:361
  57.0 8.9 %collective-permute-start.10 = (bf16[256,256]{1,0:T(8,128)(2,1)S(1)}, bf16[256,256]{1,0:T(8,128)(2,1)S(1)}, u32[]{:S(2)}, u32[]{:S(2)}) collective-permute-start(bf16[256,256]{1,0:T(8,128)(2,1)S(1)} %get-tuple-element.31), channel_id=1, source_target_pairs={{0,12},{1,13},{2,14},{3,15},{4,8},{5,9},{6,10},{7,11},{8,4},{9,5},... | collective-permute-start | bytes 393224 | tf_op jit(solution)/shard_map/ppermute | solution.py:361
  59.6 8.9 %collective-permute-start.9 = (bf16[256,256]{1,0:T(8,128)(2,1)S(1)}, bf16[256,256]{1,0:T(8,128)(2,1)S(1)}, u32[]{:S(2)}, u32[]{:S(2)}) collective-permute-start(bf16[256,256]{1,0:T(8,128)(2,1)S(1)} %get-tuple-element.32), channel_id=1, source_target_pairs={{0,8},{1,9},{2,10},{3,11},{4,12},{5,13},{6,14},{7,15},{8,0},{9,1},... | collective-permute-start | bytes 393224 | tf_op jit(solution)/shard_map/ppermute | solution.py:361
  63.7 7.4 %collective-permute-start.15 = (bf16[128,256]{1,0:T(8,128)(2,1)S(1)}, bf16[128,256]{1,0:T(8,128)(2,1)S(1)}, u32[]{:S(2)}, u32[]{:S(2)}) collective-permute-start(bf16[128,256]{1,0:T(8,128)(2,1)S(1)} %get-tuple-element.36), channel_id=1, source_target_pairs={{0,16},{1,17},{2,18},{3,19},{4,20},{5,21},{6,22},{7,23},{8,24},{9,... | collective-permute-start | bytes 196616 | tf_op jit(solution)/shard_map/ppermute | solution.py:361
  68.6 4.4 %collective-permute-start.16 = (bf16[128,256]{1,0:T(8,128)(2,1)S(1)}, bf16[128,256]{1,0:T(8,128)(2,1)S(1)}, u32[]{:S(2)}, u32[]{:S(2)}) collective-permute-start(bf16[128,256]{1,0:T(8,128)(2,1)S(1)} %slice.161), channel_id=1, source_target_pairs={{0,1},{1,0},{2,3},{3,2},{4,5},{5,4},{6,7},{7,6},{8,9},{9,8},{10,11... | collective-permute-start | bytes 196616 | tf_op jit(solution)/shard_map/ppermute | solution.py:361
  70.7 6.8 %collective-permute-start.17 = (bf16[128,256]{1,0:T(8,128)(2,1)S(1)}, bf16[128,256]{1,0:T(8,128)(2,1)S(1)}, u32[]{:S(2)}, u32[]{:S(2)}) collective-permute-start(bf16[128,256]{1,0:T(8,128)(2,1)S(1)} %get-tuple-element.35), channel_id=1, source_target_pairs={{0,17},{1,16},{2,19},{3,18},{4,21},{5,20},{6,23},{7,22},{8,25},{9,... | collective-permute-start | bytes 196616 | tf_op jit(solution)/shard_map/ppermute | solution.py:361

commit v6 on v5

--- a/solution.py
+++ b/solution.py
@@ -231,11 +231,6 @@
             weigh(i, places(0, many), allowed(many, first, turn, True))
             spread(i, places(0, many))
 
-        def body(n, carry):
-            spread(i, places(first + 4 * n - 4, 4))
-            weigh(i, places(first + 4 * n, 4), None)
-            return carry
-
         sweep(work[3 * local_blocks, local_blocks + i], far_step)
         row_total = jnp.sum(total[i], 0, keepdims=True)
         row_delta = jnp.sum(delta[i], 0, keepdims=True) / row_total
@@ -244,12 +239,26 @@
         first, quads = split(count)
         pl.when(first <= 2)(lambda: begin(2))
         pl.when(first > 2)(lambda: begin(4))
-
-        @pl.when(quads > 0)
+        start = first + 4 * (quads % 2)
+
+        @pl.when(quads % 2 == 1)
         def _():
             weigh(i, places(first, 4), None)
-            lax.fori_loop(1, quads, body, 0)
-            spread(i, places(first + 4 * quads - 4, 4))
+            spread(i, places(first, 4))
+
+        @pl.when(quads // 2 % 2 == 1)
+        def _():
+            weigh(i, places(start, 8), None)
+            spread(i, places(start, 8))
+
+        second = start + 8 * (quads // 2 % 2)
+
+        def body(n, carry):
+            weigh(i, places(second + 16 * n, 16), None)
+            spread(i, places(second + 16 * n, 16))
+            return carry
+
+        lax.fori_loop(0, quads // 4, body, 0)
 
         return carry
 
@@ -316,8 +325,8 @@
             pltpu.VMEM((rows, 2 * HEAD), BF16),
             pltpu.VMEM((local_blocks, 8, WIDE), F32),
             pltpu.VMEM((local_blocks, 8, WIDE), F32),
-            pltpu.VMEM((4 * BLOCK, WIDE), BF16),
-            pltpu.VMEM((4 * BLOCK, WIDE), BF16),
+            pltpu.VMEM((16 * BLOCK, WIDE), BF16),
+            pltpu.VMEM((16 * BLOCK, WIDE), BF16),
             pltpu.VMEM((rows, 2 * HEAD), F32),
             pltpu.SemaphoreType.DMA((6,)),
         ],

time: 77.4 us -> 79.3 us (1.025); the launches traced: 78.9 us -> 79.5 us
  starting transfers between devices: 34.1 us -> 21.1 us
  Pallas kernels: 21.5 us -> 30.1 us
  waiting for transfers between devices: 16.9 us -> 21.9 us
    ppermute x18, starting transfers between devices: 29.2 us -> 16.3 us  [swap(): return lax.ppermute(x, ('seq', 'kvh'), pairs)]
    ppermute x18, waiting for transfers between devices: 14.4 us -> 21.2 us  [swap(): return lax.ppermute(x, ('seq', 'kvh'), pairs)]
    pallas_call x1, Pallas kernels: 16.2 us -> 22.7 us  [attend(): pl.pallas_call(functools.partial(main_kernel, part_rows), in_specs=[SMEM]...]
    all_to_all x1, waiting for transfers between devices: 2.49 us -> 0.66 us  [exchange_near(): lax.all_to_all(x, ('seq', 'kvh'), 0, 0, axis_index_groups=near_groups)]
    pallas_call x1, Pallas kernels: 3.06 us -> 4.9 us  [near_sums(): pl.pallas_call(functools.partial(near_kernel, part_rows), in_specs=[SMEM]...]
  transfers between devices with their start and end apart: 19 -> 19, of which waited for: 8 -> 10; matrix products, arithmetic and copies ran while one was open for 4% -> 4% of each run, Pallas kernels for 7% -> 9%
where the time goes in v6:
time: 79.3 us; the launch traced here: 79.5 us
  Pallas kernels  30.1 us (38%)
  waiting for transfers between devices  21.9 us (28%)
  starting transfers between devices  21.1 us (27%)
  local copies, waits for them, and re-layouts  3.55 us (4%)
  other arithmetic  1.96 us (2%)
  between operations  0.95 us (1%)
    pallas_call x1, Pallas kernels, attend(): pl.pallas_call(functools.partial(main_kernel, part_rows), in_specs=[SMEM]...  22.7 us
    ppermute x18, waiting for transfers between devices, swap(): return lax.ppermute(x, ('seq', 'kvh'), pairs)  21.2 us
    ppermute x18, starting transfers between devices, swap(): return lax.ppermute(x, ('seq', 'kvh'), pairs)  16.3 us
    pallas_call x1, Pallas kernels, near_sums(): pl.pallas_call(functools.partial(near_kernel, part_rows), in_specs=[SMEM]...  4.9 us
    all_to_all x1, starting transfers between devices, exchange_near(): lax.all_to_all(x, ('seq', 'kvh'), 0, 0, axis_index_groups=near_groups)  4.76 us
    pallas_call x1, Pallas kernels, resolve(): pl.pallas_call(functools.partial(lists_kernel, part), in_specs=[SMEM] * 3...  2.44 us
  transfers between devices with their start and end apart: 19, of which 10 were waited for; matrix products, arithmetic and copies ran while one was open for 4% of the time, Pallas kernels for 9%

profile of v6, /device:TPU:0, one launch (start us, length us, event | category | flops | bytes accessed | tf_op | source)
XLA Modules:
  0.0 79.5 jit_solution(8775441148209457741)
XLA Ops:
  0.6 0.8 %fusion.13 = (bf16[128,128]{1,0:T(8,128)(2,1)S(1)}, bf16[128,128]{1,0:T(8,128)(2,1)S(1)}) fusion(bf16[128,256]{1,0:T(8,128)(2,1)} %param.8), kind=kLoop, calls=%fused_computation.49 | loop fusion | bytes 131072 | tf_op jit(solution)/shard_map/slice | solution.py:379
  1.5 0.0 copy-done.5
  1.6 3.0 %collective-permute-start.1 = (bf16[128,256]{1,0:T(8,128)(2,1)S(1)}, bf16[128,256]{1,0:T(8,128)(2,1)S(1)}, u32[]{:S(2)}, u32[]{:S(2)}) collective-permute-start(bf16[128,256]{1,0:T(8,128)(2,1)S(1)} %fusion.8), channel_id=1, source_target_pairs={{0,1},{1,0},{2,3},{3,2},{4,5},{5,4},{6,7},{7,6},{8,9},{9,8},{10,11... | collective-permute-start | bytes 196616 | tf_op jit(solution)/shard_map/ppermute | solution.py:370
  4.6 2.7 %collective-permute-start = (bf16[2,128,256]{2,1,0:T(8,128)(2,1)S(1)}, bf16[2,128,256]{2,1,0:T(8,128)(2,1)S(1)}, u32[]{:S(2)}, u32[]{:S(2)}) collective-permute-start(bf16[2,128,256]{2,1,0:T(8,128)(2,1)S(1)} %pad_maximum_fusion), channel_id=1, source_target_pairs={{0,16},{1,17},{2,18},{3,19},{4,20},{5,21},{6,22},{7,23},{8,24},{9,... | collective-permute-start | bytes 393224 | tf_op jit(solution)/shard_map/ppermute | solution.py:370
  7.3 0.0 collective-permute-done.1
  7.3 1.6 %collective-permute-start.2 = (bf16[256,256]{1,0:T(8,128)(2,1)S(1)}, bf16[256,256]{1,0:T(8,128)(2,1)S(1)}, u32[]{:S(2)}, u32[]{:S(2)}) collective-permute-start(bf16[256,256]{1,0:T(8,128)(2,1)S(1)} %pad_maximum_fusion.1), channel_id=1, source_target_pairs={{0,4},{1,5},{2,6},{3,7},{4,0},{5,1},{6,2},{7,3},{8,12},{9,13},{10,... | collective-permute-start | bytes 393224 | tf_op jit(solution)/shard_map/ppermute | solution.py:370
  8.9 2.4 %lists.1.work = s32[7,32]{1,0:T(8,128)} custom-call(s32[24,32]{1,0:T(8,128)} %bitcast.39, s32[32]{0:T(128)} %counts.1, s32[32]{0:T(128)} %spans.1), custom_call_target="tpu_custom_call" | custom-call | tf_op jit(solution)/shard_map/lists/pallas_call | solution.py:285
  11.4 1.5 %collective-permute-start.4 = (bf16[256,256]{1,0:T(8,128)(2,1)S(1)}, bf16[256,256]{1,0:T(8,128)(2,1)S(1)}, u32[]{:S(2)}, u32[]{:S(2)}) collective-permute-start(bf16[256,256]{1,0:T(8,128)(2,1)S(1)} %pad_maximum_fusion.1), channel_id=1, source_target_pairs={{0,12},{1,13},{2,14},{3,15},{4,8},{5,9},{6,10},{7,11},{8,4},{9,5},... | collective-permute-start | bytes 393224 | tf_op jit(solution)/shard_map/ppermute | solution.py:370
  12.9 0.2 collective-permute-start.3
  13.1 0.3 collective-permute-done
  13.4 0.8 %broadcast_in_dim.2 = bf16[4,2,128,256]{3,2,1,0:T(8,128)(2,1)} broadcast(bf16[2,128,256]{2,1,0:T(8,128)(2,1)S(1)} %collective-permute-done), dimensions={1,2,3} | broadcast | bytes 655360 | tf_op jit(solution)/shard_map/broadcast_in_dim | solution.py:389
  14.2 4.8 %all-to-all-start = ((bf16[8,128,256]{2,1,0:T(8,128)(2,1)}), bf16[8,128,256]{2,1,0:T(8,128)(2,1)S(1)}, u32[]{:S(2)}, u32[]{:S(2)}) async-start(bf16[8,128,256]{2,1,0:T(8,128)(2,1)} %bitcast.5), calls=%async_computation | async-start | bytes 1048576 | tf_op jit(solution)/shard_map/all_to_all | solution.py:374
  19.0 0.0 collective-permute-done.2
  19.0 0.0 copy-start.4
  19.1 0.1 collective-permute-start.5
  19.2 1.9 %collective-permute-done.5.pair_any.refs_1_ = bf16[1024,256]{1,0:T(8,128)(2,1)S(1)} collective-permute-done((bf16[1024,256]{1,0:T(8,128)(2,1)S(1)}, bf16[1024,256]{1,0:T(8,128)(2,1)S(1)}, u32[]{:S(2)}, u32[]{:S(2)}) %collective-permute-start.5) | collective-permute-done | bytes 524320 | tf_op jit(solution)/shard_map/ppermute | solution.py:370
  21.1 4.9 %near.1 = (f32[2,8,1024]{2,1,0:T(8,128)S(1)}, f32[2,8,1024]{2,1,0:T(8,128)S(1)}) custom-call(s32[7,32]{1,0:T(8,128)S(1)} %copy-done.4, bf16[256,1024]{1,0:T(8,128)(2,1)S(1)} %copy-done, bf16[256,1024]{1,0:T(8,128)(2,1)S(1)} %copy-done.1, bf16[1024,256]{1,0:T(8,128)(2,1)S(1)} %constant_dynamic-update-slice_fusion.near_any.refs_0_, ...), custom_call_target="tpu_custom_call" | custom-call | flops 1048576 | bytes 1024 | tf_op jit(solution)/shard_map/near/pallas_call | solution.py:297
  26.0 0.7 all-to-all-done
  26.6 1.9 %collective-permute-done.6.refs_3_ = bf16[1024,256]{1,0:T(8,128)(2,1)S(1)} collective-permute-done((bf16[1024,256]{1,0:T(8,128)(2,1)S(1)}, bf16[1024,256]{1,0:T(8,128)(2,1)S(1)}, u32[]{:S(2)}, u32[]{:S(2)}) %collective-permute-start.6) | collective-permute-done | bytes 524320 | tf_op jit(solution)/shard_map/ppermute | solution.py:370
  28.5 22.7 %attend.1 = (f32[2,128,1024]{2,1,0:T(8,128)S(1)}, bf16[1024,256]{1,0:T(8,128)(2,1)S(1)}, bf16[1024,256]{1,0:T(8,128)(2,1)}, bf16[1024,256]{1,0:T(8,128)(2,1)S(1)}, bf16[1024,256]{1,0:T(8,128)(2,1)}) custom-call(s32[7,32]{1,0:T(8,128)S(1)} %copy-done.4, bf16[256,1024]{1,0:T(8,128)(2,1)S(1)} %copy-done, bf16[256,1024]{1,0:T(8,128)(2,1)S(1)} %copy-done.1, ...), custom_call_target="tpu_custom_call" | custom-call | tf_op jit(solution)/shard_map/attend/pallas_call | solution.py:316
  51.3 0.1 collective-permute-start.11
  51.4 0.5 collective-permute-start.7
  51.9 0.1 multiply_convert_fusion
  52.0 0.1 copy-done.2
  52.1 0.1 copy.11
  52.2 0.5 copy.10
  52.7 0.9 %copy.14 = bf16[32,8,8,128]{3,1,2,0:T(8,128)(2,1)} copy(bf16[32,8,8,128]{3,2,1,0:T(8,128)(2,1)S(1)} %bitcast.37) | data formatting | bytes 1048576
  53.6 0.2 copy-done.3
  53.8 0.1 add_convert_fusion.3
  53.9 0.1 collective-permute-start.12
  54.0 0.1 collective-permute-start.14
  54.1 3.4 %collective-permute-start.13 = (bf16[256,256]{1,0:T(8,128)(2,1)S(1)}, bf16[256,256]{1,0:T(8,128)(2,1)S(1)}, u32[]{:S(2)}, u32[]{:S(2)}) collective-permute-start(bf16[256,256]{1,0:T(8,128)(2,1)S(1)} %get-tuple-element.29), channel_id=1, source_target_pairs={{0,8},{1,9},{2,10},{3,11},{4,12},{5,13},{6,14},{7,15},{8,0},{9,1},... | collective-permute-start | bytes 393224 | tf_op jit(solution)/shard_map/ppermute | solution.py:370
  57.5 0.1 add_convert_fusion.6
  57.5 0.1 collective-permute-start.8
  57.7 1.4 %collective-permute-start.10 = (bf16[256,256]{1,0:T(8,128)(2,1)S(1)}, bf16[256,256]{1,0:T(8,128)(2,1)S(1)}, u32[]{:S(2)}, u32[]{:S(2)}) collective-permute-start(bf16[256,256]{1,0:T(8,128)(2,1)S(1)} %get-tuple-element.31), channel_id=1, source_target_pairs={{0,12},{1,13},{2,14},{3,15},{4,8},{5,9},{6,10},{7,11},{8,4},{9,5},... | collective-permute-start | bytes 393224 | tf_op jit(solution)/shard_map/ppermute | solution.py:370
  59.1 4.9 %collective-permute-done.12 = bf16[256,256]{1,0:T(8,128)(2,1)S(1)} collective-permute-done((bf16[256,256]{1,0:T(8,128)(2,1)S(1)}, bf16[256,256]{1,0:T(8,128)(2,1)S(1)}, u32[]{:S(2)}, u32[]{:S(2)}) %collective-permute-start.12) | collective-permute-done | bytes 131104 | tf_op jit(solution)/shard_map/ppermute | solution.py:370
  64.0 0.6 collective-permute-done.13
  64.6 0.1 add_convert_fusion
  64.7 0.1 collective-permute-start.15
  64.8 3.0 %collective-permute-done.8 = bf16[256,256]{1,0:T(8,128)(2,1)S(1)} collective-permute-done((bf16[256,256]{1,0:T(8,128)(2,1)S(1)}, bf16[256,256]{1,0:T(8,128)(2,1)S(1)}, u32[]{:S(2)}, u32[]{:S(2)}) %collective-permute-start.8) | collective-permute-done | bytes 131104 | tf_op jit(solution)/shard_map/ppermute | solution.py:370
  67.8 2.6 %collective-permute-done.9 = bf16[256,256]{1,0:T(8,128)(2,1)S(1)} collective-permute-done((bf16[256,256]{1,0:T(8,128)(2,1)S(1)}, bf16[256,256]{1,0:T(8,128)(2,1)S(1)}, u32[]{:S(2)}, u32[]{:S(2)}) %collective-permute-start.9) | collective-permute-done | bytes 131104 | tf_op jit(solution)/shard_map/ppermute | solution.py:370
  70.4 0.1 convert_add_fusion
  70.5 1.5 %collective-permute-start.16 = (bf16[128,256]{1,0:T(8,128)(2,1)S(1)}, bf16[128,256]{1,0:T(8,128)(2,1)S(1)}, u32[]{:S(2)}, u32[]{:S(2)}) collective-permute-start(bf16[128,256]{1,0:T(8,128)(2,1)S(1)} %slice.161), channel_id=1, source_target_pairs={{0,1},{1,0},{2,3},{3,2},{4,5},{5,4},{6,7},{7,6},{8,9},{9,8},{10,11... | collective-permute-start | bytes 196616 | tf_op jit(solution)/shard_map/ppermute | solution.py:370
  72.0 3.5 %collective-permute-done.16 = bf16[128,256]{1,0:T(8,128)(2,1)S(1)} collective-permute-done((bf16[128,256]{1,0:T(8,128)(2,1)S(1)}, bf16[128,256]{1,0:T(8,128)(2,1)S(1)}, u32[]{:S(2)}, u32[]{:S(2)}) %collective-permute-start.16) | collective-permute-done | bytes 65568 | tf_op jit(solution)/shard_map/ppermute | solution.py:370
  75.5 2.5 %collective-permute-done.17 = bf16[128,256]{1,0:T(8,128)(2,1)S(1)} collective-permute-done((bf16[128,256]{1,0:T(8,128)(2,1)S(1)}, bf16[128,256]{1,0:T(8,128)(2,1)S(1)}, u32[]{:S(2)}, u32[]{:S(2)}) %collective-permute-start.17) | collective-permute-done | bytes 65568 | tf_op jit(solution)/shard_map/ppermute | solution.py:370
  78.1 0.1 fusion.3
  78.2 0.6 pad_maximum_fusion.2
  78.9 0.6 pad_maximum_fusion.3
  (37 shorter events, 0.3 us)
Async XLA Ops:
  0.6 0.8 %copy-start.5 = (bf16[128,256]{1,0:T(8,128)(2,1)S(1)}, bf16[128,256]{1,0:T(8,128)(2,1)}, u32[]{:S(2)}) copy-start(bf16[128,256]{1,0:T(8,128)(2,1)} %param.9) | copy-start | bytes 196612
  1.6 5.7 %collective-permute-start.1 = (bf16[128,256]{1,0:T(8,128)(2,1)S(1)}, bf16[128,256]{1,0:T(8,128)(2,1)S(1)}, u32[]{:S(2)}, u32[]{:S(2)}) collective-permute-start(bf16[128,256]{1,0:T(8,128)(2,1)S(1)} %fusion.8), channel_id=1, source_target_pairs={{0,1},{1,0},{2,3},{3,2},{4,5},{5,4},{6,7},{7,6},{8,9},{9,8},{10,11... | collective-permute-start | bytes 196616 | tf_op jit(solution)/shard_map/ppermute | solution.py:370
  4.6 8.8 %collective-permute-start = (bf16[2,128,256]{2,1,0:T(8,128)(2,1)S(1)}, bf16[2,128,256]{2,1,0:T(8,128)(2,1)S(1)}, u32[]{:S(2)}, u32[]{:S(2)}) collective-permute-start(bf16[2,128,256]{2,1,0:T(8,128)(2,1)S(1)} %pad_maximum_fusion), channel_id=1, source_target_pairs={{0,16},{1,17},{2,18},{3,19},{4,20},{5,21},{6,22},{7,23},{8,24},{9,... | collective-permute-start | bytes 393224 | tf_op jit(solution)/shard_map/ppermute | solution.py:370
  7.3 11.7 %collective-permute-start.2 = (bf16[256,256]{1,0:T(8,128)(2,1)S(1)}, bf16[256,256]{1,0:T(8,128)(2,1)S(1)}, u32[]{:S(2)}, u32[]{:S(2)}) collective-permute-start(bf16[256,256]{1,0:T(8,128)(2,1)S(1)} %pad_maximum_fusion.1), channel_id=1, source_target_pairs={{0,4},{1,5},{2,6},{3,7},{4,0},{5,1},{6,2},{7,3},{8,12},{9,13},{10,... | collective-permute-start | bytes 393224 | tf_op jit(solution)/shard_map/ppermute | solution.py:370
  11.4 7.7 %collective-permute-start.4 = (bf16[256,256]{1,0:T(8,128)(2,1)S(1)}, bf16[256,256]{1,0:T(8,128)(2,1)S(1)}, u32[]{:S(2)}, u32[]{:S(2)}) collective-permute-start(bf16[256,256]{1,0:T(8,128)(2,1)S(1)} %pad_maximum_fusion.1), channel_id=1, source_target_pairs={{0,12},{1,13},{2,14},{3,15},{4,8},{5,9},{6,10},{7,11},{8,4},{9,5},... | collective-permute-start | bytes 393224 | tf_op jit(solution)/shard_map/ppermute | solution.py:370
  12.9 6.1 %collective-permute-start.3 = (bf16[256,256]{1,0:T(8,128)(2,1)S(1)}, bf16[256,256]{1,0:T(8,128)(2,1)S(1)}, u32[]{:S(2)}, u32[]{:S(2)}) collective-permute-start(bf16[256,256]{1,0:T(8,128)(2,1)S(1)} %pad_maximum_fusion.1), channel_id=1, source_target_pairs={{0,8},{1,9},{2,10},{3,11},{4,12},{5,13},{6,14},{7,15},{8,0},{9,1},... | collective-permute-start | bytes 393224 | tf_op jit(solution)/shard_map/ppermute | solution.py:370
  14.2 6.9 %copy-start.1 = (bf16[256,1024]{1,0:T(8,128)(2,1)S(1)}, bf16[256,1024]{1,0:T(8,128)(2,1)}, u32[]{:S(2)}) copy-start(bf16[256,1024]{1,0:T(8,128)(2,1)} %do_any.3) | copy-start | bytes 1572868
  14.2 12.4 %all-to-all-start = ((bf16[8,128,256]{2,1,0:T(8,128)(2,1)}), bf16[8,128,256]{2,1,0:T(8,128)(2,1)S(1)}, u32[]{:S(2)}, u32[]{:S(2)}) async-start(bf16[8,128,256]{2,1,0:T(8,128)(2,1)} %bitcast.5), calls=%async_computation | async-start | bytes 1048576 | tf_op jit(solution)/shard_map/all_to_all | solution.py:374
  19.0 2.1 %copy-start = (bf16[256,1024]{1,0:T(8,128)(2,1)S(1)}, bf16[256,1024]{1,0:T(8,128)(2,1)}, u32[]{:S(2)}) copy-start(bf16[256,1024]{1,0:T(8,128)(2,1)} %q_any.3) | copy-start | bytes 1572868
  19.0 2.0 %copy-start.4 = (s32[7,32]{1,0:T(8,128)S(1)}, s32[7,32]{1,0:T(8,128)}, u32[]{:S(2)}) copy-start(s32[7,32]{1,0:T(8,128)} %lists.1.work) | copy-start | bytes 2692
  19.1 2.0 %collective-permute-start.5 = (bf16[1024,256]{1,0:T(8,128)(2,1)S(1)}, bf16[1024,256]{1,0:T(8,128)(2,1)S(1)}, u32[]{:S(2)}, u32[]{:S(2)}) collective-permute-start(bf16[1024,256]{1,0:T(8,128)(2,1)S(1)} %constant_dynamic-update-slice_fusion.near_any.refs_0_), channel_id=1, source_target_pairs={{0,2},{1,3},{2,0},{3,1},{4,6},{5,7},{6,4},{7,5},{8,10},{9,11},{10,... | collective-permute-start | bytes 1572872 | tf_op jit(solution)/shard_map/ppermute | solution.py:370
  26.6 1.9 %collective-permute-start.6 = (bf16[1024,256]{1,0:T(8,128)(2,1)S(1)}, bf16[1024,256]{1,0:T(8,128)(2,1)S(1)}, u32[]{:S(2)}, u32[]{:S(2)}) collective-permute-start(bf16[1024,256]{1,0:T(8,128)(2,1)S(1)} %bitcast.33), channel_id=1, source_target_pairs={{0,2},{1,3},{2,0},{3,1},{4,6},{5,7},{6,4},{7,5},{8,10},{9,11},{10,... | collective-permute-start | bytes 1572872 | tf_op jit(solution)/shard_map/ppermute | solution.py:370
  51.3 0.8 copy-start.2
  51.3 2.3 %collective-permute-start.11 = (bf16[1024,256]{1,0:T(8,128)(2,1)}, bf16[1024,256]{1,0:T(8,128)(2,1)S(1)}, u32[]{:S(2)}, u32[]{:S(2)}) collective-permute-start(bf16[1024,256]{1,0:T(8,128)(2,1)} %get-tuple-element.24), channel_id=1, source_target_pairs={{0,2},{1,3},{2,0},{3,1},{4,6},{5,7},{6,4},{7,5},{8,10},{9,11},{10,... | collective-permute-start | bytes 1572872 | tf_op jit(solution)/shard_map/ppermute | solution.py:370
  51.4 6.1 %collective-permute-start.7 = (bf16[1024,256]{1,0:T(8,128)(2,1)}, bf16[1024,256]{1,0:T(8,128)(2,1)S(1)}, u32[]{:S(2)}, u32[]{:S(2)}) collective-permute-start(bf16[1024,256]{1,0:T(8,128)(2,1)} %get-tuple-element.22), channel_id=1, source_target_pairs={{0,2},{1,3},{2,0},{3,1},{4,6},{5,7},{6,4},{7,5},{8,10},{9,11},{10,... | collective-permute-start | bytes 1572872 | tf_op jit(solution)/shard_map/ppermute | solution.py:370
  52.7 1.1 %copy-start.3 = (bf16[1024,256]{1,0:T(8,128)(2,1)S(1)}, bf16[1024,256]{1,0:T(8,128)(2,1)}, u32[]{:S(2)}) copy-start(bf16[1024,256]{1,0:T(8,128)(2,1)} %copy-done.2) | copy-start | bytes 1572868
  53.9 10.1 %collective-permute-start.12 = (bf16[256,256]{1,0:T(8,128)(2,1)S(1)}, bf16[256,256]{1,0:T(8,128)(2,1)S(1)}, u32[]{:S(2)}, u32[]{:S(2)}) collective-permute-start(bf16[256,256]{1,0:T(8,128)(2,1)S(1)} %get-tuple-element.27), channel_id=1, source_target_pairs={{0,4},{1,5},{2,6},{3,7},{4,0},{5,1},{6,2},{7,3},{8,12},{9,13},{10,... | collective-permute-start | bytes 393224 | tf_op jit(solution)/shard_map/ppermute | solution.py:370
  54.0 10.1 %collective-permute-start.14 = (bf16[256,256]{1,0:T(8,128)(2,1)S(1)}, bf16[256,256]{1,0:T(8,128)(2,1)S(1)}, u32[]{:S(2)}, u32[]{:S(2)}) collective-permute-start(bf16[256,256]{1,0:T(8,128)(2,1)S(1)} %get-tuple-element.28), channel_id=1, source_target_pairs={{0,12},{1,13},{2,14},{3,15},{4,8},{5,9},{6,10},{7,11},{8,4},{9,5},... | collective-permute-start | bytes 393224 | tf_op jit(solution)/shard_map/ppermute | solution.py:370
  54.1 10.6 %collective-permute-start.13 = (bf16[256,256]{1,0:T(8,128)(2,1)S(1)}, bf16[256,256]{1,0:T(8,128)(2,1)S(1)}, u32[]{:S(2)}, u32[]{:S(2)}) collective-permute-start(bf16[256,256]{1,0:T(8,128)(2,1)S(1)} %get-tuple-element.29), channel_id=1, source_target_pairs={{0,8},{1,9},{2,10},{3,11},{4,12},{5,13},{6,14},{7,15},{8,0},{9,1},... | collective-permute-start | bytes 393224 | tf_op jit(solution)/shard_map/ppermute | solution.py:370
  57.5 10.2 %collective-permute-start.8 = (bf16[256,256]{1,0:T(8,128)(2,1)S(1)}, bf16[256,256]{1,0:T(8,128)(2,1)S(1)}, u32[]{:S(2)}, u32[]{:S(2)}) collective-permute-start(bf16[256,256]{1,0:T(8,128)(2,1)S(1)} %get-tuple-element.30), channel_id=1, source_target_pairs={{0,4},{1,5},{2,6},{3,7},{4,0},{5,1},{6,2},{7,3},{8,12},{9,13},{10,... | collective-permute-start | bytes 393224 | tf_op jit(solution)/shard_map/ppermute | solution.py:370
  57.7 10.1 %collective-permute-start.10 = (bf16[256,256]{1,0:T(8,128)(2,1)S(1)}, bf16[256,256]{1,0:T(8,128)(2,1)S(1)}, u32[]{:S(2)}, u32[]{:S(2)}) collective-permute-start(bf16[256,256]{1,0:T(8,128)(2,1)S(1)} %get-tuple-element.31), channel_id=1, source_target_pairs={{0,12},{1,13},{2,14},{3,15},{4,8},{5,9},{6,10},{7,11},{8,4},{9,5},... | collective-permute-start | bytes 393224 | tf_op jit(solution)/shard_map/ppermute | solution.py:370
  64.0 6.4 %collective-permute-start.9 = (bf16[256,256]{1,0:T(8,128)(2,1)S(1)}, bf16[256,256]{1,0:T(8,128)(2,1)S(1)}, u32[]{:S(2)}, u32[]{:S(2)}) collective-permute-start(bf16[256,256]{1,0:T(8,128)(2,1)S(1)} %get-tuple-element.32), channel_id=1, source_target_pairs={{0,8},{1,9},{2,10},{3,11},{4,12},{5,13},{6,14},{7,15},{8,0},{9,1},... | collective-permute-start | bytes 393224 | tf_op jit(solution)/shard_map/ppermute | solution.py:370
  64.7 7.3 %collective-permute-start.15 = (bf16[128,256]{1,0:T(8,128)(2,1)S(1)}, bf16[128,256]{1,0:T(8,128)(2,1)S(1)}, u32[]{:S(2)}, u32[]{:S(2)}) collective-permute-start(bf16[128,256]{1,0:T(8,128)(2,1)S(1)} %get-tuple-element.36), channel_id=1, source_target_pairs={{0,16},{1,17},{2,18},{3,19},{4,20},{5,21},{6,22},{7,23},{8,24},{9,... | collective-permute-start | bytes 196616 | tf_op jit(solution)/shard_map/ppermute | solution.py:370
  70.5 5.0 %collective-permute-start.16 = (bf16[128,256]{1,0:T(8,128)(2,1)S(1)}, bf16[128,256]{1,0:T(8,128)(2,1)S(1)}, u32[]{:S(2)}, u32[]{:S(2)}) collective-permute-start(bf16[128,256]{1,0:T(8,128)(2,1)S(1)} %slice.161), channel_id=1, source_target_pairs={{0,1},{1,0},{2,3},{3,2},{4,5},{5,4},{6,7},{7,6},{8,9},{9,8},{10,11... | collective-permute-start | bytes 196616 | tf_op jit(solution)/shard_map/ppermute | solution.py:370
  72.0 6.1 %collective-permute-start.17 = (bf16[128,256]{1,0:T(8,128)(2,1)S(1)}, bf16[128,256]{1,0:T(8,128)(2,1)S(1)}, u32[]{:S(2)}, u32[]{:S(2)}) collective-permute-start(bf16[128,256]{1,0:T(8,128)(2,1)S(1)} %get-tuple-element.35), channel_id=1, source_target_pairs={{0,17},{1,16},{2,19},{3,18},{4,21},{5,20},{6,23},{7,22},{8,25},{9,... | collective-permute-start | bytes 196616 | tf_op jit(solution)/shard_map/ppermute | solution.py:370

commit v7 on v6

--- a/solution.py
+++ b/solution.py
@@ -394,8 +394,6 @@
     total, far_part = lax.optimization_barrier((total, far_part))
     far_pair = swap(far_part, 1, 0)
     dqt, *partials = attend(*common, total, delta, [near_part, near_pair, far_part, far_pair])
-    dq = jnp.transpose(dqt.reshape(-1, HEAD, GROUP, BLOCK), (0, 3, 2, 1)) * SCALE
-    grad_queries = dq.reshape(queries.shape).astype(BF16)
 
     def chip_rows(kept, received, m):
         rows = slice(m * span_rows, (m + 1) * span_rows)
@@ -416,6 +414,9 @@
 
     far_received, near_received = swap(partials[3], 1, 0), swap(partials[1], 1, 0)
     far_others = sent_to_middles(partials[2], far_received)
+    dqt, *far_others = lax.optimization_barrier((dqt, *far_others))
+    dq = jnp.transpose(dqt.reshape(-1, HEAD, GROUP, BLOCK), (0, 3, 2, 1)) * SCALE
+    grad_queries = dq.reshape(queries.shape).astype(BF16)
     near_others = sent_to_middles(partials[0], near_received)
     far_sums = to_owners(added(partials[2], far_received, far_others), half)
     near_grads = to_owners(added(partials[0], near_received, near_others), 0)

time: 79.3 us -> 75.7 us (0.955); the launches traced: 79.5 us -> 75 us
  Pallas kernels: 30.1 us -> 13.6 us
  starting transfers between devices: 21.1 us -> 35 us
  waiting for transfers between devices: 21.9 us -> 18.4 us
  other arithmetic: 1.96 us -> 2.87 us
    pallas_call x1, Pallas kernels: 22.7 us -> 8.72 us  [attend(): pl.pallas_call(functools.partial(main_kernel, part_rows), in_specs=[SMEM]...]
    ppermute x18, starting transfers between devices: 16.3 us -> 30.2 us  [swap(): return lax.ppermute(x, ('seq', 'kvh'), pairs)]
    ppermute x18, waiting for transfers between devices: 21.2 us -> 15.6 us  [swap(): return lax.ppermute(x, ('seq', 'kvh'), pairs)]
    all_to_all x1, waiting for transfers between devices: 0.66 us -> 2.76 us  [exchange_near(): lax.all_to_all(x, ('seq', 'kvh'), 0, 0, axis_index_groups=near_groups)]
    pallas_call x1, Pallas kernels: 4.9 us -> 2.8 us  [near_sums(): pl.pallas_call(functools.partial(near_kernel, part_rows), in_specs=[SMEM]...]
    another operation x3, other arithmetic: 0.11 us -> 1.02 us
    unnamed x17 -> x27, local copies, waits for them, and re-layouts: 1.36 us -> 1.96 us
  transfers between devices with their start and end apart: 19 -> 19, of which waited for: 10 -> 8; matrix products, arithmetic and copies ran while one was open for 4% -> 5% of each run, Pallas kernels for 9% -> 7%
where the time goes in v7:
time: 75.7 us; the launch traced here: 75 us
  starting transfers between devices  35 us (46%)
  waiting for transfers between devices  18.4 us (24%)
  Pallas kernels  13.6 us (18%)
  local copies, waits for them, and re-layouts  4.15 us (5%)
  other arithmetic  2.87 us (4%)
  between operations  1.01 us (1%)
    ppermute x18, starting transfers between devices, swap(): return lax.ppermute(x, ('seq', 'kvh'), pairs)  30.2 us
    ppermute x18, waiting for transfers between devices, swap(): return lax.ppermute(x, ('seq', 'kvh'), pairs)  15.6 us
    pallas_call x1, Pallas kernels, attend(): pl.pallas_call(functools.partial(main_kernel, part_rows), in_specs=[SMEM]...  8.72 us
    all_to_all x1, starting transfers between devices, exchange_near(): lax.all_to_all(x, ('seq', 'kvh'), 0, 0, axis_index_groups=near_groups)  4.74 us
    pallas_call x1, Pallas kernels, near_sums(): pl.pallas_call(functools.partial(near_kernel, part_rows), in_specs=[SMEM]...  2.8 us
    all_to_all x1, waiting for transfers between devices, exchange_near(): lax.all_to_all(x, ('seq', 'kvh'), 0, 0, axis_index_groups=near_groups)  2.76 us
    pallas_call x1, Pallas kernels, resolve(): pl.pallas_call(functools.partial(lists_kernel, part), in_specs=[SMEM] * 3...  2.09 us
    unnamed x27, local copies, waits for them, and re-layouts  1.96 us
  transfers between devices with their start and end apart: 19, of which 8 were waited for; matrix products, arithmetic and copies ran while one was open for 5% of the time, Pallas kernels for 7%

profile of v7, /device:TPU:0, one launch (start us, length us, event | category | flops | bytes accessed | tf_op | source)
XLA Modules:
  0.0 75.0 jit_solution(2437966706963790659)
XLA Ops:
  0.6 0.8 %fusion.13 = (bf16[128,128]{1,0:T(8,128)(2,1)S(1)}, bf16[128,128]{1,0:T(8,128)(2,1)S(1)}) fusion(bf16[128,256]{1,0:T(8,128)(2,1)} %param.8), kind=kLoop, calls=%fused_computation.49 | loop fusion | bytes 131072 | tf_op jit(solution)/shard_map/slice | solution.py:379
  1.5 0.0 copy-done.10
  1.6 3.0 %collective-permute-start.1 = (bf16[128,256]{1,0:T(8,128)(2,1)S(1)}, bf16[128,256]{1,0:T(8,128)(2,1)S(1)}, u32[]{:S(2)}, u32[]{:S(2)}) collective-permute-start(bf16[128,256]{1,0:T(8,128)(2,1)S(1)} %fusion.8), channel_id=1, source_target_pairs={{0,1},{1,0},{2,3},{3,2},{4,5},{5,4},{6,7},{7,6},{8,9},{9,8},{10,11... | collective-permute-start | bytes 196616 | tf_op jit(solution)/shard_map/ppermute | solution.py:370
  4.6 2.7 %collective-permute-start = (bf16[2,128,256]{2,1,0:T(8,128)(2,1)S(1)}, bf16[2,128,256]{2,1,0:T(8,128)(2,1)S(1)}, u32[]{:S(2)}, u32[]{:S(2)}) collective-permute-start(bf16[2,128,256]{2,1,0:T(8,128)(2,1)S(1)} %pad_maximum_fusion), channel_id=1, source_target_pairs={{0,16},{1,17},{2,18},{3,19},{4,20},{5,21},{6,22},{7,23},{8,24},{9,... | collective-permute-start | bytes 393224 | tf_op jit(solution)/shard_map/ppermute | solution.py:370
  7.3 0.0 collective-permute-done.1
  7.3 1.6 %collective-permute-start.2 = (bf16[256,256]{1,0:T(8,128)(2,1)S(1)}, bf16[256,256]{1,0:T(8,128)(2,1)S(1)}, u32[]{:S(2)}, u32[]{:S(2)}) collective-permute-start(bf16[256,256]{1,0:T(8,128)(2,1)S(1)} %pad_maximum_fusion.1), channel_id=1, source_target_pairs={{0,4},{1,5},{2,6},{3,7},{4,0},{5,1},{6,2},{7,3},{8,12},{9,13},{10,... | collective-permute-start | bytes 393224 | tf_op jit(solution)/shard_map/ppermute | solution.py:370
  8.9 2.1 %lists.1.work = s32[7,32]{1,0:T(8,128)} custom-call(s32[24,32]{1,0:T(8,128)} %bitcast.39, s32[32]{0:T(128)} %counts.1, s32[32]{0:T(128)} %spans.1), custom_call_target="tpu_custom_call" | custom-call | tf_op jit(solution)/shard_map/lists/pallas_call | solution.py:285
  11.0 1.5 %collective-permute-start.4 = (bf16[256,256]{1,0:T(8,128)(2,1)S(1)}, bf16[256,256]{1,0:T(8,128)(2,1)S(1)}, u32[]{:S(2)}, u32[]{:S(2)}) collective-permute-start(bf16[256,256]{1,0:T(8,128)(2,1)S(1)} %pad_maximum_fusion.1), channel_id=1, source_target_pairs={{0,12},{1,13},{2,14},{3,15},{4,8},{5,9},{6,10},{7,11},{8,4},{9,5},... | collective-permute-start | bytes 393224 | tf_op jit(solution)/shard_map/ppermute | solution.py:370
  12.5 0.6 collective-permute-start.3
  13.2 0.2 collective-permute-done
  13.4 0.8 %broadcast_in_dim.2 = bf16[4,2,128,256]{3,2,1,0:T(8,128)(2,1)} broadcast(bf16[2,128,256]{2,1,0:T(8,128)(2,1)S(1)} %collective-permute-done), dimensions={1,2,3} | broadcast | bytes 655360 | tf_op jit(solution)/shard_map/broadcast_in_dim | solution.py:389
  14.2 4.7 %all-to-all-start = ((bf16[8,128,256]{2,1,0:T(8,128)(2,1)}), bf16[8,128,256]{2,1,0:T(8,128)(2,1)S(1)}, u32[]{:S(2)}, u32[]{:S(2)}) async-start(bf16[8,128,256]{2,1,0:T(8,128)(2,1)} %bitcast.5), calls=%async_computation | async-start | bytes 1048576 | tf_op jit(solution)/shard_map/all_to_all | solution.py:374
  19.0 0.0 collective-permute-done.2
  19.0 0.0 collective-permute-done.3
  19.0 0.0 copy-start.3
  19.1 0.1 collective-permute-start.5
  19.1 1.9 %collective-permute-done.5.pair_any.refs_1_ = bf16[1024,256]{1,0:T(8,128)(2,1)S(1)} collective-permute-done((bf16[1024,256]{1,0:T(8,128)(2,1)S(1)}, bf16[1024,256]{1,0:T(8,128)(2,1)S(1)}, u32[]{:S(2)}, u32[]{:S(2)}) %collective-permute-start.5) | collective-permute-done | bytes 524320 | tf_op jit(solution)/shard_map/ppermute | solution.py:370
  21.0 2.8 %near.1 = (f32[2,8,1024]{2,1,0:T(8,128)S(1)}, f32[2,8,1024]{2,1,0:T(8,128)S(1)}) custom-call(s32[7,32]{1,0:T(8,128)S(1)} %copy-done.3, bf16[256,1024]{1,0:T(8,128)(2,1)S(1)} %copy-done, bf16[256,1024]{1,0:T(8,128)(2,1)S(1)} %copy-done.1, bf16[1024,256]{1,0:T(8,128)(2,1)S(1)} %constant_dynamic-update-slice_fusion.near_any.refs_0_, ...), custom_call_target="tpu_custom_call" | custom-call | flops 1048576 | bytes 1024 | tf_op jit(solution)/shard_map/near/pallas_call | solution.py:297
  23.9 2.8 %all-to-all-done = bf16[8,128,256]{2,1,0:T(8,128)(2,1)S(1)} async-done(((bf16[8,128,256]{2,1,0:T(8,128)(2,1)}), bf16[8,128,256]{2,1,0:T(8,128)(2,1)S(1)}, u32[]{:S(2)}, u32[]{:S(2)}) %all-to-all-start) | async-done | bytes 524320 | tf_op jit(solution)/shard_map/all_to_all | solution.py:374
  26.6 1.9 %collective-permute-done.6.refs_3_ = bf16[1024,256]{1,0:T(8,128)(2,1)S(1)} collective-permute-done((bf16[1024,256]{1,0:T(8,128)(2,1)S(1)}, bf16[1024,256]{1,0:T(8,128)(2,1)S(1)}, u32[]{:S(2)}, u32[]{:S(2)}) %collective-permute-start.6) | collective-permute-done | bytes 524320 | tf_op jit(solution)/shard_map/ppermute | solution.py:370
  28.5 8.7 %attend.1 = (f32[2,128,1024]{2,1,0:T(8,128)S(1)}, bf16[1024,256]{1,0:T(8,128)(2,1)S(1)}, bf16[1024,256]{1,0:T(8,128)(2,1)S(1)}, bf16[1024,256]{1,0:T(8,128)(2,1)S(1)}, bf16[1024,256]{1,0:T(8,128)(2,1)S(1)}) custom-call(s32[7,32]{1,0:T(8,128)S(1)} %copy-done.3, bf16[256,1024]{1,0:T(8,128)(2,1)S(1)} %copy-done, bf16[256,1024]{1,0:T(8,128)(2,1)S(1)} %copy-done.1, ...), custom_call_target="tpu_custom_call" | custom-call | tf_op jit(solution)/shard_map/attend/pallas_call | solution.py:316
  37.3 9.1 %collective-permute-start.7 = (bf16[1024,256]{1,0:T(8,128)(2,1)S(1)}, bf16[1024,256]{1,0:T(8,128)(2,1)S(1)}, u32[]{:S(2)}, u32[]{:S(2)}) collective-permute-start(bf16[1024,256]{1,0:T(8,128)(2,1)S(1)} %get-tuple-element.26), channel_id=1, source_target_pairs={{0,2},{1,3},{2,0},{3,1},{4,6},{5,7},{6,4},{7,5},{8,10},{9,11},{10,... | collective-permute-start | bytes 1572872 | tf_op jit(solution)/shard_map/ppermute | solution.py:370
  46.4 0.1 collective-permute-start.11
  46.5 1.5 %collective-permute-done.7 = bf16[1024,256]{1,0:T(8,128)(2,1)S(1)} collective-permute-done((bf16[1024,256]{1,0:T(8,128)(2,1)S(1)}, bf16[1024,256]{1,0:T(8,128)(2,1)S(1)}, u32[]{:S(2)}, u32[]{:S(2)}) %collective-permute-start.7) | collective-permute-done | bytes 524320 | tf_op jit(solution)/shard_map/ppermute | solution.py:370
  47.9 0.1 add_convert_fusion.4
  48.0 0.1 collective-permute-start.10
  48.1 0.1 collective-permute-start.9
  48.2 3.4 %collective-permute-start.8 = (bf16[256,256]{1,0:T(8,128)(2,1)S(1)}, bf16[256,256]{1,0:T(8,128)(2,1)S(1)}, u32[]{:S(2)}, u32[]{:S(2)}) collective-permute-start(bf16[256,256]{1,0:T(8,128)(2,1)S(1)} %get-tuple-element.40), channel_id=1, source_target_pairs={{0,4},{1,5},{2,6},{3,7},{4,0},{5,1},{6,2},{7,3},{8,12},{9,13},{10,... | collective-permute-start | bytes 393224 | tf_op jit(solution)/shard_map/ppermute | solution.py:370
  51.6 0.1 add_convert_fusion.3
  51.7 0.1 collective-permute-start.12
  51.8 1.5 %collective-permute-start.14 = (bf16[256,256]{1,0:T(8,128)(2,1)S(1)}, bf16[256,256]{1,0:T(8,128)(2,1)S(1)}, u32[]{:S(2)}, u32[]{:S(2)}) collective-permute-start(bf16[256,256]{1,0:T(8,128)(2,1)S(1)} %get-tuple-element.36), channel_id=1, source_target_pairs={{0,12},{1,13},{2,14},{3,15},{4,8},{5,9},{6,10},{7,11},{8,4},{9,5},... | collective-permute-start | bytes 393224 | tf_op jit(solution)/shard_map/ppermute | solution.py:370
  53.2 2.1 %collective-permute-done.10 = bf16[256,256]{1,0:T(8,128)(2,1)S(1)} collective-permute-done((bf16[256,256]{1,0:T(8,128)(2,1)S(1)}, bf16[256,256]{1,0:T(8,128)(2,1)S(1)}, u32[]{:S(2)}, u32[]{:S(2)}) %collective-permute-start.10) | collective-permute-done | bytes 131104 | tf_op jit(solution)/shard_map/ppermute | solution.py:370
  55.4 2.8 %collective-permute-done.8 = bf16[256,256]{1,0:T(8,128)(2,1)S(1)} collective-permute-done((bf16[256,256]{1,0:T(8,128)(2,1)S(1)}, bf16[256,256]{1,0:T(8,128)(2,1)S(1)}, u32[]{:S(2)}, u32[]{:S(2)}) %collective-permute-start.8) | collective-permute-done | bytes 131104 | tf_op jit(solution)/shard_map/ppermute | solution.py:370
  58.2 0.7 copy-done.8
  58.9 0.1 multiply_convert_fusion
  59.0 0.1 copy.11
  59.1 0.5 copy.10
  59.6 0.9 %copy.14 = bf16[32,8,8,128]{3,1,2,0:T(8,128)(2,1)} copy(bf16[32,8,8,128]{3,2,1,0:T(8,128)(2,1)S(1)} %bitcast.37) | data formatting | bytes 1048576
  60.5 0.0 copy-done.7
  60.6 0.2 copy-done.9
  60.8 1.0 %add_convert_fusion = bf16[256,256]{1,0:T(8,128)(2,1)S(1)} fusion(bf16[256,256]{1,0:T(8,128)(2,1)S(1)} %copy-done.5, bf16[256,256]{1,0:T(8,128)(2,1)S(1)} %copy-done.7, bf16[256,256]{1,0:T(8,128)(2,1)S(1)} %copy-done.9, bf16[1024,256]{1,0:T(8,128)(2,1)S(1)} %collective-permute-done.7, bf16[1024,256]{1,0:T(8,128)(2,1)} %copy-done.2), kind=kLoop, calls=%fused_computation.7 | loop fusion | flops 655360 | bytes 786432 | tf_op jit(solution)/shard_map/convert.8
  61.8 5.8 %collective-permute-start.17 = (bf16[128,256]{1,0:T(8,128)(2,1)S(1)}, bf16[128,256]{1,0:T(8,128)(2,1)S(1)}, u32[]{:S(2)}, u32[]{:S(2)}) collective-permute-start(bf16[128,256]{1,0:T(8,128)(2,1)S(1)} %get-tuple-element.43), channel_id=1, source_target_pairs={{0,17},{1,16},{2,19},{3,18},{4,21},{5,20},{6,23},{7,22},{8,25},{9,... | collective-permute-start | bytes 196616 | tf_op jit(solution)/shard_map/ppermute | solution.py:370
  67.6 0.1 convert_add_fusion
  67.7 0.7 collective-permute-start.16
  68.4 5.2 %collective-permute-done.15 = bf16[128,256]{1,0:T(8,128)(2,1)S(1)} collective-permute-done((bf16[128,256]{1,0:T(8,128)(2,1)S(1)}, bf16[128,256]{1,0:T(8,128)(2,1)S(1)}, u32[]{:S(2)}, u32[]{:S(2)}) %collective-permute-start.15) | collective-permute-done | bytes 65568 | tf_op jit(solution)/shard_map/ppermute | solution.py:370
  73.6 0.1 fusion.3
  73.7 0.6 pad_maximum_fusion.2
  74.4 0.6 pad_maximum_fusion.3
  (47 shorter events, 0.3 us)
Async XLA Ops:
  0.6 0.8 %copy-start.10 = (bf16[128,256]{1,0:T(8,128)(2,1)S(1)}, bf16[128,256]{1,0:T(8,128)(2,1)}, u32[]{:S(2)}) copy-start(bf16[128,256]{1,0:T(8,128)(2,1)} %param.9) | copy-start | bytes 196612
  1.6 5.7 %collective-permute-start.1 = (bf16[128,256]{1,0:T(8,128)(2,1)S(1)}, bf16[128,256]{1,0:T(8,128)(2,1)S(1)}, u32[]{:S(2)}, u32[]{:S(2)}) collective-permute-start(bf16[128,256]{1,0:T(8,128)(2,1)S(1)} %fusion.8), channel_id=1, source_target_pairs={{0,1},{1,0},{2,3},{3,2},{4,5},{5,4},{6,7},{7,6},{8,9},{9,8},{10,11... | collective-permute-start | bytes 196616 | tf_op jit(solution)/shard_map/ppermute | solution.py:370
  4.6 8.8 %collective-permute-start = (bf16[2,128,256]{2,1,0:T(8,128)(2,1)S(1)}, bf16[2,128,256]{2,1,0:T(8,128)(2,1)S(1)}, u32[]{:S(2)}, u32[]{:S(2)}) collective-permute-start(bf16[2,128,256]{2,1,0:T(8,128)(2,1)S(1)} %pad_maximum_fusion), channel_id=1, source_target_pairs={{0,16},{1,17},{2,18},{3,19},{4,20},{5,21},{6,22},{7,23},{8,24},{9,... | collective-permute-start | bytes 393224 | tf_op jit(solution)/shard_map/ppermute | solution.py:370
  7.3 11.7 %collective-permute-start.2 = (bf16[256,256]{1,0:T(8,128)(2,1)S(1)}, bf16[256,256]{1,0:T(8,128)(2,1)S(1)}, u32[]{:S(2)}, u32[]{:S(2)}) collective-permute-start(bf16[256,256]{1,0:T(8,128)(2,1)S(1)} %pad_maximum_fusion.1), channel_id=1, source_target_pairs={{0,4},{1,5},{2,6},{3,7},{4,0},{5,1},{6,2},{7,3},{8,12},{9,13},{10,... | collective-permute-start | bytes 393224 | tf_op jit(solution)/shard_map/ppermute | solution.py:370
  11.0 8.0 %collective-permute-start.4 = (bf16[256,256]{1,0:T(8,128)(2,1)S(1)}, bf16[256,256]{1,0:T(8,128)(2,1)S(1)}, u32[]{:S(2)}, u32[]{:S(2)}) collective-permute-start(bf16[256,256]{1,0:T(8,128)(2,1)S(1)} %pad_maximum_fusion.1), channel_id=1, source_target_pairs={{0,12},{1,13},{2,14},{3,15},{4,8},{5,9},{6,10},{7,11},{8,4},{9,5},... | collective-permute-start | bytes 393224 | tf_op jit(solution)/shard_map/ppermute | solution.py:370
  12.5 6.5 %collective-permute-start.3 = (bf16[256,256]{1,0:T(8,128)(2,1)S(1)}, bf16[256,256]{1,0:T(8,128)(2,1)S(1)}, u32[]{:S(2)}, u32[]{:S(2)}) collective-permute-start(bf16[256,256]{1,0:T(8,128)(2,1)S(1)} %pad_maximum_fusion.1), channel_id=1, source_target_pairs={{0,8},{1,9},{2,10},{3,11},{4,12},{5,13},{6,14},{7,15},{8,0},{9,1},... | collective-permute-start | bytes 393224 | tf_op jit(solution)/shard_map/ppermute | solution.py:370
  14.2 6.8 %copy-start.1 = (bf16[256,1024]{1,0:T(8,128)(2,1)S(1)}, bf16[256,1024]{1,0:T(8,128)(2,1)}, u32[]{:S(2)}) copy-start(bf16[256,1024]{1,0:T(8,128)(2,1)} %do_any.3) | copy-start | bytes 1572868
  14.2 12.4 %all-to-all-start = ((bf16[8,128,256]{2,1,0:T(8,128)(2,1)}), bf16[8,128,256]{2,1,0:T(8,128)(2,1)S(1)}, u32[]{:S(2)}, u32[]{:S(2)}) async-start(bf16[8,128,256]{2,1,0:T(8,128)(2,1)} %bitcast.5), calls=%async_computation | async-start | bytes 1048576 | tf_op jit(solution)/shard_map/all_to_all | solution.py:374
  18.9 2.1 %copy-start = (bf16[256,1024]{1,0:T(8,128)(2,1)S(1)}, bf16[256,1024]{1,0:T(8,128)(2,1)}, u32[]{:S(2)}) copy-start(bf16[256,1024]{1,0:T(8,128)(2,1)} %q_any.3) | copy-start | bytes 1572868
  19.0 2.0 %copy-start.3 = (s32[7,32]{1,0:T(8,128)S(1)}, s32[7,32]{1,0:T(8,128)}, u32[]{:S(2)}) copy-start(s32[7,32]{1,0:T(8,128)} %lists.1.work) | copy-start | bytes 2692
  19.1 2.0 %collective-permute-start.5 = (bf16[1024,256]{1,0:T(8,128)(2,1)S(1)}, bf16[1024,256]{1,0:T(8,128)(2,1)S(1)}, u32[]{:S(2)}, u32[]{:S(2)}) collective-permute-start(bf16[1024,256]{1,0:T(8,128)(2,1)S(1)} %constant_dynamic-update-slice_fusion.near_any.refs_0_), channel_id=1, source_target_pairs={{0,2},{1,3},{2,0},{3,1},{4,6},{5,7},{6,4},{7,5},{8,10},{9,11},{10,... | collective-permute-start | bytes 1572872 | tf_op jit(solution)/shard_map/ppermute | solution.py:370
  26.6 1.9 %collective-permute-start.6 = (bf16[1024,256]{1,0:T(8,128)(2,1)S(1)}, bf16[1024,256]{1,0:T(8,128)(2,1)S(1)}, u32[]{:S(2)}, u32[]{:S(2)}) collective-permute-start(bf16[1024,256]{1,0:T(8,128)(2,1)S(1)} %bitcast.33), channel_id=1, source_target_pairs={{0,2},{1,3},{2,0},{3,1},{4,6},{5,7},{6,4},{7,5},{8,10},{9,11},{10,... | collective-permute-start | bytes 1572872 | tf_op jit(solution)/shard_map/ppermute | solution.py:370
  37.3 10.8 %copy-start.2 = (bf16[1024,256]{1,0:T(8,128)(2,1)}, bf16[1024,256]{1,0:T(8,128)(2,1)S(1)}, u32[]{:S(2)}) copy-start(bf16[1024,256]{1,0:T(8,128)(2,1)S(1)} %get-tuple-element.25) | copy-start | bytes 1572868
  37.3 10.6 %collective-permute-start.7 = (bf16[1024,256]{1,0:T(8,128)(2,1)S(1)}, bf16[1024,256]{1,0:T(8,128)(2,1)S(1)}, u32[]{:S(2)}, u32[]{:S(2)}) collective-permute-start(bf16[1024,256]{1,0:T(8,128)(2,1)S(1)} %get-tuple-element.26), channel_id=1, source_target_pairs={{0,2},{1,3},{2,0},{3,1},{4,6},{5,7},{6,4},{7,5},{8,10},{9,11},{10,... | collective-permute-start | bytes 1572872 | tf_op jit(solution)/shard_map/ppermute | solution.py:370
  46.4 5.2 %collective-permute-start.11 = (bf16[1024,256]{1,0:T(8,128)(2,1)S(1)}, bf16[1024,256]{1,0:T(8,128)(2,1)S(1)}, u32[]{:S(2)}, u32[]{:S(2)}) collective-permute-start(bf16[1024,256]{1,0:T(8,128)(2,1)S(1)} %get-tuple-element.29), channel_id=1, source_target_pairs={{0,2},{1,3},{2,0},{3,1},{4,6},{5,7},{6,4},{7,5},{8,10},{9,11},{10,... | collective-permute-start | bytes 1572872 | tf_op jit(solution)/shard_map/ppermute | solution.py:370
  48.0 7.3 %collective-permute-start.10 = (bf16[256,256]{1,0:T(8,128)(2,1)S(1)}, bf16[256,256]{1,0:T(8,128)(2,1)S(1)}, u32[]{:S(2)}, u32[]{:S(2)}) collective-permute-start(bf16[256,256]{1,0:T(8,128)(2,1)S(1)} %get-tuple-element.38), channel_id=1, source_target_pairs={{0,12},{1,13},{2,14},{3,15},{4,8},{5,9},{6,10},{7,11},{8,4},{9,5},... | collective-permute-start | bytes 393224 | tf_op jit(solution)/shard_map/ppermute | solution.py:370
  48.1 7.3 %collective-permute-start.9 = (bf16[256,256]{1,0:T(8,128)(2,1)S(1)}, bf16[256,256]{1,0:T(8,128)(2,1)S(1)}, u32[]{:S(2)}, u32[]{:S(2)}) collective-permute-start(bf16[256,256]{1,0:T(8,128)(2,1)S(1)} %get-tuple-element.39), channel_id=1, source_target_pairs={{0,8},{1,9},{2,10},{3,11},{4,12},{5,13},{6,14},{7,15},{8,0},{9,1},... | collective-permute-start | bytes 393224 | tf_op jit(solution)/shard_map/ppermute | solution.py:370
  48.2 10.0 %collective-permute-start.8 = (bf16[256,256]{1,0:T(8,128)(2,1)S(1)}, bf16[256,256]{1,0:T(8,128)(2,1)S(1)}, u32[]{:S(2)}, u32[]{:S(2)}) collective-permute-start(bf16[256,256]{1,0:T(8,128)(2,1)S(1)} %get-tuple-element.40), channel_id=1, source_target_pairs={{0,4},{1,5},{2,6},{3,7},{4,0},{5,1},{6,2},{7,3},{8,12},{9,13},{10,... | collective-permute-start | bytes 393224 | tf_op jit(solution)/shard_map/ppermute | solution.py:370
  51.7 15.9 %collective-permute-start.12 = (bf16[256,256]{1,0:T(8,128)(2,1)S(1)}, bf16[256,256]{1,0:T(8,128)(2,1)S(1)}, u32[]{:S(2)}, u32[]{:S(2)}) collective-permute-start(bf16[256,256]{1,0:T(8,128)(2,1)S(1)} %get-tuple-element.35), channel_id=1, source_target_pairs={{0,4},{1,5},{2,6},{3,7},{4,0},{5,1},{6,2},{7,3},{8,12},{9,13},{10,... | collective-permute-start | bytes 393224 | tf_op jit(solution)/shard_map/ppermute | solution.py:370
  51.8 15.8 %collective-permute-start.14 = (bf16[256,256]{1,0:T(8,128)(2,1)S(1)}, bf16[256,256]{1,0:T(8,128)(2,1)S(1)}, u32[]{:S(2)}, u32[]{:S(2)}) collective-permute-start(bf16[256,256]{1,0:T(8,128)(2,1)S(1)} %get-tuple-element.36), channel_id=1, source_target_pairs={{0,12},{1,13},{2,14},{3,15},{4,8},{5,9},{6,10},{7,11},{8,4},{9,5},... | collective-permute-start | bytes 393224 | tf_op jit(solution)/shard_map/ppermute | solution.py:370
  55.4 2.9 %copy-start.4 = (bf16[256,256]{1,0:T(8,128)(2,1)}, bf16[256,256]{1,0:T(8,128)(2,1)S(1)}, u32[]{:S(2)}) copy-start(bf16[256,256]{1,0:T(8,128)(2,1)S(1)} %collective-permute-done.10) | copy-start | bytes 393220
  55.4 12.2 %collective-permute-start.13 = (bf16[256,256]{1,0:T(8,128)(2,1)S(1)}, bf16[256,256]{1,0:T(8,128)(2,1)S(1)}, u32[]{:S(2)}, u32[]{:S(2)}) collective-permute-start(bf16[256,256]{1,0:T(8,128)(2,1)S(1)} %get-tuple-element.37), channel_id=1, source_target_pairs={{0,8},{1,9},{2,10},{3,11},{4,12},{5,13},{6,14},{7,15},{8,0},{9,1},... | collective-permute-start | bytes 393224 | tf_op jit(solution)/shard_map/ppermute | solution.py:370
  55.4 2.9 %copy-start.6 = (bf16[256,256]{1,0:T(8,128)(2,1)}, bf16[256,256]{1,0:T(8,128)(2,1)S(1)}, u32[]{:S(2)}) copy-start(bf16[256,256]{1,0:T(8,128)(2,1)S(1)} %collective-permute-done.9) | copy-start | bytes 393220
  58.2 0.7 copy-start.8
  59.6 0.9 %copy-start.5 = (bf16[256,256]{1,0:T(8,128)(2,1)S(1)}, bf16[256,256]{1,0:T(8,128)(2,1)}, u32[]{:S(2)}) copy-start(bf16[256,256]{1,0:T(8,128)(2,1)} %copy-done.4) | copy-start | bytes 393220
  59.6 1.0 %copy-start.7 = (bf16[256,256]{1,0:T(8,128)(2,1)S(1)}, bf16[256,256]{1,0:T(8,128)(2,1)}, u32[]{:S(2)}) copy-start(bf16[256,256]{1,0:T(8,128)(2,1)} %copy-done.6) | copy-start | bytes 393220
  59.6 1.1 %copy-start.9 = (bf16[256,256]{1,0:T(8,128)(2,1)S(1)}, bf16[256,256]{1,0:T(8,128)(2,1)}, u32[]{:S(2)}) copy-start(bf16[256,256]{1,0:T(8,128)(2,1)} %copy-done.8) | copy-start | bytes 393220
  61.8 11.8 %collective-permute-start.17 = (bf16[128,256]{1,0:T(8,128)(2,1)S(1)}, bf16[128,256]{1,0:T(8,128)(2,1)S(1)}, u32[]{:S(2)}, u32[]{:S(2)}) collective-permute-start(bf16[128,256]{1,0:T(8,128)(2,1)S(1)} %get-tuple-element.43), channel_id=1, source_target_pairs={{0,17},{1,16},{2,19},{3,18},{4,21},{5,20},{6,23},{7,22},{8,25},{9,... | collective-permute-start | bytes 196616 | tf_op jit(solution)/shard_map/ppermute | solution.py:370
  67.5 6.0 %collective-permute-start.15 = (bf16[128,256]{1,0:T(8,128)(2,1)S(1)}, bf16[128,256]{1,0:T(8,128)(2,1)S(1)}, u32[]{:S(2)}, u32[]{:S(2)}) collective-permute-start(bf16[128,256]{1,0:T(8,128)(2,1)S(1)} %get-tuple-element.44), channel_id=1, source_target_pairs={{0,16},{1,17},{2,18},{3,19},{4,20},{5,21},{6,22},{7,23},{8,24},{9,... | collective-permute-start | bytes 196616 | tf_op jit(solution)/shard_map/ppermute | solution.py:370
  67.7 5.9 %collective-permute-start.16 = (bf16[128,256]{1,0:T(8,128)(2,1)S(1)}, bf16[128,256]{1,0:T(8,128)(2,1)S(1)}, u32[]{:S(2)}, u32[]{:S(2)}) collective-permute-start(bf16[128,256]{1,0:T(8,128)(2,1)S(1)} %slice.161), channel_id=1, source_target_pairs={{0,1},{1,0},{2,3},{3,2},{4,5},{5,4},{6,7},{7,6},{8,9},{9,8},{10,11... | collective-permute-start | bytes 196616 | tf_op jit(solution)/shard_map/ppermute | solution.py:370
